TPU v7x, 32 devices: a whole 2x2x4 slice. The times are simulated.
32 devices in a mesh: node: 8 (over y, x, core), mode: 4 (over z).
Axes of the slice: x: 2, y: 2, z: 4, core: 2. Of those that a mesh axis runs over, the one named last changes fastest.
Arguments:
- coords: float32 [3, 196608], P(None, 'node'), may hold values from 0 to 4
- wavevec: float32 [3, 256], replicated, may hold values from -6 to 6
- wave_amp: float32 [2, 256], replicated, may hold values from -6 to 6
- mode_shapes: bfloat16 [2000, 196608], P('mode', 'node'), may hold values from -0.013671875 to 0.013671875
- modal_frf: float32 [2, 2000], P(None, 'mode'), may hold values from -6 to 6
- radiation: bfloat16 [2, 2000, 4096], P(None, 'mode', 'node'), may hold values from -0.125 to 0.125
Outputs:
- cross_spectrum: float32 [2, 4096, 4096], P(None, ('node', 'mode'))
- field_pressure: bfloat16 [4096, 512], P(('node', 'mode'))
All inputs are finite; a program needn't handle non-finite values.
Results may differ from a plain program's by a relative error of at most 0.0065.
Values may be sent and summed in bfloat16 or wider, within the bound.
No kernel may reach another device: no remote copies, remote signals or barrier semaphores. Data moves between devices by JAX's collectives and lax.ppermute only.
A program may use at most 64 MiB of HBM per device.

v0:
```python
import jax
import jax.numpy as jnp
from jax import lax
from jax.sharding import PartitionSpec as P


def pressure_block(position, wavevec, wave_amp):
    phases = (
        position[0][:, None] * wavevec[0][None, :]
        + position[1][:, None] * wavevec[1][None, :]
        + position[2][:, None] * wavevec[2][None, :]
    )
    cosine = jnp.cos(phases)
    sines = jnp.sin(phases)
    real_part = wave_amp[0][None, :] * cosine - wave_amp[1][None, :] * sines
    imag_part = wave_amp[0][None, :] * sines + wave_amp[1][None, :] * cosine
    return jnp.concatenate([real_part, imag_part], axis=1).astype(jnp.bfloat16)


def modal_forces(coords, wavevec, wave_amp, mode_shapes, stride):
    block_count = mode_shapes.shape[1] // stride

    def advance(summed, number):
        offset = number * stride
        position = lax.dynamic_slice_in_dim(coords, offset, stride, 1)
        shapes = lax.dynamic_slice_in_dim(mode_shapes, offset, stride, 1)
        pressures = pressure_block(position, wavevec, wave_amp)
        product = jnp.dot(shapes, pressures, preferred_element_type=jnp.float32)
        return (summed + product, None)

    initial = jnp.zeros((mode_shapes.shape[0], 2 * wavevec.shape[1]), jnp.float32)
    summed, _ = lax.scan(advance, initial, jnp.arange(block_count, dtype=jnp.int32))
    return summed


def modal_response(forces, modal_frf):
    waves_count = forces.shape[1] // 2
    force_real = forces[:, :waves_count]
    force_imag = forces[:, waves_count:]
    gain_real = modal_frf[0][:, None]
    gain_imag = modal_frf[1][:, None]
    modal_real = gain_real * force_real - gain_imag * force_imag
    modal_imag = gain_real * force_imag + gain_imag * force_real
    upper = jnp.concatenate([modal_real, modal_imag], axis=1)
    lower = jnp.concatenate([-modal_imag, modal_real], axis=1)
    return jnp.concatenate([upper, lower], axis=0).astype(jnp.bfloat16)


def cross_spectra(owned_rows, others):
    waves_count = owned_rows.shape[1] // 2
    turned = jnp.concatenate([owned_rows[:, waves_count:], -owned_rows[:, :waves_count]], axis=1)
    stacked = jnp.concatenate([owned_rows, turned], axis=0)
    product = lax.dot_general(
        stacked, others, (((1,), (1,)), ((), ())), preferred_element_type=jnp.float32
    )
    return product.reshape(2, owned_rows.shape[0], others.shape[0]) * (1.0 / waves_count)


def project_field(transfer, operand):
    return lax.dot_general(
        transfer, operand, (((0,), (0,)), ((), ())), preferred_element_type=jnp.float32
    )


def body(coords, wavevec, wave_amp, mode_shapes, modal_frf, radiation):
    stride = min(2048, mode_shapes.shape[1])
    partial_forces = modal_forces(coords, wavevec, wave_amp, mode_shapes, stride)
    forces = lax.psum(partial_forces, "node")
    operand = modal_response(forces, modal_frf)
    transfer = radiation.reshape(2 * radiation.shape[1], radiation.shape[2])
    owned_rows = lax.psum_scatter(
        project_field(transfer, operand), "mode", scatter_dimension=0, tiled=True
    ).astype(jnp.bfloat16)
    spectra_out = cross_spectra(
        owned_rows, lax.all_gather(owned_rows, ("node", "mode"), axis=0, tiled=True)
    )
    return (spectra_out, owned_rows)


def solution(mesh):
    placed = (
        P(None, "node"),
        P(),
        P(),
        P("mode", "node"),
        P(None, "mode"),
        P(None, "mode", "node"),
    )
    return jax.shard_map(
        body,
        mesh=mesh,
        in_specs=placed,
        out_specs=(P(None, ("node", "mode"), None), P(("node", "mode"), None)),
        check_vma=False,
    )
```

profile of v0, /device:TPU:0, one launch (start us, length us, event | category | flops | bytes accessed | tf_op | source)
XLA Modules:
  0.0 356.8 jit_solution(947184386927734231)
XLA Ops:
  7.2 180.1 %while.11 = (s32[]{:T(128)}, f32[500,512]{1,0:T(8,128)S(1)}, s32[12]{0:T(128)S(1)}, bf16[500,24576]{1,0:T(8,128)(2,1)}, f32[2,256]{1,0:T(2,128)}, /*index=5*/f32...) while((s32[]{:T(128)}, f32[500,512]{1,0:T(8,128)S(1)}, ...), condition=%wide.region_1.2_spmd.clone, body=%wide.region_0.1_spmd.clone.sunk | while | flops 1060098048 | bytes 8396009 | solution.py:32
  10.3 9.0 %subtract_convert_fusion.3 = (bf16[2048,256]{1,0:T(8,128)(2,1)S(1)}, bf16[2048,256]{1,0:T(8,128)(2,1)S(1)}) fusion(f32[256]{0:T(256)S(1)} %bitcast.41, f32[256]{0:T(256)S(1)} %bitcast.39, f32[2048]{0:T(1024)S(1)} %bitcast.37, f32[256]{0:T(256)S(1)} %bitcast.40, f32[2048]{0:T(1024)S(1)} %bitcast.36, f32[256]{0:T(256)S(1)} %bitcast.38, ...), kind=kLoop, calls=%fused_computation.5.clone.1 | loop fusion | flops 6815744 | bytes 2126848 | tf_op jit(solution)/shard_map/convert
  19.3 2.9 select_add_fusion.2
  25.3 9.0 %subtract_convert_fusion.3 = (bf16[2048,256]{1,0:T(8,128)(2,1)S(1)}, bf16[2048,256]{1,0:T(8,128)(2,1)S(1)}) fusion(f32[256]{0:T(256)S(1)} %bitcast.41, f32[256]{0:T(256)S(1)} %bitcast.39, f32[2048]{0:T(1024)S(1)} %bitcast.37, f32[256]{0:T(256)S(1)} %bitcast.40, f32[2048]{0:T(1024)S(1)} %bitcast.36, f32[256]{0:T(256)S(1)} %bitcast.38, ...), kind=kLoop, calls=%fused_computation.5.clone.1 | loop fusion | flops 6815744 | bytes 2126848 | tf_op jit(solution)/shard_map/convert
  34.3 2.9 select_add_fusion.2
  40.3 9.0 %subtract_convert_fusion.3 = (bf16[2048,256]{1,0:T(8,128)(2,1)S(1)}, bf16[2048,256]{1,0:T(8,128)(2,1)S(1)}) fusion(f32[256]{0:T(256)S(1)} %bitcast.41, f32[256]{0:T(256)S(1)} %bitcast.39, f32[2048]{0:T(1024)S(1)} %bitcast.37, f32[256]{0:T(256)S(1)} %bitcast.40, f32[2048]{0:T(1024)S(1)} %bitcast.36, f32[256]{0:T(256)S(1)} %bitcast.38, ...), kind=kLoop, calls=%fused_computation.5.clone.1 | loop fusion | flops 6815744 | bytes 2126848 | tf_op jit(solution)/shard_map/convert
  49.3 2.9 select_add_fusion.2
  55.3 9.0 %subtract_convert_fusion.3 = (bf16[2048,256]{1,0:T(8,128)(2,1)S(1)}, bf16[2048,256]{1,0:T(8,128)(2,1)S(1)}) fusion(f32[256]{0:T(256)S(1)} %bitcast.41, f32[256]{0:T(256)S(1)} %bitcast.39, f32[2048]{0:T(1024)S(1)} %bitcast.37, f32[256]{0:T(256)S(1)} %bitcast.40, f32[2048]{0:T(1024)S(1)} %bitcast.36, f32[256]{0:T(256)S(1)} %bitcast.38, ...), kind=kLoop, calls=%fused_computation.5.clone.1 | loop fusion | flops 6815744 | bytes 2126848 | tf_op jit(solution)/shard_map/convert
  64.3 2.9 select_add_fusion.2
  70.3 9.0 %subtract_convert_fusion.3 = (bf16[2048,256]{1,0:T(8,128)(2,1)S(1)}, bf16[2048,256]{1,0:T(8,128)(2,1)S(1)}) fusion(f32[256]{0:T(256)S(1)} %bitcast.41, f32[256]{0:T(256)S(1)} %bitcast.39, f32[2048]{0:T(1024)S(1)} %bitcast.37, f32[256]{0:T(256)S(1)} %bitcast.40, f32[2048]{0:T(1024)S(1)} %bitcast.36, f32[256]{0:T(256)S(1)} %bitcast.38, ...), kind=kLoop, calls=%fused_computation.5.clone.1 | loop fusion | flops 6815744 | bytes 2126848 | tf_op jit(solution)/shard_map/convert
  79.3 2.9 select_add_fusion.2
  85.3 9.0 %subtract_convert_fusion.3 = (bf16[2048,256]{1,0:T(8,128)(2,1)S(1)}, bf16[2048,256]{1,0:T(8,128)(2,1)S(1)}) fusion(f32[256]{0:T(256)S(1)} %bitcast.41, f32[256]{0:T(256)S(1)} %bitcast.39, f32[2048]{0:T(1024)S(1)} %bitcast.37, f32[256]{0:T(256)S(1)} %bitcast.40, f32[2048]{0:T(1024)S(1)} %bitcast.36, f32[256]{0:T(256)S(1)} %bitcast.38, ...), kind=kLoop, calls=%fused_computation.5.clone.1 | loop fusion | flops 6815744 | bytes 2126848 | tf_op jit(solution)/shard_map/convert
  94.3 2.9 select_add_fusion.2
  100.3 9.0 %subtract_convert_fusion.3 = (bf16[2048,256]{1,0:T(8,128)(2,1)S(1)}, bf16[2048,256]{1,0:T(8,128)(2,1)S(1)}) fusion(f32[256]{0:T(256)S(1)} %bitcast.41, f32[256]{0:T(256)S(1)} %bitcast.39, f32[2048]{0:T(1024)S(1)} %bitcast.37, f32[256]{0:T(256)S(1)} %bitcast.40, f32[2048]{0:T(1024)S(1)} %bitcast.36, f32[256]{0:T(256)S(1)} %bitcast.38, ...), kind=kLoop, calls=%fused_computation.5.clone.1 | loop fusion | flops 6815744 | bytes 2126848 | tf_op jit(solution)/shard_map/convert
  109.4 2.9 select_add_fusion.2
  115.3 9.0 %subtract_convert_fusion.3 = (bf16[2048,256]{1,0:T(8,128)(2,1)S(1)}, bf16[2048,256]{1,0:T(8,128)(2,1)S(1)}) fusion(f32[256]{0:T(256)S(1)} %bitcast.41, f32[256]{0:T(256)S(1)} %bitcast.39, f32[2048]{0:T(1024)S(1)} %bitcast.37, f32[256]{0:T(256)S(1)} %bitcast.40, f32[2048]{0:T(1024)S(1)} %bitcast.36, f32[256]{0:T(256)S(1)} %bitcast.38, ...), kind=kLoop, calls=%fused_computation.5.clone.1 | loop fusion | flops 6815744 | bytes 2126848 | tf_op jit(solution)/shard_map/convert
  124.4 2.9 select_add_fusion.2
  130.4 9.0 %subtract_convert_fusion.3 = (bf16[2048,256]{1,0:T(8,128)(2,1)S(1)}, bf16[2048,256]{1,0:T(8,128)(2,1)S(1)}) fusion(f32[256]{0:T(256)S(1)} %bitcast.41, f32[256]{0:T(256)S(1)} %bitcast.39, f32[2048]{0:T(1024)S(1)} %bitcast.37, f32[256]{0:T(256)S(1)} %bitcast.40, f32[2048]{0:T(1024)S(1)} %bitcast.36, f32[256]{0:T(256)S(1)} %bitcast.38, ...), kind=kLoop, calls=%fused_computation.5.clone.1 | loop fusion | flops 6815744 | bytes 2126848 | tf_op jit(solution)/shard_map/convert
  139.4 2.9 select_add_fusion.2
  145.4 9.0 %subtract_convert_fusion.3 = (bf16[2048,256]{1,0:T(8,128)(2,1)S(1)}, bf16[2048,256]{1,0:T(8,128)(2,1)S(1)}) fusion(f32[256]{0:T(256)S(1)} %bitcast.41, f32[256]{0:T(256)S(1)} %bitcast.39, f32[2048]{0:T(1024)S(1)} %bitcast.37, f32[256]{0:T(256)S(1)} %bitcast.40, f32[2048]{0:T(1024)S(1)} %bitcast.36, f32[256]{0:T(256)S(1)} %bitcast.38, ...), kind=kLoop, calls=%fused_computation.5.clone.1 | loop fusion | flops 6815744 | bytes 2126848 | tf_op jit(solution)/shard_map/convert
  154.4 2.9 select_add_fusion.2
  160.4 9.0 %subtract_convert_fusion.3 = (bf16[2048,256]{1,0:T(8,128)(2,1)S(1)}, bf16[2048,256]{1,0:T(8,128)(2,1)S(1)}) fusion(f32[256]{0:T(256)S(1)} %bitcast.41, f32[256]{0:T(256)S(1)} %bitcast.39, f32[2048]{0:T(1024)S(1)} %bitcast.37, f32[256]{0:T(256)S(1)} %bitcast.40, f32[2048]{0:T(1024)S(1)} %bitcast.36, f32[256]{0:T(256)S(1)} %bitcast.38, ...), kind=kLoop, calls=%fused_computation.5.clone.1 | loop fusion | flops 6815744 | bytes 2126848 | tf_op jit(solution)/shard_map/convert
  169.4 2.9 select_add_fusion.2
  175.4 9.0 %subtract_convert_fusion.3 = (bf16[2048,256]{1,0:T(8,128)(2,1)S(1)}, bf16[2048,256]{1,0:T(8,128)(2,1)S(1)}) fusion(f32[256]{0:T(256)S(1)} %bitcast.41, f32[256]{0:T(256)S(1)} %bitcast.39, f32[2048]{0:T(1024)S(1)} %bitcast.37, f32[256]{0:T(256)S(1)} %bitcast.40, f32[2048]{0:T(1024)S(1)} %bitcast.36, f32[256]{0:T(256)S(1)} %bitcast.38, ...), kind=kLoop, calls=%fused_computation.5.clone.1 | loop fusion | flops 6815744 | bytes 2126848 | tf_op jit(solution)/shard_map/convert
  184.4 2.9 select_add_fusion.2
  190.0 57.8 %all-reduce.2.cloned.1.call-done = f32[500,512]{1,0:T(8,128)} async-done(((f32[500,512]{1,0:T(8,128)}), f32[500,512]{1,0:T(8,128)}) %all-reduce.2.cloned.1.call-update) | async-done | bytes 1024016 | tf_op jit(solution)/shard_map/psum | solution.py:68
  249.2 1.7 convolution_bitcast_fusion
  251.0 26.3 %reduce-scatter.2.cloned.1.call-done = f32[128,512]{0,1:T(8,128)} async-done(((f32[512,512]{0,1:T(8,128)}), f32[128,512]{0,1:T(8,128)}) %reduce-scatter.2.cloned.1.call-update) | async-done | bytes 262160 | tf_op jit(solution)/shard_map/reduce_scatter | solution.py:71
  277.3 1.6 convert_element_type.3
  279.0 1.7 copy.10
  281.5 63.2 %all-gather.2.cloned.1.call-done = bf16[4096,512]{0,1:T(8,128)(2,1)} async-done(((bf16[128,512]{0,1:T(8,128)(2,1)}), bf16[4096,512]{0,1:T(8,128)(2,1)}) %all-gather.2.cloned.1.call-update) | async-done | bytes 4194320 | tf_op jit(solution)/shard_map/all_gather | solution.py:75
  344.7 5.6 %convolution_multiply_fusion = f32[256,4096]{1,0:T(8,128)} fusion(bf16[4096,512]{0,1:T(8,128)(2,1)} %all-gather.2.cloned.1.call-done, bf16[128,256]{0,1:T(8,128)(2,1)S(1)} %get-tuple-element.98, bf16[128,256]{0,1:T(8,128)(2,1)S(1)} %get-tuple-element.97, bf16[128,512]{0,1:T(8,128)(2,1)} %convert_element_type.3), kind=kOutput, calls=%fused_computation.14 | convolution fusion | flops 1075576832 | bytes 8650752 | tf_op jit(solution)/shard_map/dot_general | solution.py:53
  (53 shorter events, 33.4 us)
Async XLA Ops:
  7.2 240.6 %all-reduce.2.cloned.1.call-start = ((), (), s32[]{:S(2)}) async-start(), calls=%async_computation.1 | async-start | bytes 2064384 | tf_op jit(solution)/shard_map/psum | solution.py:68
  187.4 1.0 copy-start
  188.4 1.7 copy-start.1
  188.4 89.0 %reduce-scatter.2.cloned.1.call-start = ((), (), s32[]{:S(2)}) async-start(), calls=%async_computation.2 | async-start | bytes 1310720 | tf_op jit(solution)/shard_map/reduce_scatter | solution.py:71
  251.0 93.7 %all-gather.2.cloned.1.call-start = ((), (), s32[]{:S(2)}) async-start(), calls=%async_computation.3 | async-start | bytes 4325376 | tf_op jit(solution)/shard_map/all_gather | solution.py:75
Sparse Core Ops, SparseCore 0:
  188.5 59.2 all-reduce.1
  251.1 26.2 reduce-scatter.1
  280.6 64.0 all-gather.1
where the time goes:
time: 359 us; the launch traced here: 357 us
  waiting for transfers between devices  147 us (41%)
  other arithmetic  112 us (31%)
  matrix products  42.6 us (12%)
  local copies, waits for them, and re-layouts  32.6 us (9%)
  between operations  13.8 us (4%)
  loops' own time  8.41 us (2%)
    another operation x13, other arithmetic  109 us
    all_gather x1, waiting for transfers between devices, body(): lax.all_gather(owned_rows, ('node', 'mode'), axis=0, tiled=True)  63.2 us
    psum x1, waiting for transfers between devices, body(): forces = lax.psum(partial_forces, 'node')  57.8 us
    dot_general x12, matrix products, advance(): product = jnp.dot(shapes, pressures, preferred_element_type=jnp.float32)  35.3 us
    reduce_scatter x1, waiting for transfers between devices, body(): lax.psum_scatter(project_field(transfer, operand), 'mode', scatter_dimens...  26.3 us
    slice x12, local copies, waits for them, and re-layouts, pressure_block(): position[0][:, None] * wavevec[0][None, :]  11.6 us
    slice x12, local copies, waits for them, and re-layouts, pressure_block(): wavevec[0][None, :]  9.73 us
    another operation x1, loops' own time, modal_forces(): lax.scan(advance, initial, jnp.arange(block_count, dtype=jnp.int32))  8.41 us
  transfers between devices with their start and end apart: 3, of which 3 were waited for; matrix products, arithmetic and copies ran while one was open for 1% of the time, Pallas kernels for 0%

commit v1 on v0

v1 whole, which is shorter than its diff:
```python
import functools

import jax
import jax.numpy as jnp
from jax import lax
from jax.experimental import pallas as pl
from jax.experimental.pallas import tpu as pltpu
from jax.sharding import PartitionSpec as P

SINE = (4.441535719696892, -7.264680836400963, 3.2520496076552887)
COSINE = (1.414204080330576, -6.977642043687199, 5.715238221214665, -1.7283481089755481)
COORD_PIECES = (0, 0, 1, 1, 0, 2)
WAVE_PIECES = (0, 1, 0, 1, 2, 0)
TURNS = 0.15915494309189535


def circle(turns):
    r = turns - jnp.round(turns)
    u = r * r
    s = r * (SINE[0] + u * (SINE[1] + u * SINE[2]))
    c = COSINE[0] + u * (COSINE[1] + u * (COSINE[2] + u * COSINE[3]))
    return c * c - 1.0, s * c


def pieces(x, order):
    first = x.astype(jnp.bfloat16).astype(jnp.float32)
    second = (x - first).astype(jnp.bfloat16).astype(jnp.float32)
    third = x - first - second
    blank = jnp.zeros((8 - x.shape[0], x.shape[1]), jnp.float32)
    parts = [jnp.concatenate([p, blank], axis=0) for p in (first, second, third)]
    return jnp.concatenate([parts[i] for i in order], axis=0).astype(jnp.bfloat16)


def forces_kernel(half, sub, coords_ref, wave_ref, shapes_ref, out_ref, wave_pieces, even, odd):
    step = pl.program_id(0)
    waves = wave_ref.shape[1]

    def fill(start, buffer):
        for j in range(half // sub):
            at = pl.multiple_of(start + j * sub, sub)
            turns = lax.dot_general(
                pieces(coords_ref[:, pl.ds(at, sub)], COORD_PIECES),
                wave_pieces[...],
                (((0,), (0,)), ((), ())),
                preferred_element_type=jnp.float32,
            )
            cosine, sine = circle(turns)
            buffer[j * sub : (j + 1) * sub, :waves] = cosine.astype(jnp.bfloat16)
            buffer[j * sub : (j + 1) * sub, waves:] = sine.astype(jnp.bfloat16)

    @pl.when(step == 0)
    def _():
        wave_pieces[...] = pieces(wave_ref[...] * TURNS, WAVE_PIECES)
        out_ref[...] = jnp.zeros_like(out_ref)
        fill(0, even)

    here = step * (2 * half)
    fill(here + half, odd)
    out_ref[...] += jnp.dot(shapes_ref[:, :half], even[...], preferred_element_type=jnp.float32)
    fill(jnp.where(step == pl.num_programs(0) - 1, 0, here + 2 * half), even)
    out_ref[...] += jnp.dot(shapes_ref[:, half:], odd[...], preferred_element_type=jnp.float32)


def unit_forces(coords, wavevec, mode_shapes):
    modes, nodes = mode_shapes.shape
    waves = wavevec.shape[1]
    half, sub = 2048, 256
    return pl.pallas_call(
        functools.partial(forces_kernel, half, sub),
        grid=(nodes // (2 * half),),
        in_specs=[
            pl.BlockSpec((3, nodes), lambda i: (0, 0)),
            pl.BlockSpec((3, waves), lambda i: (0, 0)),
            pl.BlockSpec((modes, 2 * half), lambda i: (0, i)),
        ],
        out_specs=pl.BlockSpec((modes, 2 * waves), lambda i: (0, 0)),
        out_shape=jax.ShapeDtypeStruct((modes, 2 * waves), jnp.float32),
        scratch_shapes=[
            pltpu.VMEM((8 * len(WAVE_PIECES), waves), jnp.bfloat16),
            pltpu.VMEM((half, 2 * waves), jnp.bfloat16),
            pltpu.VMEM((half, 2 * waves), jnp.bfloat16),
        ],
        compiler_params=pltpu.CompilerParams(vmem_limit_bytes=48 << 20),
        cost_estimate=pl.CostEstimate(
            flops=4 * modes * nodes * waves, bytes_accessed=2 * modes * nodes, transcendentals=0
        ),
    )(coords, wavevec, mode_shapes)


def modal_response(forces, wave_amp, modal_frf):
    waves = forces.shape[1] // 2
    cosine, sine = forces[:, :waves], forces[:, waves:]
    amp_real, amp_imag = wave_amp[0][None, :], wave_amp[1][None, :]
    force_real = amp_real * cosine - amp_imag * sine
    force_imag = amp_real * sine + amp_imag * cosine
    gain_real, gain_imag = modal_frf[0][:, None], modal_frf[1][:, None]
    modal_real = gain_real * force_real - gain_imag * force_imag
    modal_imag = gain_real * force_imag + gain_imag * force_real
    upper = jnp.concatenate([modal_real, modal_imag], axis=1)
    lower = jnp.concatenate([-modal_imag, modal_real], axis=1)
    return jnp.concatenate([upper, lower], axis=0).astype(jnp.bfloat16)


def cross_spectra(owned_rows, others):
    waves = owned_rows.shape[1] // 2
    turned = jnp.concatenate([owned_rows[:, waves:], -owned_rows[:, :waves]], axis=1)
    stacked = jnp.concatenate([owned_rows, turned], axis=0)
    product = lax.dot_general(
        stacked, others, (((1,), (1,)), ((), ())), preferred_element_type=jnp.float32
    )
    return product.reshape(2, owned_rows.shape[0], others.shape[0]) * (1.0 / waves)


def project_field(transfer, operand):
    return lax.dot_general(
        transfer, operand, (((0,), (0,)), ((), ())), preferred_element_type=jnp.float32
    )


def body(coords, wavevec, wave_amp, mode_shapes, modal_frf, radiation):
    forces = lax.psum(unit_forces(coords, wavevec, mode_shapes), "node")
    operand = modal_response(forces, wave_amp, modal_frf)
    transfer = radiation.reshape(2 * radiation.shape[1], radiation.shape[2])
    owned_rows = lax.psum_scatter(
        project_field(transfer, operand), "mode", scatter_dimension=0, tiled=True
    ).astype(jnp.bfloat16)
    spectra_out = cross_spectra(
        owned_rows, lax.all_gather(owned_rows, ("node", "mode"), axis=0, tiled=True)
    )
    return (spectra_out, owned_rows)


def solution(mesh):
    placed = (
        P(None, "node"),
        P(),
        P(),
        P("mode", "node"),
        P(None, "mode"),
        P(None, "mode", "node"),
    )
    return jax.shard_map(
        body,
        mesh=mesh,
        in_specs=placed,
        out_specs=(P(None, ("node", "mode"), None), P(("node", "mode"), None)),
        check_vma=False,
    )
```

time: 359 us -> 207 us (0.58)
  other arithmetic: 112 us -> 3.98 us
  matrix products: 42.6 us -> 7.27 us
  Pallas kernels: 0 us -> 28.9 us
  local copies, waits for them, and re-layouts: 32.6 us -> 3.95 us
  loops' own time: 8.41 us -> 0 us
    another operation x13 -> x2, other arithmetic: 109 us -> 1.48 us
    dot_general x12 -> x0, matrix products: 35.3 us -> none  [advance(): product = jnp.dot(shapes, pressures, preferred_element_type=jnp.float32)]
    pallas_call x0 -> x1, Pallas kernels: none -> 28.9 us  [unit_forces(): pl.pallas_call(functools.partial(forces_kernel, half, sub), grid=(nodes /...]
    slice x25 -> x2, local copies, waits for them, and re-layouts: 21.4 us -> 0.01 us  [the longest x1 0.01 us: modal_response(): gain_real, gain_imag = (modal_frf[0][:, None], modal_frf[1][:, None])]
    another operation x1 -> x0, loops' own time: 8.41 us -> none  [modal_forces(): lax.scan(advance, initial, jnp.arange(block_count, dtype=jnp.int32))]
    dynamic_slice x12 -> x0, local copies, waits for them, and re-layouts: 7.04 us -> none  [modal_forces(): lax.scan(advance, initial, jnp.arange(block_count, dtype=jnp.int32))]
where the time goes in v1:
time: 207 us; the launch traced here: 206 us
  waiting for transfers between devices  148 us (71%)
  Pallas kernels  28.9 us (14%)
  between operations  13.8 us (7%)
  matrix products  7.27 us (4%)
  other arithmetic  3.98 us (2%)
  local copies, waits for them, and re-layouts  3.95 us (2%)
    all_gather x1, waiting for transfers between devices, body(): lax.all_gather(owned_rows, ('node', 'mode'), axis=0, tiled=True)  63.2 us
    psum x1, waiting for transfers between devices, body(): forces = lax.psum(unit_forces(coords, wavevec, mode_shapes), 'node')  58.7 us
    pallas_call x1, Pallas kernels, unit_forces(): pl.pallas_call(functools.partial(forces_kernel, half, sub), grid=(nodes /...  28.9 us
    reduce_scatter x1, waiting for transfers between devices, body(): lax.psum_scatter(project_field(transfer, operand), 'mode', scatter_dimens...  26.3 us
    dot_general x1, matrix products, cross_spectra(): lax.dot_general(stacked, others, (((1,), (1,)), ((), ())), preferred_elem...  5.56 us
  transfers between devices with their start and end apart: 3, of which 3 were waited for; matrix products, arithmetic and copies ran while one was open for 1% of the time, Pallas kernels for 0%

profile of v1, /device:TPU:0, one launch (start us, length us, event | category | flops | bytes accessed | tf_op | source)
XLA Modules:
  0.0 206.3 jit_solution(2632585390735661175)
XLA Ops:
  7.2 0.0 all-reduce.2.cloned.1.call-start
  7.2 0.0 copy-start
  7.2 1.0 copy-done
  8.2 0.0 copy-start.1
  8.2 0.7 copy-done.1
  8.9 0.0 copy-start.2
  8.9 28.9 %shard_map.77 = f32[500,512]{1,0:T(8,128)} custom-call(f32[3,24576]{1,0:T(4,128)S(1)} %copy-done, f32[3,256]{1,0:T(4,128)S(1)} %copy-done.1, bf16[500,24576]{1,0:T(8,128)(2,1)} %shapes_ref.1), custom_call_target="tpu_custom_call" | custom-call | flops 12582912000 | bytes 24576000 | tf_op jit(solution)/shard_map/pallas_call | solution.py:68
  37.8 0.0 copy-start.4
  37.8 0.0 copy-start.3
  37.8 0.0 all-reduce.2.cloned.1.call-update
  37.9 0.0 reduce-scatter.2.cloned.1.call-start
  37.9 0.0 copy-done.2
  37.9 0.2 copy.9
  38.1 0.2 reshape.12
  38.3 0.2 copy-done.4
  38.5 0.0 copy-done.3
  38.5 58.7 %all-reduce.2.cloned.1.call-done = f32[500,512]{1,0:T(8,128)} async-done(((f32[500,512]{1,0:T(8,128)}), f32[500,512]{1,0:T(8,128)}) %all-reduce.2.cloned.1.call-update) | async-done | bytes 1024016 | tf_op jit(solution)/shard_map/psum | solution.py:121
  97.2 1.4 fusion.14
  98.7 1.7 convolution_bitcast_fusion
  100.4 0.0 reduce-scatter.2.cloned.1.call-update
  100.5 0.0 all-gather.2.cloned.1.call-start
  100.5 26.3 %reduce-scatter.2.cloned.1.call-done = f32[128,512]{0,1:T(8,128)} async-done(((f32[512,512]{0,1:T(8,128)}), f32[128,512]{0,1:T(8,128)}) %reduce-scatter.2.cloned.1.call-update) | async-done | bytes 262160 | tf_op jit(solution)/shard_map/reduce_scatter | solution.py:124
  126.8 1.6 convert_element_type.4
  128.5 0.0 all-gather.2.cloned.1.call-update
  128.5 1.7 copy.10
  130.1 0.9 fusion.15
  131.0 63.2 %all-gather.2.cloned.1.call-done = bf16[4096,512]{0,1:T(8,128)(2,1)} async-done(((bf16[128,512]{0,1:T(8,128)(2,1)}), bf16[4096,512]{0,1:T(8,128)(2,1)}) %all-gather.2.cloned.1.call-update) | async-done | bytes 4194320 | tf_op jit(solution)/shard_map/all_gather | solution.py:128
  194.2 5.6 %convolution_multiply_fusion = f32[256,4096]{1,0:T(8,128)} fusion(bf16[4096,512]{0,1:T(8,128)(2,1)} %all-gather.2.cloned.1.call-done, bf16[128,256]{0,1:T(8,128)(2,1)S(1)} %get-tuple-element.10, bf16[128,256]{0,1:T(8,128)(2,1)S(1)} %get-tuple-element.9, bf16[128,512]{0,1:T(8,128)(2,1)} %convert_element_type.4), kind=kOutput, calls=%fused_computation | convolution fusion | flops 1075576832 | bytes 8650752 | tf_op jit(solution)/shard_map/dot_general | solution.py:108
  (3 shorter events, 0.0 us)
Async XLA Ops:
  7.2 90.1 %all-reduce.2.cloned.1.call-start = ((), (), s32[]{:S(2)}) async-start(), calls=%async_computation.1 | async-start | bytes 2064384 | tf_op jit(solution)/shard_map/psum | solution.py:121
  7.2 1.0 copy-start
  8.2 0.7 copy-start.1
  8.9 29.0 %copy-start.2 = (bf16[2,500,512]{2,0,1:T(2,128)(2,1)S(1)}, bf16[2,500,512]{2,0,1:T(2,128)(2,1)}, u32[]{:S(2)}) copy-start(bf16[2,500,512]{2,0,1:T(2,128)(2,1)} %param.11) | copy-start | bytes 3072004
  37.8 0.7 copy-start.4
  37.8 0.7 copy-start.3
  37.9 89.0 %reduce-scatter.2.cloned.1.call-start = ((), (), s32[]{:S(2)}) async-start(), calls=%async_computation.2 | async-start | bytes 1310720 | tf_op jit(solution)/shard_map/reduce_scatter | solution.py:124
  100.5 93.7 %all-gather.2.cloned.1.call-start = ((), (), s32[]{:S(2)}) async-start(), calls=%async_computation.3 | async-start | bytes 4325376 | tf_op jit(solution)/shard_map/all_gather | solution.py:128
Sparse Core Ops, SparseCore 0:
  38.0 59.2 all-reduce.1
  100.6 26.2 reduce-scatter.1
  130.1 64.0 all-gather.1

commit v2 on v1

v2 whole, which is shorter than its diff:
```python
import functools

import jax
import jax.numpy as jnp
from jax import lax
from jax.experimental import pallas as pl
from jax.experimental.pallas import tpu as pltpu
from jax.sharding import PartitionSpec as P

SINE = (4.441535719696892, -7.264680836400963, 3.2520496076552887)
COSINE = (1.414204080330576, -6.977642043687199, 5.715238221214665, -1.7283481089755481)
COORD_PIECES = (0, 0, 1, 1, 0, 2)
WAVE_PIECES = (0, 1, 0, 1, 2, 0)
TURNS = 0.15915494309189535
CHUNKS = 1
BIG = pltpu.CompilerParams(vmem_limit_bytes=48 << 20)


def circle(turns):
    r = turns - jnp.round(turns)
    u = r * r
    s = r * (SINE[0] + u * (SINE[1] + u * SINE[2]))
    c = COSINE[0] + u * (COSINE[1] + u * (COSINE[2] + u * COSINE[3]))
    return c * c - 1.0, s * c


def pieces(x, order):
    first = x.astype(jnp.bfloat16).astype(jnp.float32)
    second = (x - first).astype(jnp.bfloat16).astype(jnp.float32)
    third = x - first - second
    blank = jnp.zeros((8 - x.shape[0], x.shape[1]), jnp.float32)
    parts = [jnp.concatenate([p, blank], axis=0) for p in (first, second, third)]
    return jnp.concatenate([parts[i] for i in order], axis=0).astype(jnp.bfloat16)


def forces_kernel(
    half, sub, coords_ref, wave_ref, shapes_ref, mine_ref, other_ref, wave_pieces, even, odd
):
    step = pl.program_id(0)
    waves = wave_ref.shape[1]
    own = waves // 2

    def fill(start, buffer):
        for j in range(half // sub):
            at = pl.multiple_of(start + j * sub, sub)
            turns = lax.dot_general(
                pieces(coords_ref[:, pl.ds(at, sub)], COORD_PIECES),
                wave_pieces[...],
                (((0,), (0,)), ((), ())),
                preferred_element_type=jnp.float32,
            )
            cosine, sine = (x.astype(jnp.bfloat16) for x in circle(turns))
            rows = slice(j * sub, (j + 1) * sub)
            buffer[rows, :own] = cosine[:, :own]
            buffer[rows, own : 2 * own] = sine[:, :own]
            buffer[rows, 2 * own : 3 * own] = cosine[:, own:]
            buffer[rows, 3 * own :] = sine[:, own:]

    def add(columns, buffer):
        product = jnp.dot(
            shapes_ref[:, columns], buffer[...], preferred_element_type=jnp.float32
        )
        mine_ref[...] += product[:, :waves]
        other_ref[...] += product[:, waves:]

    @pl.when(step == 0)
    def _():
        wave_pieces[...] = pieces(wave_ref[...] * TURNS, WAVE_PIECES)
        mine_ref[...] = jnp.zeros_like(mine_ref)
        other_ref[...] = jnp.zeros_like(other_ref)
        fill(0, even)

    here = step * (2 * half)
    fill(here + half, odd)
    add(slice(0, half), even)
    fill(jnp.where(step == pl.num_programs(0) - 1, 0, here + 2 * half), even)
    add(slice(half, 2 * half), odd)


def unit_forces(coords, wavevec, mode_shapes):
    modes, nodes = mode_shapes.shape
    waves = wavevec.shape[1]
    half, sub = 2048, 256
    out = jax.ShapeDtypeStruct((modes, waves), jnp.float32)
    return pl.pallas_call(
        functools.partial(forces_kernel, half, sub),
        grid=(nodes // (2 * half),),
        in_specs=[
            pl.BlockSpec((3, nodes), lambda i: (0, 0)),
            pl.BlockSpec((3, waves), lambda i: (0, 0)),
            pl.BlockSpec((modes, 2 * half), lambda i: (0, i)),
        ],
        out_specs=[pl.BlockSpec((modes, waves), lambda i: (0, 0))] * 2,
        out_shape=[out, out],
        scratch_shapes=[
            pltpu.VMEM((8 * len(WAVE_PIECES), waves), jnp.bfloat16),
            pltpu.VMEM((half, 2 * waves), jnp.bfloat16),
            pltpu.VMEM((half, 2 * waves), jnp.bfloat16),
        ],
        compiler_params=BIG,
        cost_estimate=pl.CostEstimate(
            flops=12 * modes * nodes * waves, bytes_accessed=2 * modes * nodes, transcendentals=0
        ),
    )(coords, wavevec, mode_shapes)


def field_kernel(
    blocks, kept_ref, last_ref, amp_ref, frf_ref, own_ref, mate_ref, total_ref, *sent_refs
):
    forces = kept_ref[...] + last_ref[...].astype(jnp.float32)
    waves = forces.shape[1] // 2
    cosine, sine = forces[:, :waves], forces[:, waves:]
    amp_real, amp_imag = amp_ref[0:1, :], amp_ref[1:2, :]
    force_real = amp_real * cosine - amp_imag * sine
    force_imag = amp_real * sine + amp_imag * cosine
    gain_real, gain_imag = frf_ref[:, 0:1], frf_ref[:, 1:2]
    real = gain_real * force_real - gain_imag * force_imag
    imag = gain_real * force_imag + gain_imag * force_real
    upper = jnp.concatenate([real, imag], axis=1).astype(jnp.bfloat16)
    lower = jnp.concatenate([-imag, real], axis=1).astype(jnp.bfloat16)
    over_modes = (((0,), (0,)), ((), ()))
    width = own_ref.shape[2] // blocks
    for side, transfer in enumerate((own_ref, mate_ref)):
        field = lax.dot_general(
            upper, transfer[0], over_modes, preferred_element_type=jnp.float32
        ) + lax.dot_general(lower, transfer[1], over_modes, preferred_element_type=jnp.float32)
        total_ref[side] = field[:, :width]
        for k, sent in enumerate(sent_refs):
            sent[side] = field[:, (k + 1) * width : (k + 2) * width].astype(jnp.bfloat16)


def partial_fields(blocks, kept, last, amp, frf, own, mate):
    waves = kept.shape[1]
    shape = (2, waves, own.shape[2] // blocks)
    return pl.pallas_call(
        functools.partial(field_kernel, blocks),
        out_shape=[jax.ShapeDtypeStruct(shape, jnp.float32)]
        + [jax.ShapeDtypeStruct(shape, jnp.bfloat16)] * (blocks - 1),
        compiler_params=BIG,
        cost_estimate=pl.CostEstimate(
            flops=8 * own.shape[1] * own.shape[2] * waves,
            bytes_accessed=4 * own.size,
            transcendentals=0,
        ),
    )(kept, last, amp, frf, own, mate)


def spectra_kernel(chunks, blocks, place_ref, *refs):
    ours = refs[:chunks]
    theirs = refs[chunks : 2 * chunks]
    left_ours = refs[2 * chunks : 3 * chunks]
    left_theirs = refs[3 * chunks : 4 * chunks]
    out_ref, left = refs[-2:]
    depth, rows = ours[0].shape[-2:]
    waves = depth // 2
    first = (pl.program_id(0) == 0) & (pl.program_id(1) == 0)

    @pl.when(first)
    def _():
        for n, ref in enumerate((*left_ours, *left_theirs)):
            turned = ref[...].astype(jnp.float32).T
            real, imag = turned[:, :waves], turned[:, waves:]
            left[n, :rows] = turned.astype(jnp.bfloat16)
            left[n, rows:] = jnp.concatenate([imag, -real], axis=1).astype(jnp.bfloat16)

    scale = 1.0 / (2 * chunks * waves)
    for z in range(blocks):
        at = lax.rem(place_ref[1] - z + blocks, blocks)
        total = 0.0
        for n, ref in enumerate((*ours, *theirs)):
            total = total + jnp.dot(left[n], ref[at, 0], preferred_element_type=jnp.float32)
        out_ref[0, :, z * rows : (z + 1) * rows] = total[:rows] * scale
        out_ref[1, :, z * rows : (z + 1) * rows] = total[rows:] * scale


def cross_spectra(place, blocks, groups, ours, theirs, left_ours, left_theirs):
    chunks = len(ours)
    depth, rows = left_ours[0].shape
    bits = groups.bit_length() - 1

    def at(core_of_data, group, side, place_ref):
        turn = jnp.bitwise_xor(group, place_ref[0])
        flipped = 0
        for b in range(bits):
            flipped = flipped + ((turn >> b) & 1) * (1 << (bits - 1 - b))
        same = jnp.where(core_of_data == 0, turn, flipped)
        return (same, 0, jnp.bitwise_xor(side, core_of_data), 0, 0)

    def of_ours(g, s, place_ref):
        return at(place_ref[2], g, s, place_ref)

    def of_theirs(g, s, place_ref):
        return at(1 - place_ref[2], g, s, place_ref)

    block = (None, blocks, 1, depth, rows)
    whole = pl.BlockSpec((depth, rows), lambda g, s, place_ref: (0, 0))
    return pl.pallas_call(
        functools.partial(spectra_kernel, chunks, blocks),
        grid_spec=pltpu.PrefetchScalarGridSpec(
            num_scalar_prefetch=1,
            grid=(groups, 2),
            in_specs=[pl.BlockSpec(block, of_ours)] * chunks
            + [pl.BlockSpec(block, of_theirs)] * chunks
            + [whole] * (2 * chunks),
            out_specs=pl.BlockSpec(
                (2, rows, blocks * rows), lambda g, s, place_ref: (0, 0, 2 * g + s)
            ),
            scratch_shapes=[pltpu.VMEM((2 * chunks, 2 * rows, depth), jnp.bfloat16)],
        ),
        out_shape=jax.ShapeDtypeStruct((2, rows, 2 * groups * blocks * rows), jnp.float32),
        compiler_params=BIG,
    )(place, *ours, *theirs, *left_ours, *left_theirs)


def body(nodes, blocks, coords, wavevec, wave_amp, mode_shapes, modal_frf, radiation):
    groups = nodes // 2
    bits = groups.bit_length() - 1
    node, mode = lax.axis_index("node"), lax.axis_index("mode")
    core = lax.rem(node, 2)
    place = jnp.stack([node // 2, mode, core]).astype(jnp.int32)

    def to_mate(x):
        return lax.ppermute(x, "node", [(i, i ^ 1) for i in range(nodes)])

    def across(x, step):
        def flip(i):
            return i ^ (2 << (step if i % 2 == 0 else bits - 1 - step))

        return lax.ppermute(x, "node", [(i, flip(i)) for i in range(nodes)])

    def along(x, k):
        return lax.ppermute(x, "mode", [(i, (i + k) % blocks) for i in range(blocks)])

    width = radiation.shape[2] // blocks
    doubled = jnp.concatenate([radiation, radiation[:, :, : (blocks - 1) * width]], axis=2)
    own = lax.dynamic_slice_in_dim(doubled, mode * width, blocks * width, 2)
    mate = to_mate(own)
    frf = modal_frf.T

    size = wavevec.shape[1] // 2 // CHUNKS
    halves = jnp.roll(jnp.stack(jnp.split(wavevec, 2, axis=1)), core, axis=0)
    amps = jnp.where(core == 0, *jnp.split(wave_amp, 2, axis=1))

    ours, theirs, left_ours, left_theirs = [], [], [], []
    for chunk in range(CHUNKS):
        part = slice(chunk * size, (chunk + 1) * size)
        mine, other = unit_forces(
            coords, jnp.concatenate([halves[0, :, part], halves[1, :, part]], axis=1), mode_shapes
        )
        kept = mine + to_mate(other)
        for step in range(bits - 1):
            kept = kept + across(kept.astype(jnp.bfloat16), step).astype(jnp.float32)
        last = across(kept.astype(jnp.bfloat16), bits - 1)
        total, *sent = partial_fields(blocks, kept, last, amps[:, part], frf, own, mate)
        for k, block in enumerate(sent):
            total = total + along(block, k + 1).astype(jnp.float32)
        field = total.astype(jnp.bfloat16)
        column = jnp.stack([field] + [along(field, k) for k in range(1, blocks)])
        gathered = [column]
        for step in range(bits):
            gathered = gathered + [across(x, step) for x in gathered]
        mates = [to_mate(x) for x in gathered]
        ours.append(jnp.stack(gathered))
        theirs.append(jnp.stack(mates))
        left_ours.append(field[0])
        left_theirs.append(mates[0][0, 1])
    spectra = cross_spectra(place, blocks, groups, ours, theirs, left_ours, left_theirs)
    in_order = [
        jnp.where(core == 0, a, b)
        for first, second in ((left_ours, left_theirs), (left_theirs, left_ours))
        for a, b in zip(first, second)
    ]
    field_pressure = jnp.concatenate(
        [x[:size] for x in in_order] + [x[size:] for x in in_order], axis=0
    ).T
    return (spectra, field_pressure)


def solution(mesh):
    placed = (
        P(None, "node"),
        P(),
        P(),
        P("mode", "node"),
        P(None, "mode"),
        P(None, "mode", "node"),
    )
    return jax.shard_map(
        functools.partial(body, mesh.shape["node"], mesh.shape["mode"]),
        mesh=mesh,
        in_specs=placed,
        out_specs=(P(None, ("node", "mode"), None), P(("node", "mode"), None)),
        check_vma=False,
    )
```

time: 207 us -> 118 us (0.57)
  waiting for transfers between devices: 148 us -> 46.2 us
  starting transfers between devices: 0.12 us -> 21.3 us
  between operations: 13.8 us -> 0.84 us
  Pallas kernels: 28.9 us -> 38.8 us
  matrix products: 7.27 us -> 0 us
    all_gather x1 -> x0, waiting for transfers between devices: 63.2 us -> none  [body(): lax.all_gather(owned_rows, ('node', 'mode'), axis=0, tiled=True)]
    psum x1 -> x0, waiting for transfers between devices: 58.7 us -> none  [body(): forces = lax.psum(unit_forces(coords, wavevec, mode_shapes), 'node')]
    ppermute x0 -> x17, waiting for transfers between devices: none -> 46.2 us  [the longest x5 28.5 us: across(): return lax.ppermute(x, 'node', [(i, flip(i)) for i in range(nodes)])]
    reduce_scatter x1 -> x0, waiting for transfers between devices: 26.3 us -> none  [body(): lax.psum_scatter(project_field(transfer, operand), 'mode', scatter_dimens...]
    ppermute x0 -> x17, starting transfers between devices: none -> 21.3 us  [the longest x6 11.9 us: along(): lax.ppermute(x, 'mode', [(i, (i + k) % blocks) for i in range(blocks)])]
    pallas_call x0 -> x2, Pallas kernels: none -> 7.39 us  [the longest x1 6.34 us: cross_spectra(): pl.pallas_call(functools.partial(spectra_kernel, chunks, blocks), grid_sp...]
    dot_general x2 -> x0, matrix products: 7.27 us -> none  [the longest x1 5.56 us: cross_spectra(): lax.dot_general(stacked, others, (((1,), (1,)), ((), ())), preferred_elem...]
    pallas_call x1, Pallas kernels: 28.9 us -> 31.4 us  [unit_forces(): pl.pallas_call(functools.partial(forces_kernel, half, sub), grid=(nodes /...]
  transfers between devices with their start and end apart: 3 -> 17, of which waited for: 3 -> 9; matrix products, arithmetic and copies ran while one was open for 1% -> 6% of each run, Pallas kernels for 0% -> 0%
where the time goes in v2:
time: 118 us; the launch traced here: 117 us
  waiting for transfers between devices  46.2 us (39%)
  Pallas kernels  38.8 us (33%)
  starting transfers between devices  21.3 us (18%)
  local copies, waits for them, and re-layouts  5.67 us (5%)
  other arithmetic  4.45 us (4%)
    pallas_call x1, Pallas kernels, unit_forces(): pl.pallas_call(functools.partial(forces_kernel, half, sub), grid=(nodes /...  31.4 us
    ppermute x5, waiting for transfers between devices, across(): return lax.ppermute(x, 'node', [(i, flip(i)) for i in range(nodes)])  28.5 us
    ppermute x6, waiting for transfers between devices, along(): lax.ppermute(x, 'mode', [(i, (i + k) % blocks) for i in range(blocks)])  17.7 us
    ppermute x6, starting transfers between devices, along(): lax.ppermute(x, 'mode', [(i, (i + k) % blocks) for i in range(blocks)])  11.9 us
    ppermute x5, starting transfers between devices, across(): return lax.ppermute(x, 'node', [(i, flip(i)) for i in range(nodes)])  8.32 us
    pallas_call x1, Pallas kernels, cross_spectra(): pl.pallas_call(functools.partial(spectra_kernel, chunks, blocks), grid_sp...  6.34 us
  transfers between devices with their start and end apart: 17, of which 9 were waited for; matrix products, arithmetic and copies ran while one was open for 6% of the time, Pallas kernels for 0%

profile of v2, /device:TPU:0, one launch (start us, length us, event | category | flops | bytes accessed | tf_op | source)
XLA Modules:
  0.0 117.3 jit_solution(12466818991245969734)
XLA Ops:
  0.7 0.7 slice_bitcast_fusion.4
  1.4 1.0 copy-done
  2.4 31.4 %shard_map.77 = (f32[500,256]{1,0:T(8,128)S(1)}, f32[500,256]{1,0:T(8,128)S(1)}) custom-call(f32[3,24576]{1,0:T(4,128)S(1)} %copy-done, f32[3,256]{1,0:T(4,128)S(1)} %pad_maximum_fusion.3.wave_ref, bf16[500,24576]{1,0:T(8,128)(2,1)} %shapes_ref.1), custom_call_target="tpu_custom_call" | custom-call | flops 37748736000 | bytes 24576000 | tf_op jit(solution)/shard_map/pallas_call | solution.py:85
  33.8 0.5 collective-permute-start
  34.5 1.0 slice.38
  35.4 0.4 fusion.own_ref
  35.8 1.7 %copy.15 = bf16[2,500,512]{2,0,1:T(2,128)(2,1)} copy(bf16[2,500,512]{2,1,0:T(8,128)(2,1)S(1)} %fusion.own_ref) | data formatting | bytes 2048000 | tf_op jit(solution)/shard_map/dynamic_slice | solution.py:236
  37.6 1.1 fusion.6
  38.7 3.0 %collective-permute-start.1 = (bf16[500,256]{1,0:T(8,128)(2,1)S(1)}, bf16[500,256]{1,0:T(8,128)(2,1)S(1)}, u32[]{:S(2)}, u32[]{:S(2)}) collective-permute-start(bf16[500,256]{1,0:T(8,128)(2,1)S(1)} %get-tuple-element.20), channel_id=1, source_target_pairs={{0,8},{4,20},{8,0},{12,28},{16,24},{20,4},{24,16},{28,12},{1,9},{5... | collective-permute-start | bytes 768008 | tf_op jit(solution)/shard_map/ppermute | solution.py:229
  41.7 4.3 %collective-permute-done.1 = bf16[500,256]{1,0:T(8,128)(2,1)S(1)} collective-permute-done((bf16[500,256]{1,0:T(8,128)(2,1)S(1)}, bf16[500,256]{1,0:T(8,128)(2,1)S(1)}, u32[]{:S(2)}, u32[]{:S(2)}) %collective-permute-start.1) | collective-permute-done | bytes 256032 | tf_op jit(solution)/shard_map/ppermute | solution.py:229
  46.1 2.1 %collective-permute-start.2 = (bf16[500,256]{1,0:T(8,128)(2,1)S(1)}, bf16[500,256]{1,0:T(8,128)(2,1)S(1)}, u32[]{:S(2)}, u32[]{:S(2)}) collective-permute-start(bf16[500,256]{1,0:T(8,128)(2,1)S(1)} %get-tuple-element.18), channel_id=1, source_target_pairs={{0,16},{4,12},{8,24},{12,4},{16,0},{20,28},{24,8},{28,20},{1,17},{... | collective-permute-start | bytes 768008 | tf_op jit(solution)/shard_map/ppermute | solution.py:229
  48.4 0.2 copy.16.mate_ref
  48.6 4.0 %collective-permute-done.2.last_ref = bf16[500,256]{1,0:T(8,128)(2,1)S(1)} collective-permute-done((bf16[500,256]{1,0:T(8,128)(2,1)S(1)}, bf16[500,256]{1,0:T(8,128)(2,1)S(1)}, u32[]{:S(2)}, u32[]{:S(2)}) %collective-permute-start.2) | collective-permute-done | bytes 256032 | tf_op jit(solution)/shard_map/ppermute | solution.py:229
  52.6 1.1 shard_map.78
  53.6 3.1 %collective-permute-start.4 = (bf16[2,256,128]{2,1,0:T(8,128)(2,1)S(1)}, bf16[2,256,128]{2,1,0:T(8,128)(2,1)S(1)}, u32[]{:S(2)}, u32[]{:S(2)}) collective-permute-start(bf16[2,256,128]{2,1,0:T(8,128)(2,1)S(1)} %get-tuple-element.11), channel_id=1, source_target_pairs={{0,1},{1,2},{2,3},{3,0},{4,5},{5,6},{6,7},{7,4},{8,9},{9,10},{10,1... | collective-permute-start | bytes 393224 | tf_op jit(solution)/shard_map/ppermute | solution.py:232
  56.7 2.8 %collective-permute-start.5 = (bf16[2,256,128]{2,1,0:T(8,128)(2,1)S(1)}, bf16[2,256,128]{2,1,0:T(8,128)(2,1)S(1)}, u32[]{:S(2)}, u32[]{:S(2)}) collective-permute-start(bf16[2,256,128]{2,1,0:T(8,128)(2,1)S(1)} %get-tuple-element.12), channel_id=1, source_target_pairs={{0,2},{1,3},{2,0},{3,1},{4,6},{5,7},{6,4},{7,5},{8,10},{9,11},{10,... | collective-permute-start | bytes 393224 | tf_op jit(solution)/shard_map/ppermute | solution.py:232
  59.5 1.3 %collective-permute-start.6 = (bf16[2,256,128]{2,1,0:T(8,128)(2,1)S(1)}, bf16[2,256,128]{2,1,0:T(8,128)(2,1)S(1)}, u32[]{:S(2)}, u32[]{:S(2)}) collective-permute-start(bf16[2,256,128]{2,1,0:T(8,128)(2,1)S(1)} %get-tuple-element.13), channel_id=1, source_target_pairs={{0,3},{1,0},{2,1},{3,2},{4,7},{5,4},{6,5},{7,6},{8,11},{9,8},{10,9... | collective-permute-start | bytes 393224 | tf_op jit(solution)/shard_map/ppermute | solution.py:232
  60.7 2.6 %collective-permute-done.4 = bf16[2,256,128]{2,1,0:T(8,128)(2,1)S(1)} collective-permute-done((bf16[2,256,128]{2,1,0:T(8,128)(2,1)S(1)}, bf16[2,256,128]{2,1,0:T(8,128)(2,1)S(1)}, u32[]{:S(2)}, u32[]{:S(2)}) %collective-permute-start.4) | collective-permute-done | bytes 131104 | tf_op jit(solution)/shard_map/ppermute | solution.py:232
  63.4 3.3 %collective-permute-done.5 = bf16[2,256,128]{2,1,0:T(8,128)(2,1)S(1)} collective-permute-done((bf16[2,256,128]{2,1,0:T(8,128)(2,1)S(1)}, bf16[2,256,128]{2,1,0:T(8,128)(2,1)S(1)}, u32[]{:S(2)}, u32[]{:S(2)}) %collective-permute-start.5) | collective-permute-done | bytes 131104 | tf_op jit(solution)/shard_map/ppermute | solution.py:232
  66.8 4.2 %collective-permute-start.9 = (bf16[2,256,128]{2,1,0:T(8,128)(2,1)S(1)}, bf16[2,256,128]{2,1,0:T(8,128)(2,1)S(1)}, u32[]{:S(2)}, u32[]{:S(2)}) collective-permute-start(bf16[2,256,128]{2,1,0:T(8,128)(2,1)S(1)} %add_convert_fusion), channel_id=1, source_target_pairs={{0,3},{1,0},{2,1},{3,2},{4,7},{5,4},{6,5},{7,6},{8,11},{9,8},{10,9... | collective-permute-start | bytes 393224 | tf_op jit(solution)/shard_map/ppermute | solution.py:232
  71.0 0.6 collective-permute-start.8
  71.6 3.2 %collective-permute-done.9 = bf16[2,256,128]{2,1,0:T(8,128)(2,1)S(1)} collective-permute-done((bf16[2,256,128]{2,1,0:T(8,128)(2,1)S(1)}, bf16[2,256,128]{2,1,0:T(8,128)(2,1)S(1)}, u32[]{:S(2)}, u32[]{:S(2)}) %collective-permute-start.9) | collective-permute-done | bytes 131104 | tf_op jit(solution)/shard_map/ppermute | solution.py:232
  74.9 8.5 %collective-permute-done.8 = bf16[2,256,128]{2,1,0:T(8,128)(2,1)S(1)} collective-permute-done((bf16[2,256,128]{2,1,0:T(8,128)(2,1)S(1)}, bf16[2,256,128]{2,1,0:T(8,128)(2,1)S(1)}, u32[]{:S(2)}, u32[]{:S(2)}) %collective-permute-start.8) | collective-permute-done | bytes 131104 | tf_op jit(solution)/shard_map/ppermute | solution.py:232
  83.4 1.6 %collective-permute-start.10 = (bf16[4,2,256,128]{3,2,1,0:T(8,128)(2,1)S(1)}, bf16[4,2,256,128]{3,2,1,0:T(8,128)(2,1)S(1)}, u32[]{:S(2)}, u32[]{:S(2)}) collective-permute-start(bf16[4,2,256,128]{3,2,1,0:T(8,128)(2,1)S(1)} %get-tuple-element.25), channel_id=1, source_target_pairs={{0,8},{4,20},{8,0},{12,28},{16,24},{20,4},{24,16},{28,12},{1,9},{5... | collective-permute-start | bytes 1572872 | tf_op jit(solution)/shard_map/ppermute | solution.py:229
  85.0 1.5 %collective-permute-start.11 = (bf16[4,2,256,128]{3,2,1,0:T(8,128)(2,1)S(1)}, bf16[4,2,256,128]{3,2,1,0:T(8,128)(2,1)S(1)}, u32[]{:S(2)}, u32[]{:S(2)}) collective-permute-start(bf16[4,2,256,128]{3,2,1,0:T(8,128)(2,1)S(1)} %get-tuple-element.25), channel_id=1, source_target_pairs={{0,16},{4,12},{8,24},{12,4},{16,0},{20,28},{24,8},{28,20},{1,17},{... | collective-permute-start | bytes 1572872 | tf_op jit(solution)/shard_map/ppermute | solution.py:229
  86.6 11.6 %collective-permute-done.10 = bf16[4,2,256,128]{3,2,1,0:T(8,128)(2,1)S(1)} collective-permute-done((bf16[4,2,256,128]{3,2,1,0:T(8,128)(2,1)S(1)}, bf16[4,2,256,128]{3,2,1,0:T(8,128)(2,1)S(1)}, u32[]{:S(2)}, u32[]{:S(2)}) %collective-permute-start.10) | collective-permute-done | bytes 524320 | tf_op jit(solution)/shard_map/ppermute | solution.py:229
  98.4 0.5 collective-permute-start.15
  98.9 8.6 %collective-permute-done.12 = bf16[4,2,256,128]{3,2,1,0:T(8,128)(2,1)} collective-permute-done((bf16[4,2,256,128]{3,2,1,0:T(8,128)(2,1)S(1)}, bf16[4,2,256,128]{3,2,1,0:T(8,128)(2,1)}, u32[]{:S(2)}, u32[]{:S(2)}) %collective-permute-start.12) | collective-permute-done | bytes 524320 | tf_op jit(solution)/shard_map/ppermute | solution.py:229
  107.5 0.8 copy.17
  108.3 1.3 %pad_maximum_fusion.refs_0_ = bf16[4,4,2,256,128]{4,3,2,1,0:T(8,128)(2,1)S(1)} fusion(bf16[1,4,2,256,128]{4,3,2,1,0:T(8,128)(2,1)} %bitcast.15, bf16[1,4,2,256,128]{4,3,2,1,0:T(8,128)(2,1)S(1)} %bitcast.43, bf16[1,4,2,256,128]{4,3,2,1,0:T(8,128)(2,1)S(1)} %bitcast.42, bf16[1,4,2,256,128]{4,3,2,1,0:T(8,128)(2,1)S(1)} %get-tuple-element.24), kind=kLoop, calls=%fused_computation | loop fusion | flops 3145728 | bytes 4194304 | tf_op jit(solution)/shard_map/stack | solution.py:263
  109.7 1.3 %pad_maximum_fusion.1.refs_1_ = bf16[4,4,2,256,128]{4,3,2,1,0:T(8,128)(2,1)S(1)} fusion(bf16[1,4,2,256,128]{4,3,2,1,0:T(8,128)(2,1)S(1)} %bitcast.45, bf16[1,4,2,256,128]{4,3,2,1,0:T(8,128)(2,1)} %bitcast.18, bf16[1,4,2,256,128]{4,3,2,1,0:T(8,128)(2,1)S(1)} %bitcast.44, bf16[1,4,2,256,128]{4,3,2,1,0:T(8,128)(2,1)S(1)} %bitcast.41), kind=kLoop, calls=%fused_computation.1 | loop fusion | flops 3145728 | bytes 4194304 | tf_op jit(solution)/shard_map/stack | solution.py:264
  111.0 6.3 %shard_map.79 = f32[2,128,4096]{2,1,0:T(8,128)} custom-call(s32[3]{0:T(128)S(1)} %pad_add_fusion.place_ref, bf16[4,4,2,256,128]{4,3,2,1,0:T(8,128)(2,1)S(1)} %pad_maximum_fusion.refs_0_, bf16[4,4,2,256,128]{4,3,2,1,0:T(8,128)(2,1)S(1)} %pad_maximum_fusion.1.refs_1_, bf16[256,128]{1,0:T(8,128)(2,1)S(1)} %slice_bitcast_fusion.1.refs_2_, ...), custom_call_target="tpu_custom_call" | custom-call | tf_op jit(solution)/shard_map/pallas_call | solution.py:197
  (37 shorter events, 1.1 us)
Async XLA Ops:
  1.4 1.0 copy-start
  2.4 31.9 %copy-start.1 = (bf16[2,500,512]{2,0,1:T(2,128)(2,1)S(1)}, bf16[2,500,512]{2,0,1:T(2,128)(2,1)}, u32[]{:S(2)}) copy-start(bf16[2,500,512]{2,0,1:T(2,128)(2,1)} %param.11) | copy-start | bytes 3072004
  33.8 3.8 %collective-permute-start = (f32[500,256]{1,0:T(8,128)S(1)}, f32[500,256]{1,0:T(8,128)}, u32[]{:S(2)}, u32[]{:S(2)}) collective-permute-start(f32[500,256]{1,0:T(8,128)S(1)} %get-tuple-element.9), channel_id=1, source_target_pairs={{0,4},{4,0},{8,12},{12,8},{16,20},{20,16},{24,28},{28,24},{1,5},{5... | collective-permute-start | bytes 1536008 | tf_op jit(solution)/shard_map/ppermute | solution.py:223
  37.5 10.7 %copy-start.2 = (f32[2,500]{1,0:T(2,128)S(1)}, f32[2,500]{1,0:T(2,128)}, u32[]{:S(2)}) copy-start(f32[2,500]{1,0:T(2,128)} %param.10) | copy-start | bytes 12004
  37.6 10.9 %copy-start.3 = (f32[2,256]{1,0:T(2,128)S(1)}, f32[2,256]{1,0:T(2,128)}, u32[]{:S(2)}) copy-start(f32[2,256]{1,0:T(2,128)} %param.8) | copy-start | bytes 6148
  37.6 10.9 %collective-permute-start.3 = (bf16[2,500,512]{2,0,1:T(2,128)(2,1)}, bf16[2,500,512]{2,0,1:T(2,128)(2,1)S(1)}, u32[]{:S(2)}, u32[]{:S(2)}) collective-permute-start(bf16[2,500,512]{2,0,1:T(2,128)(2,1)} %copy.15), channel_id=1, source_target_pairs={{0,4},{4,0},{8,12},{12,8},{16,20},{20,16},{24,28},{28,24},{1,5},{5... | collective-permute-start | bytes 3072008 | tf_op jit(solution)/shard_map/ppermute | solution.py:223
  38.7 7.3 %collective-permute-start.1 = (bf16[500,256]{1,0:T(8,128)(2,1)S(1)}, bf16[500,256]{1,0:T(8,128)(2,1)S(1)}, u32[]{:S(2)}, u32[]{:S(2)}) collective-permute-start(bf16[500,256]{1,0:T(8,128)(2,1)S(1)} %get-tuple-element.20), channel_id=1, source_target_pairs={{0,8},{4,20},{8,0},{12,28},{16,24},{20,4},{24,16},{28,12},{1,9},{5... | collective-permute-start | bytes 768008 | tf_op jit(solution)/shard_map/ppermute | solution.py:229
  46.1 6.4 %collective-permute-start.2 = (bf16[500,256]{1,0:T(8,128)(2,1)S(1)}, bf16[500,256]{1,0:T(8,128)(2,1)S(1)}, u32[]{:S(2)}, u32[]{:S(2)}) collective-permute-start(bf16[500,256]{1,0:T(8,128)(2,1)S(1)} %get-tuple-element.18), channel_id=1, source_target_pairs={{0,16},{4,12},{8,24},{12,4},{16,0},{20,28},{24,8},{28,20},{1,17},{... | collective-permute-start | bytes 768008 | tf_op jit(solution)/shard_map/ppermute | solution.py:229
  53.6 9.7 %collective-permute-start.4 = (bf16[2,256,128]{2,1,0:T(8,128)(2,1)S(1)}, bf16[2,256,128]{2,1,0:T(8,128)(2,1)S(1)}, u32[]{:S(2)}, u32[]{:S(2)}) collective-permute-start(bf16[2,256,128]{2,1,0:T(8,128)(2,1)S(1)} %get-tuple-element.11), channel_id=1, source_target_pairs={{0,1},{1,2},{2,3},{3,0},{4,5},{5,6},{6,7},{7,4},{8,9},{9,10},{10,1... | collective-permute-start | bytes 393224 | tf_op jit(solution)/shard_map/ppermute | solution.py:232
  56.7 10.0 %collective-permute-start.5 = (bf16[2,256,128]{2,1,0:T(8,128)(2,1)S(1)}, bf16[2,256,128]{2,1,0:T(8,128)(2,1)S(1)}, u32[]{:S(2)}, u32[]{:S(2)}) collective-permute-start(bf16[2,256,128]{2,1,0:T(8,128)(2,1)S(1)} %get-tuple-element.12), channel_id=1, source_target_pairs={{0,2},{1,3},{2,0},{3,1},{4,6},{5,7},{6,4},{7,5},{8,10},{9,11},{10,... | collective-permute-start | bytes 393224 | tf_op jit(solution)/shard_map/ppermute | solution.py:232
  59.5 7.3 %collective-permute-start.6 = (bf16[2,256,128]{2,1,0:T(8,128)(2,1)S(1)}, bf16[2,256,128]{2,1,0:T(8,128)(2,1)S(1)}, u32[]{:S(2)}, u32[]{:S(2)}) collective-permute-start(bf16[2,256,128]{2,1,0:T(8,128)(2,1)S(1)} %get-tuple-element.13), channel_id=1, source_target_pairs={{0,3},{1,0},{2,1},{3,2},{4,7},{5,4},{6,5},{7,6},{8,11},{9,8},{10,9... | collective-permute-start | bytes 393224 | tf_op jit(solution)/shard_map/ppermute | solution.py:232
  66.8 8.1 %collective-permute-start.9 = (bf16[2,256,128]{2,1,0:T(8,128)(2,1)S(1)}, bf16[2,256,128]{2,1,0:T(8,128)(2,1)S(1)}, u32[]{:S(2)}, u32[]{:S(2)}) collective-permute-start(bf16[2,256,128]{2,1,0:T(8,128)(2,1)S(1)} %add_convert_fusion), channel_id=1, source_target_pairs={{0,3},{1,0},{2,1},{3,2},{4,7},{5,4},{6,5},{7,6},{8,11},{9,8},{10,9... | collective-permute-start | bytes 393224 | tf_op jit(solution)/shard_map/ppermute | solution.py:232
  71.0 12.4 %collective-permute-start.8 = (bf16[2,256,128]{2,1,0:T(8,128)(2,1)S(1)}, bf16[2,256,128]{2,1,0:T(8,128)(2,1)S(1)}, u32[]{:S(2)}, u32[]{:S(2)}) collective-permute-start(bf16[2,256,128]{2,1,0:T(8,128)(2,1)S(1)} %add_convert_fusion), channel_id=1, source_target_pairs={{0,2},{1,3},{2,0},{3,1},{4,6},{5,7},{6,4},{7,5},{8,10},{9,11},{10,... | collective-permute-start | bytes 393224 | tf_op jit(solution)/shard_map/ppermute | solution.py:232
  71.5 11.8 %collective-permute-start.7 = (bf16[2,256,128]{2,1,0:T(8,128)(2,1)S(1)}, bf16[2,256,128]{2,1,0:T(8,128)(2,1)S(1)}, u32[]{:S(2)}, u32[]{:S(2)}) collective-permute-start(bf16[2,256,128]{2,1,0:T(8,128)(2,1)S(1)} %add_convert_fusion), channel_id=1, source_target_pairs={{0,1},{1,2},{2,3},{3,0},{4,5},{5,6},{6,7},{7,4},{8,9},{9,10},{10,1... | collective-permute-start | bytes 393224 | tf_op jit(solution)/shard_map/ppermute | solution.py:232
  83.4 14.8 %collective-permute-start.10 = (bf16[4,2,256,128]{3,2,1,0:T(8,128)(2,1)S(1)}, bf16[4,2,256,128]{3,2,1,0:T(8,128)(2,1)S(1)}, u32[]{:S(2)}, u32[]{:S(2)}) collective-permute-start(bf16[4,2,256,128]{3,2,1,0:T(8,128)(2,1)S(1)} %get-tuple-element.25), channel_id=1, source_target_pairs={{0,8},{4,20},{8,0},{12,28},{16,24},{20,4},{24,16},{28,12},{1,9},{5... | collective-permute-start | bytes 1572872 | tf_op jit(solution)/shard_map/ppermute | solution.py:229
  85.0 13.4 %collective-permute-start.11 = (bf16[4,2,256,128]{3,2,1,0:T(8,128)(2,1)S(1)}, bf16[4,2,256,128]{3,2,1,0:T(8,128)(2,1)S(1)}, u32[]{:S(2)}, u32[]{:S(2)}) collective-permute-start(bf16[4,2,256,128]{3,2,1,0:T(8,128)(2,1)S(1)} %get-tuple-element.25), channel_id=1, source_target_pairs={{0,16},{4,12},{8,24},{12,4},{16,0},{20,28},{24,8},{28,20},{1,17},{... | collective-permute-start | bytes 1572872 | tf_op jit(solution)/shard_map/ppermute | solution.py:229
  86.5 12.4 %collective-permute-start.13 = (bf16[4,2,256,128]{3,2,1,0:T(8,128)(2,1)S(1)}, bf16[4,2,256,128]{3,2,1,0:T(8,128)(2,1)S(1)}, u32[]{:S(2)}, u32[]{:S(2)}) collective-permute-start(bf16[4,2,256,128]{3,2,1,0:T(8,128)(2,1)S(1)} %get-tuple-element.25), channel_id=1, source_target_pairs={{0,4},{4,0},{8,12},{12,8},{16,20},{20,16},{24,28},{28,24},{1,5},{5... | collective-permute-start | bytes 1572872 | tf_op jit(solution)/shard_map/ppermute | solution.py:223
  98.2 9.3 %collective-permute-start.12 = (bf16[4,2,256,128]{3,2,1,0:T(8,128)(2,1)S(1)}, bf16[4,2,256,128]{3,2,1,0:T(8,128)(2,1)}, u32[]{:S(2)}, u32[]{:S(2)}) collective-permute-start(bf16[4,2,256,128]{3,2,1,0:T(8,128)(2,1)S(1)} %collective-permute-done.10), channel_id=1, source_target_pairs={{0,16},{4,12},{8,24},{12,4},{16,0},{20,28},{24,8},{28,20},{1,17},{... | collective-permute-start | bytes 1572872 | tf_op jit(solution)/shard_map/ppermute | solution.py:229
  98.4 11.3 %collective-permute-start.14 = (bf16[4,2,256,128]{3,2,1,0:T(8,128)(2,1)S(1)}, bf16[4,2,256,128]{3,2,1,0:T(8,128)(2,1)S(1)}, u32[]{:S(2)}, u32[]{:S(2)}) collective-permute-start(bf16[4,2,256,128]{3,2,1,0:T(8,128)(2,1)S(1)} %collective-permute-done.10), channel_id=1, source_target_pairs={{0,4},{4,0},{8,12},{12,8},{16,20},{20,16},{24,28},{28,24},{1,5},{5... | collective-permute-start | bytes 1572872 | tf_op jit(solution)/shard_map/ppermute | solution.py:223
  98.4 11.2 %collective-permute-start.15 = (bf16[4,2,256,128]{3,2,1,0:T(8,128)(2,1)S(1)}, bf16[4,2,256,128]{3,2,1,0:T(8,128)(2,1)}, u32[]{:S(2)}, u32[]{:S(2)}) collective-permute-start(bf16[4,2,256,128]{3,2,1,0:T(8,128)(2,1)S(1)} %collective-permute-done.11), channel_id=1, source_target_pairs={{0,4},{4,0},{8,12},{12,8},{16,20},{20,16},{24,28},{28,24},{1,5},{5... | collective-permute-start | bytes 1572872 | tf_op jit(solution)/shard_map/ppermute | solution.py:223
  107.5 2.1 %collective-permute-start.16 = (bf16[4,2,256,128]{3,2,1,0:T(8,128)(2,1)}, bf16[4,2,256,128]{3,2,1,0:T(8,128)(2,1)S(1)}, u32[]{:S(2)}, u32[]{:S(2)}) collective-permute-start(bf16[4,2,256,128]{3,2,1,0:T(8,128)(2,1)} %collective-permute-done.12), channel_id=1, source_target_pairs={{0,4},{4,0},{8,12},{12,8},{16,20},{20,16},{24,28},{28,24},{1,5},{5... | collective-permute-start | bytes 1572872 | tf_op jit(solution)/shard_map/ppermute | solution.py:223

commit v3 on v1

v3 whole, which is shorter than its diff:
```python
import functools

import jax
import jax.numpy as jnp
from jax import lax
from jax.experimental import pallas as pl
from jax.experimental.pallas import tpu as pltpu
from jax.sharding import PartitionSpec as P

SINE = (4.441535719696892, -7.264680836400963, 3.2520496076552887)
COSINE = (1.414204080330576, -6.977642043687199, 5.715238221214665, -1.7283481089755481)
COORD_PIECES = (0, 0, 1, 1, 0, 2)
WAVE_PIECES = (0, 1, 0, 1, 2, 0)
TURNS = 0.15915494309189535
CHUNKS = 2
BIG = pltpu.CompilerParams(vmem_limit_bytes=48 << 20)


def circle(turns):
    r = turns - jnp.round(turns)
    u = r * r
    s = r * (SINE[0] + u * (SINE[1] + u * SINE[2]))
    c = COSINE[0] + u * (COSINE[1] + u * (COSINE[2] + u * COSINE[3]))
    return c * c - 1.0, s * c


def pieces(x, order):
    first = x.astype(jnp.bfloat16).astype(jnp.float32)
    second = (x - first).astype(jnp.bfloat16).astype(jnp.float32)
    third = x - first - second
    blank = jnp.zeros((8 - x.shape[0], x.shape[1]), jnp.float32)
    parts = [jnp.concatenate([p, blank], axis=0) for p in (first, second, third)]
    return jnp.concatenate([parts[i] for i in order], axis=0).astype(jnp.bfloat16)


def forces_kernel(
    piece,
    sub,
    coords_ref,
    wave_ref,
    shapes_ref,
    mine_ref,
    other_ref,
    wave_pieces,
    even_turns,
    odd_turns,
    even,
    odd,
):
    step, steps = pl.program_id(0), pl.num_programs(0)
    waves = wave_ref.shape[1]
    own = waves // 2
    count = shapes_ref.shape[1] // piece
    nodes = coords_ref.shape[1]
    turns, load = (even_turns, odd_turns), (even, odd)

    def phase(start, into):
        for j in range(0, piece, sub):
            at = pl.multiple_of(start + j, sub)
            into[j : j + sub, :] = lax.dot_general(
                pieces(coords_ref[:, pl.ds(at, sub)], COORD_PIECES),
                wave_pieces[...],
                (((0,), (0,)), ((), ())),
                preferred_element_type=jnp.float32,
            )

    def points(angles, into):
        for j in range(0, piece, 64):
            rows = slice(j, j + 64)
            cosine, sine = (x.astype(jnp.bfloat16) for x in circle(angles[rows, :]))
            into[rows, :own] = cosine[:, :own]
            into[rows, own : 2 * own] = sine[:, :own]
            into[rows, 2 * own : 3 * own] = cosine[:, own:]
            into[rows, 3 * own :] = sine[:, own:]

    @pl.when(step == 0)
    def _():
        first, second = wave_ref[:, :own], wave_ref[:, own:]
        swap = lax.rem(lax.axis_index("node"), 2) == 1
        ordered = jnp.concatenate(
            [jnp.where(swap, second, first), jnp.where(swap, first, second)], axis=1
        )
        wave_pieces[...] = pieces(ordered * TURNS, WAVE_PIECES)
        mine_ref[...] = jnp.zeros_like(mine_ref)
        other_ref[...] = jnp.zeros_like(other_ref)
        phase(0, turns[0])
        phase(piece, turns[1])
        points(turns[0], load[0])

    for p in range(count):
        ahead = (step * count + p + 2) * piece
        phase(jnp.where(ahead >= nodes, 0, ahead), turns[p % 2])
        points(turns[(p + 1) % 2], load[(p + 1) % 2])
        product = jnp.dot(
            shapes_ref[:, p * piece : (p + 1) * piece],
            load[p % 2][...],
            preferred_element_type=jnp.float32,
        )
        mine_ref[...] += product[:, :waves]
        other_ref[...] += product[:, waves:]


def unit_forces(coords, wavevec, mode_shapes):
    modes, nodes = mode_shapes.shape
    waves = wavevec.shape[1]
    block, piece, sub = 4096, 1024, 256
    out = jax.ShapeDtypeStruct((modes, waves), jnp.float32)
    return pl.pallas_call(
        functools.partial(forces_kernel, piece, sub),
        grid=(nodes // block,),
        in_specs=[
            pl.BlockSpec((3, nodes), lambda i: (0, 0)),
            pl.BlockSpec((3, waves), lambda i: (0, 0)),
            pl.BlockSpec((modes, block), lambda i: (0, i)),
        ],
        out_specs=[pl.BlockSpec((modes, waves), lambda i: (0, 0))] * 2,
        out_shape=[out, out],
        scratch_shapes=[
            pltpu.VMEM((8 * len(WAVE_PIECES), waves), jnp.bfloat16),
            pltpu.VMEM((piece, waves), jnp.float32),
            pltpu.VMEM((piece, waves), jnp.float32),
            pltpu.VMEM((piece, 2 * waves), jnp.bfloat16),
            pltpu.VMEM((piece, 2 * waves), jnp.bfloat16),
        ],
        compiler_params=BIG,
        cost_estimate=pl.CostEstimate(
            flops=12 * modes * nodes * waves, bytes_accessed=2 * modes * nodes, transcendentals=0
        ),
    )(coords, wavevec, mode_shapes)


def field_kernel(
    blocks, kept_ref, last_ref, amp_ref, frf_ref, own_ref, mate_ref, *refs
):
    totals, sends, whole = refs[:CHUNKS], refs[CHUNKS:-1], refs[-1]
    forces = kept_ref[...] + last_ref[...].astype(jnp.float32)
    waves = forces.shape[1] // 2
    cosine, sine = forces[:, :waves], forces[:, waves:]
    swap = lax.rem(lax.axis_index("node"), 2) == 1
    amp = jnp.where(swap, amp_ref[:, waves:], amp_ref[:, :waves])
    amp_real, amp_imag = amp[0:1, :], amp[1:2, :]
    force_real = amp_real * cosine - amp_imag * sine
    force_imag = amp_real * sine + amp_imag * cosine
    frf = frf_ref[...].T
    gain_real, gain_imag = frf[:, 0:1], frf[:, 1:2]
    real = gain_real * force_real - gain_imag * force_imag
    imag = gain_real * force_imag + gain_imag * force_real
    upper = jnp.concatenate([real, imag], axis=1).astype(jnp.bfloat16)
    lower = jnp.concatenate([-imag, real], axis=1).astype(jnp.bfloat16)
    over_modes = (((0,), (0,)), ((), ()))
    width = own_ref.shape[2] // blocks
    size = waves // CHUNKS
    turned = width % 128 != 0
    for side, transfer in enumerate((own_ref, mate_ref)):
        whole[...] = lax.dot_general(
            upper, transfer[0], over_modes, preferred_element_type=jnp.float32
        ) + lax.dot_general(lower, transfer[1], over_modes, preferred_element_type=jnp.float32)
        for k in range(blocks):
            if turned:
                field = whole[:, k * width : (k + 1) * width]
            else:
                to = lax.rem(lax.axis_index("mode") + k, blocks)
                field = whole[:, pl.ds(pl.multiple_of(to * width, width), width)]
            for c in range(CHUNKS):
                part = jnp.concatenate(
                    [
                        field[c * size : (c + 1) * size],
                        field[waves + c * size : waves + (c + 1) * size],
                    ],
                    axis=0,
                )
                if k == 0:
                    totals[c][side] = part
                else:
                    sends[c * (blocks - 1) + k - 1][side] = part.astype(jnp.bfloat16)


def partial_fields(blocks, kept, last, amp, frf, own, mate):
    waves = kept.shape[1]
    width = own.shape[2] // blocks
    shape = (2, waves // CHUNKS, width)
    if width % 128 != 0:
        mode = lax.axis_index("mode")

        def turn(x):
            doubled = jnp.concatenate([x, x[:, :, : (blocks - 1) * width]], axis=2)
            return lax.dynamic_slice_in_dim(doubled, mode * width, blocks * width, 2)

        own, mate = turn(own), turn(mate)
    out = pl.pallas_call(
        functools.partial(field_kernel, blocks),
        out_shape=[jax.ShapeDtypeStruct(shape, jnp.float32)] * CHUNKS
        + [jax.ShapeDtypeStruct(shape, jnp.bfloat16)] * (CHUNKS * (blocks - 1)),
        scratch_shapes=[pltpu.VMEM((waves, own.shape[2]), jnp.float32)],
        compiler_params=BIG,
        cost_estimate=pl.CostEstimate(
            flops=8 * own.shape[1] * own.shape[2] * waves,
            bytes_accessed=4 * own.size,
            transcendentals=0,
        ),
    )(kept, last, amp, frf, own, mate)
    return out[:CHUNKS], [
        out[CHUNKS + c * (blocks - 1) : CHUNKS + (c + 1) * (blocks - 1)] for c in range(CHUNKS)
    ]


def own_rows_kernel(*refs):
    fields, left, pressure = refs[:-2], refs[-2], refs[-1]
    rows = left.shape[1] // 2
    size = left.shape[2] // 2
    waves = pressure.shape[1] // 2
    swap = lax.rem(lax.axis_index("node"), 2) == 1
    turned = [ref[...].astype(jnp.float32).T for ref in fields]
    for n, field in enumerate(turned):
        real, imag = field[:, :size], field[:, size:]
        left[n, :rows] = field.astype(jnp.bfloat16)
        left[n, rows:] = jnp.concatenate([imag, -real], axis=1).astype(jnp.bfloat16)
    real = [field[:, :size] for field in turned]
    imag = [field[:, size:] for field in turned]
    for part, at in ((real, 0), (imag, waves)):
        ours = jnp.concatenate(part[:CHUNKS], axis=1)
        theirs = jnp.concatenate(part[CHUNKS:], axis=1)
        half = slice(at, at + waves // 2), slice(at + waves // 2, at + waves)
        pressure[:, half[0]] = jnp.where(swap, theirs, ours).astype(jnp.bfloat16)
        pressure[:, half[1]] = jnp.where(swap, ours, theirs).astype(jnp.bfloat16)


def own_rows(fields):
    depth, rows = fields[0].shape
    return pl.pallas_call(
        own_rows_kernel,
        out_shape=[
            jax.ShapeDtypeStruct((len(fields), 2 * rows, depth), jnp.bfloat16),
            jax.ShapeDtypeStruct((rows, len(fields) * depth), jnp.bfloat16),
        ],
        compiler_params=BIG,
    )(*fields)


def spectra_kernel(blocks, place_ref, left_ref, *refs):
    data, out_ref = refs[: 2 * CHUNKS], refs[-1]
    depth, rows = data[0].shape[-2:]
    scale = 1.0 / (CHUNKS * depth)
    for z in range(blocks):
        at = lax.rem(lax.axis_index("mode") - z + blocks, blocks)
        total = 0.0
        for n, ref in enumerate(data):
            total = total + jnp.dot(left_ref[n], ref[at], preferred_element_type=jnp.float32)
        out_ref[0, :, z * rows : (z + 1) * rows] = total[:rows] * scale
        out_ref[1, :, z * rows : (z + 1) * rows] = total[rows:] * scale


def cross_spectra(place, blocks, groups, spectra, left, ours, theirs):
    depth, rows = ours[0].shape[-2:]

    def of_ours(s, place_ref):
        return (0, jnp.bitwise_xor(s, place_ref[1]), 0, 0)

    def of_theirs(s, place_ref):
        return (0, jnp.bitwise_xor(s, 1 - place_ref[1]), 0, 0)

    block = (blocks, None, depth, rows)
    started = spectra is not None
    return pl.pallas_call(
        functools.partial(spectra_kernel, blocks),
        grid_spec=pltpu.PrefetchScalarGridSpec(
            num_scalar_prefetch=1,
            grid=(2,),
            in_specs=[pl.BlockSpec(left.shape, lambda s, place_ref: (0, 0, 0))]
            + [pl.BlockSpec(block, of_ours)] * CHUNKS
            + [pl.BlockSpec(block, of_theirs)] * CHUNKS
            + [pl.BlockSpec(memory_space=pl.ANY)] * started,
            out_specs=pl.BlockSpec(
                (2, rows, blocks * rows), lambda s, place_ref: (0, 0, 2 * place_ref[0] + s)
            ),
        ),
        out_shape=jax.ShapeDtypeStruct((2, rows, 2 * groups * blocks * rows), jnp.float32),
        input_output_aliases={2 + 2 * CHUNKS: 0} if started else {},
        compiler_params=BIG,
        cost_estimate=pl.CostEstimate(
            flops=8 * CHUNKS * depth * rows * rows * blocks,
            bytes_accessed=32 * rows * rows * blocks,
            transcendentals=0,
        ),
    )(place, left, *ours, *theirs, *([spectra] if started else []))


def body(nodes, blocks, coords, wavevec, wave_amp, mode_shapes, modal_frf, radiation):
    groups = nodes // 2
    bits = groups.bit_length() - 1
    node = lax.axis_index("node")
    group, core = node // 2, lax.rem(node, 2)

    def reverse(p):
        return sum(((p >> b) & 1) << (bits - 1 - b) for b in range(bits))

    def to_mate(x):
        return lax.ppermute(x, "node", [(i, i ^ 1) for i in range(nodes)])

    def across(x, step):
        def flip(i):
            return i ^ (2 << (step if i % 2 == 0 else bits - 1 - step))

        return lax.ppermute(x, "node", [(i, flip(i)) for i in range(nodes)])

    def along(x, k):
        return lax.ppermute(x, "mode", [(i, (i + k) % blocks) for i in range(blocks)])

    mate = to_mate(radiation)
    mine, other = unit_forces(coords, wavevec, mode_shapes)
    kept = mine + to_mate(other)
    for step in range(bits - 1):
        kept = kept + across(kept.astype(jnp.bfloat16), step).astype(jnp.float32)
    last = across(kept.astype(jnp.bfloat16), bits - 1)
    totals, sends = partial_fields(blocks, kept, last, wave_amp, modal_frf, radiation, mate)

    fields, gathered, mates = [], [], []
    for total, sent in zip(totals, sends):
        for k, block in enumerate(sent):
            total = total + along(block, k + 1).astype(jnp.float32)
        fields.append(total.astype(jnp.bfloat16))
    for field in fields:
        parts = [jnp.stack([field] + [along(field, k) for k in range(1, blocks)])]
        for step in range(bits):
            parts = parts + [across(x, step) for x in parts]
        gathered.append(parts)
        mates.append([to_mate(x) for x in parts])
    left, field_pressure = own_rows(
        [field[0] for field in fields] + [parts[0][0, 1] for parts in mates]
    )
    spectra = None
    for p in range(groups):
        at = jnp.bitwise_xor(group, jnp.where(core == 0, p, reverse(p)))
        spectra = cross_spectra(
            jnp.stack([at, core]).astype(jnp.int32),
            blocks,
            groups,
            spectra,
            left,
            [parts[p] for parts in gathered],
            [parts[reverse(p)] for parts in mates],
        )
    return (spectra, field_pressure)


def solution(mesh):
    placed = (
        P(None, "node"),
        P(),
        P(),
        P("mode", "node"),
        P(None, "mode"),
        P(None, "mode", "node"),
    )
    return jax.shard_map(
        functools.partial(body, mesh.shape["node"], mesh.shape["mode"]),
        mesh=mesh,
        in_specs=placed,
        out_specs=(P(None, ("node", "mode"), None), P(("node", "mode"), None)),
        check_vma=False,
    )
```

time: 207 us -> 104 us (0.50)
  waiting for transfers between devices: 148 us -> 21.5 us
  starting transfers between devices: 0.12 us -> 36.9 us
  between operations: 13.8 us -> 0.8 us
  Pallas kernels: 28.9 us -> 40.9 us
  matrix products: 7.27 us -> 0 us
  other arithmetic: 3.98 us -> 0.5 us
    all_gather x1 -> x0, waiting for transfers between devices: 63.2 us -> none  [body(): lax.all_gather(owned_rows, ('node', 'mode'), axis=0, tiled=True)]
    psum x1 -> x0, waiting for transfers between devices: 58.7 us -> none  [body(): forces = lax.psum(unit_forces(coords, wavevec, mode_shapes), 'node')]
    ppermute x0 -> x30, starting transfers between devices: none -> 36.9 us  [the longest x12 21.5 us: along(): lax.ppermute(x, 'mode', [(i, (i + k) % blocks) for i in range(blocks)])]
    reduce_scatter x1 -> x0, waiting for transfers between devices: 26.3 us -> none  [body(): lax.psum_scatter(project_field(transfer, operand), 'mode', scatter_dimens...]
    ppermute x0 -> x30, waiting for transfers between devices: none -> 21.5 us  [the longest x8 18.8 us: across(): return lax.ppermute(x, 'node', [(i, flip(i)) for i in range(nodes)])]
    pallas_call x1 -> x7, Pallas kernels: 28.9 us -> 40.9 us  [the longest x1 29 us: unit_forces(): pl.pallas_call(functools.partial(forces_kernel, piece, sub), grid=(nodes...]
    dot_general x2 -> x0, matrix products: 7.27 us -> none  [the longest x1 5.56 us: cross_spectra(): lax.dot_general(stacked, others, (((1,), (1,)), ((), ())), preferred_elem...]
  transfers between devices with their start and end apart: 3 -> 30, of which waited for: 3 -> 10; matrix products, arithmetic and copies ran while one was open for 1% -> 2% of each run, Pallas kernels for 0% -> 8%
where the time goes in v3:
time: 104 us
  Pallas kernels  40.9 us (39%)
  starting transfers between devices  36.9 us (35%)
  waiting for transfers between devices  21.5 us (21%)
  local copies, waits for them, and re-layouts  3.25 us (3%)
    pallas_call x1, Pallas kernels, unit_forces(): pl.pallas_call(functools.partial(forces_kernel, piece, sub), grid=(nodes...  29 us
    ppermute x12, starting transfers between devices, along(): lax.ppermute(x, 'mode', [(i, (i + k) % blocks) for i in range(blocks)])  21.5 us
    ppermute x8, waiting for transfers between devices, across(): return lax.ppermute(x, 'node', [(i, flip(i)) for i in range(nodes)])  18.8 us
    ppermute x8, starting transfers between devices, across(): return lax.ppermute(x, 'node', [(i, flip(i)) for i in range(nodes)])  14 us
    pallas_call x4, Pallas kernels, cross_spectra(): pl.pallas_call(functools.partial(spectra_kernel, blocks), grid_spec=pltpu...  9.56 us
  transfers between devices with their start and end apart: 30, of which 10 were waited for; matrix products, arithmetic and copies ran while one was open for 2% of the time, Pallas kernels for 8%

profile of v3, /device:TPU:0, one launch (start us, length us, event | category | flops | bytes accessed | tf_op | source)
XLA Modules:
  0.0 103.8 jit_solution(10323626128166277280)
XLA Ops:
  0.6 1.0 copy-done.2
  2.3 29.0 %shard_map.77 = (f32[500,256]{1,0:T(8,128)S(1)}, f32[500,256]{1,0:T(8,128)S(1)}) custom-call(f32[3,24576]{1,0:T(4,128)S(1)} %copy-done.2, f32[3,256]{1,0:T(4,128)S(1)} %copy-done.3, bf16[500,24576]{1,0:T(8,128)(2,1)} %shapes_ref.1), custom_call_target="tpu_custom_call" | custom-call | flops 37748736000 | bytes 24576000 | tf_op jit(solution)/shard_map/pallas_call | solution.py:108
  31.9 1.4 %collective-permute-done = f32[500,256]{1,0:T(8,128)S(1)} collective-permute-done((f32[500,256]{1,0:T(8,128)S(1)}, f32[500,256]{1,0:T(8,128)S(1)}, u32[]{:S(2)}, u32[]{:S(2)}) %collective-permute-start) | collective-permute-done | bytes 512032 | tf_op jit(solution)/shard_map/ppermute | solution.py:298
  33.4 2.9 %collective-permute-start.1 = (bf16[500,256]{1,0:T(8,128)(2,1)S(1)}, bf16[500,256]{1,0:T(8,128)(2,1)S(1)}, u32[]{:S(2)}, u32[]{:S(2)}) collective-permute-start(bf16[500,256]{1,0:T(8,128)(2,1)S(1)} %get-tuple-element.28), channel_id=1, source_target_pairs={{0,8},{4,20},{8,0},{12,28},{16,24},{20,4},{24,16},{28,12},{1,9},{5... | collective-permute-start | bytes 768008 | tf_op jit(solution)/shard_map/ppermute | solution.py:304
  36.4 4.3 %collective-permute-done.1 = bf16[500,256]{1,0:T(8,128)(2,1)S(1)} collective-permute-done((bf16[500,256]{1,0:T(8,128)(2,1)S(1)}, bf16[500,256]{1,0:T(8,128)(2,1)S(1)}, u32[]{:S(2)}, u32[]{:S(2)}) %collective-permute-start.1) | collective-permute-done | bytes 256032 | tf_op jit(solution)/shard_map/ppermute | solution.py:304
  40.7 2.1 %collective-permute-start.2 = (bf16[500,256]{1,0:T(8,128)(2,1)S(1)}, bf16[500,256]{1,0:T(8,128)(2,1)S(1)}, u32[]{:S(2)}, u32[]{:S(2)}) collective-permute-start(bf16[500,256]{1,0:T(8,128)(2,1)S(1)} %get-tuple-element.26), channel_id=1, source_target_pairs={{0,16},{4,12},{8,24},{12,4},{16,0},{20,28},{24,8},{28,20},{1,17},{... | collective-permute-start | bytes 768008 | tf_op jit(solution)/shard_map/ppermute | solution.py:304
  43.0 1.4 %copy.14.mate_ref = bf16[2,500,512]{2,1,0:T(8,128)(2,1)S(1)} copy(bf16[2,500,512]{2,0,1:T(2,128)(2,1)} %collective-permute-done.3) | data formatting | bytes 2048000 | tf_op jit(solution)/shard_map/ppermute | solution.py:298
  44.4 2.7 %collective-permute-done.2.last_ref = bf16[500,256]{1,0:T(8,128)(2,1)S(1)} collective-permute-done((bf16[500,256]{1,0:T(8,128)(2,1)S(1)}, bf16[500,256]{1,0:T(8,128)(2,1)S(1)}, u32[]{:S(2)}, u32[]{:S(2)}) %collective-permute-start.2) | collective-permute-done | bytes 256032 | tf_op jit(solution)/shard_map/ppermute | solution.py:304
  47.2 1.5 %shard_map.78 = (f32[2,128,128]{2,1,0:T(8,128)S(1)}, f32[2,128,128]{2,1,0:T(8,128)S(1)}, bf16[2,128,128]{2,1,0:T(8,128)(2,1)S(1)}, bf16[2,128,128]{2,1,0:T(8,128...) custom-call(f32[500,256]{1,0:T(8,128)S(1)} %get-tuple-element.27.kep, ...), custom_call_target="tpu_custom_call" | custom-call | flops 524288000 | bytes 2048000 | tf_op jit(solution)/shard_map/pallas_call | solution.py:190
  48.6 2.1 %collective-permute-start.7 = (bf16[2,128,128]{2,1,0:T(8,128)(2,1)S(1)}, bf16[2,128,128]{2,1,0:T(8,128)(2,1)S(1)}, u32[]{:S(2)}, u32[]{:S(2)}) collective-permute-start(bf16[2,128,128]{2,1,0:T(8,128)(2,1)S(1)} %get-tuple-element.21), channel_id=1, source_target_pairs={{0,1},{1,2},{2,3},{3,0},{4,5},{5,6},{6,7},{7,4},{8,9},{9,10},{10,1... | collective-permute-start | bytes 196616 | tf_op jit(solution)/shard_map/ppermute | solution.py:307
  50.8 2.6 %collective-permute-start.8 = (bf16[2,128,128]{2,1,0:T(8,128)(2,1)S(1)}, bf16[2,128,128]{2,1,0:T(8,128)(2,1)S(1)}, u32[]{:S(2)}, u32[]{:S(2)}) collective-permute-start(bf16[2,128,128]{2,1,0:T(8,128)(2,1)S(1)} %get-tuple-element.22), channel_id=1, source_target_pairs={{0,2},{1,3},{2,0},{3,1},{4,6},{5,7},{6,4},{7,5},{8,10},{9,11},{10,... | collective-permute-start | bytes 196616 | tf_op jit(solution)/shard_map/ppermute | solution.py:307
  53.4 1.3 %collective-permute-start.9 = (bf16[2,128,128]{2,1,0:T(8,128)(2,1)S(1)}, bf16[2,128,128]{2,1,0:T(8,128)(2,1)S(1)}, u32[]{:S(2)}, u32[]{:S(2)}) collective-permute-start(bf16[2,128,128]{2,1,0:T(8,128)(2,1)S(1)} %get-tuple-element.23), channel_id=1, source_target_pairs={{0,3},{1,0},{2,1},{3,2},{4,7},{5,4},{6,5},{7,6},{8,11},{9,8},{10,9... | collective-permute-start | bytes 196616 | tf_op jit(solution)/shard_map/ppermute | solution.py:307
  55.8 2.8 %collective-permute-start.6 = (bf16[2,128,128]{2,1,0:T(8,128)(2,1)S(1)}, bf16[2,128,128]{2,1,0:T(8,128)(2,1)S(1)}, u32[]{:S(2)}, u32[]{:S(2)}) collective-permute-start(bf16[2,128,128]{2,1,0:T(8,128)(2,1)S(1)} %get-tuple-element.19), channel_id=1, source_target_pairs={{0,3},{1,0},{2,1},{3,2},{4,7},{5,4},{6,5},{7,6},{8,11},{9,8},{10,9... | collective-permute-start | bytes 196616 | tf_op jit(solution)/shard_map/ppermute | solution.py:307
  59.4 1.1 %collective-permute-start.14 = (bf16[2,128,128]{2,1,0:T(8,128)(2,1)S(1)}, bf16[2,128,128]{2,1,0:T(8,128)(2,1)S(1)}, u32[]{:S(2)}, u32[]{:S(2)}) collective-permute-start(bf16[2,128,128]{2,1,0:T(8,128)(2,1)S(1)} %add_convert_fusion), channel_id=1, source_target_pairs={{0,1},{1,2},{2,3},{3,0},{4,5},{5,6},{6,7},{7,4},{8,9},{9,10},{10,1... | collective-permute-start | bytes 196616 | tf_op jit(solution)/shard_map/ppermute | solution.py:307
  60.5 3.2 %collective-permute-start.15 = (bf16[2,128,128]{2,1,0:T(8,128)(2,1)S(1)}, bf16[2,128,128]{2,1,0:T(8,128)(2,1)S(1)}, u32[]{:S(2)}, u32[]{:S(2)}) collective-permute-start(bf16[2,128,128]{2,1,0:T(8,128)(2,1)S(1)} %add_convert_fusion), channel_id=1, source_target_pairs={{0,2},{1,3},{2,0},{3,1},{4,6},{5,7},{6,4},{7,5},{8,10},{9,11},{10,... | collective-permute-start | bytes 196616 | tf_op jit(solution)/shard_map/ppermute | solution.py:307
  64.3 4.8 %collective-permute-start.10 = (bf16[2,128,128]{2,1,0:T(8,128)(2,1)S(1)}, bf16[2,128,128]{2,1,0:T(8,128)(2,1)S(1)}, u32[]{:S(2)}, u32[]{:S(2)}) collective-permute-start(bf16[2,128,128]{2,1,0:T(8,128)(2,1)S(1)} %add_convert_fusion.1), channel_id=1, source_target_pairs={{0,1},{1,2},{2,3},{3,0},{4,5},{5,6},{6,7},{7,4},{8,9},{9,10},{10,1... | collective-permute-start | bytes 196616 | tf_op jit(solution)/shard_map/ppermute | solution.py:307
  69.3 2.2 %collective-permute-start.12 = (bf16[2,128,128]{2,1,0:T(8,128)(2,1)S(1)}, bf16[2,128,128]{2,1,0:T(8,128)(2,1)S(1)}, u32[]{:S(2)}, u32[]{:S(2)}) collective-permute-start(bf16[2,128,128]{2,1,0:T(8,128)(2,1)S(1)} %add_convert_fusion.1), channel_id=1, source_target_pairs={{0,3},{1,0},{2,1},{3,2},{4,7},{5,4},{6,5},{7,6},{8,11},{9,8},{10,9... | collective-permute-start | bytes 196616 | tf_op jit(solution)/shard_map/ppermute | solution.py:307
  71.6 1.6 %collective-permute-start.25 = (bf16[4,2,128,128]{3,2,1,0:T(8,128)(2,1)S(1)}, bf16[4,2,128,128]{3,2,1,0:T(8,128)(2,1)S(1)}, u32[]{:S(2)}, u32[]{:S(2)}) collective-permute-start(bf16[4,2,128,128]{3,2,1,0:T(8,128)(2,1)S(1)} %pad_maximum_fusion.1.refs_1_), channel_id=1, source_target_pairs={{0,16},{4,12},{8,24},{12,4},{16,0},{20,28},{24,8},{28,20},{1,17},{... | collective-permute-start | bytes 786440 | tf_op jit(solution)/shard_map/ppermute | solution.py:304
  73.3 1.5 %collective-permute-start.20 = (bf16[4,2,128,128]{3,2,1,0:T(8,128)(2,1)S(1)}, bf16[4,2,128,128]{3,2,1,0:T(8,128)(2,1)S(1)}, u32[]{:S(2)}, u32[]{:S(2)}) collective-permute-start(bf16[4,2,128,128]{3,2,1,0:T(8,128)(2,1)S(1)} %pad_maximum_fusion.1.refs_1_), channel_id=1, source_target_pairs={{0,8},{4,20},{8,0},{12,28},{16,24},{20,4},{24,16},{28,12},{1,9},{5... | collective-permute-start | bytes 786440 | tf_op jit(solution)/shard_map/ppermute | solution.py:304
  74.9 1.2 %collective-permute-start.18 = (bf16[4,2,128,128]{3,2,1,0:T(8,128)(2,1)S(1)}, bf16[4,2,128,128]{3,2,1,0:T(8,128)(2,1)S(1)}, u32[]{:S(2)}, u32[]{:S(2)}) collective-permute-start(bf16[4,2,128,128]{3,2,1,0:T(8,128)(2,1)S(1)} %pad_maximum_fusion.refs_0_), channel_id=1, source_target_pairs={{0,8},{4,20},{8,0},{12,28},{16,24},{20,4},{24,16},{28,12},{1,9},{5... | collective-permute-start | bytes 786440 | tf_op jit(solution)/shard_map/ppermute | solution.py:304
  76.2 1.6 %collective-permute-start.24 = (bf16[4,2,128,128]{3,2,1,0:T(8,128)(2,1)S(1)}, bf16[4,2,128,128]{3,2,1,0:T(8,128)(2,1)S(1)}, u32[]{:S(2)}, u32[]{:S(2)}) collective-permute-start(bf16[4,2,128,128]{3,2,1,0:T(8,128)(2,1)S(1)} %pad_maximum_fusion.refs_0_), channel_id=1, source_target_pairs={{0,16},{4,12},{8,24},{12,4},{16,0},{20,28},{24,8},{28,20},{1,17},{... | collective-permute-start | bytes 786440 | tf_op jit(solution)/shard_map/ppermute | solution.py:304
  77.7 2.4 %collective-permute-done.25.refs_1_ = bf16[4,2,128,128]{3,2,1,0:T(8,128)(2,1)S(1)} collective-permute-done((bf16[4,2,128,128]{3,2,1,0:T(8,128)(2,1)S(1)}, bf16[4,2,128,128]{3,2,1,0:T(8,128)(2,1)S(1)}, u32[]{:S(2)}, u32[]{:S(2)}) %collective-permute-start.25) | collective-permute-done | bytes 262176 | tf_op jit(solution)/shard_map/ppermute | solution.py:304
  80.2 1.2 %collective-permute-done.20.refs_1_ = bf16[4,2,128,128]{3,2,1,0:T(8,128)(2,1)S(1)} collective-permute-done((bf16[4,2,128,128]{3,2,1,0:T(8,128)(2,1)S(1)}, bf16[4,2,128,128]{3,2,1,0:T(8,128)(2,1)S(1)}, u32[]{:S(2)}, u32[]{:S(2)}) %collective-permute-start.20) | collective-permute-done | bytes 262176 | tf_op jit(solution)/shard_map/ppermute | solution.py:304
  81.4 1.5 %collective-permute-start.21 = (bf16[4,2,128,128]{3,2,1,0:T(8,128)(2,1)S(1)}, bf16[4,2,128,128]{3,2,1,0:T(8,128)(2,1)S(1)}, u32[]{:S(2)}, u32[]{:S(2)}) collective-permute-start(bf16[4,2,128,128]{3,2,1,0:T(8,128)(2,1)S(1)} %collective-permute-done.20.refs_1_), channel_id=1, source_target_pairs={{0,16},{4,12},{8,24},{12,4},{16,0},{20,28},{24,8},{28,20},{1,17},{... | collective-permute-start | bytes 786440 | tf_op jit(solution)/shard_map/ppermute | solution.py:304
  82.9 4.1 %collective-permute-done.18.refs_0_ = bf16[4,2,128,128]{3,2,1,0:T(8,128)(2,1)S(1)} collective-permute-done((bf16[4,2,128,128]{3,2,1,0:T(8,128)(2,1)S(1)}, bf16[4,2,128,128]{3,2,1,0:T(8,128)(2,1)S(1)}, u32[]{:S(2)}, u32[]{:S(2)}) %collective-permute-start.18) | collective-permute-done | bytes 262176 | tf_op jit(solution)/shard_map/ppermute | solution.py:304
  87.0 1.5 %collective-permute-start.19 = (bf16[4,2,128,128]{3,2,1,0:T(8,128)(2,1)S(1)}, bf16[4,2,128,128]{3,2,1,0:T(8,128)(2,1)S(1)}, u32[]{:S(2)}, u32[]{:S(2)}) collective-permute-start(bf16[4,2,128,128]{3,2,1,0:T(8,128)(2,1)S(1)} %collective-permute-done.18.refs_0_), channel_id=1, source_target_pairs={{0,16},{4,12},{8,24},{12,4},{16,0},{20,28},{24,8},{28,20},{1,17},{... | collective-permute-start | bytes 786440 | tf_op jit(solution)/shard_map/ppermute | solution.py:304
  89.6 3.8 %collective-permute-done.19.refs_0_ = bf16[4,2,128,128]{3,2,1,0:T(8,128)(2,1)S(1)} collective-permute-done((bf16[4,2,128,128]{3,2,1,0:T(8,128)(2,1)S(1)}, bf16[4,2,128,128]{3,2,1,0:T(8,128)(2,1)S(1)}, u32[]{:S(2)}, u32[]{:S(2)}) %collective-permute-start.19) | collective-permute-done | bytes 262176 | tf_op jit(solution)/shard_map/ppermute | solution.py:304
  93.4 0.9 shard_map.79
  94.3 2.4 %shard_map.80.refs_4_ = f32[2,128,4096]{2,1,0:T(8,128)} custom-call(s32[2]{0:T(128)S(1)} %pad_add_fusion.3.place_ref, bf16[4,256,128]{2,1,0:T(8,128)(2,1)S(1)} %get-tuple-element.24.left_ref, bf16[4,2,128,128]{3,2,1,0:T(8,128)(2,1)S(1)} %pad_maximum_fusion.refs_0_, bf16[4,2,128,128]{3,2,1,0:T(8,128)(2,1)S(1)} %pad_maximum_fusion.1.refs_1_, ...), custom_call_target="tpu_custom_call" | custom-call | flops 134217728 | bytes 2097152 | tf_op jit(solution)/shard_map/pallas_call | solution.py:264
  96.6 2.4 %shard_map.81.refs_4_ = f32[2,128,4096]{2,1,0:T(8,128)} custom-call(s32[2]{0:T(128)S(1)} %pad_add_fusion.2.place_ref, bf16[4,256,128]{2,1,0:T(8,128)(2,1)S(1)} %get-tuple-element.24.left_ref, bf16[4,2,128,128]{3,2,1,0:T(8,128)(2,1)S(1)} %collective-permute-done.18.refs_0_, ...), custom_call_target="tpu_custom_call", output_to_operand_aliasing={{}: (6, {})} | custom-call | flops 134217728 | bytes 2097152 | tf_op jit(solution)/shard_map/pallas_call | solution.py:264
  99.0 2.4 %shard_map.82.refs_4_ = f32[2,128,4096]{2,1,0:T(8,128)} custom-call(s32[2]{0:T(128)S(1)} %get-tuple-element.31.place_ref, bf16[4,256,128]{2,1,0:T(8,128)(2,1)S(1)} %get-tuple-element.24.left_ref, bf16[4,2,128,128]{3,2,1,0:T(8,128)(2,1)S(1)} %collective-permute-done.24.refs_0_, ...), custom_call_target="tpu_custom_call", output_to_operand_aliasing={{}: (6, {})} | custom-call | flops 134217728 | bytes 2097152 | tf_op jit(solution)/shard_map/pallas_call | solution.py:264
  101.4 2.4 %shard_map.83 = f32[2,128,4096]{2,1,0:T(8,128)} custom-call(s32[2]{0:T(128)S(1)} %get-tuple-element.30.place_ref, bf16[4,256,128]{2,1,0:T(8,128)(2,1)S(1)} %get-tuple-element.24.left_ref, bf16[4,2,128,128]{3,2,1,0:T(8,128)(2,1)S(1)} %collective-permute-done.19.refs_0_, ...), custom_call_target="tpu_custom_call", output_to_operand_aliasing={{}: (6, {})} | custom-call | flops 134217728 | bytes 2097152 | tf_op jit(solution)/shard_map/pallas_call | solution.py:264
  (60 shorter events, 5.6 us)
Async XLA Ops:
  2.3 29.5 %copy-start.4 = (bf16[2,500,512]{2,0,1:T(2,128)(2,1)S(1)}, bf16[2,500,512]{2,0,1:T(2,128)(2,1)}, u32[]{:S(2)}) copy-start(bf16[2,500,512]{2,0,1:T(2,128)(2,1)} %param.11) | copy-start | bytes 3072004
  31.3 15.9 %copy-start = (f32[2,500]{1,0:T(2,128)S(1)}, f32[2,500]{1,0:T(2,128)}, u32[]{:S(2)}) copy-start(f32[2,500]{1,0:T(2,128)} %frf_ref.1) | copy-start | bytes 12004
  31.3 2.0 %collective-permute-start = (f32[500,256]{1,0:T(8,128)S(1)}, f32[500,256]{1,0:T(8,128)S(1)}, u32[]{:S(2)}, u32[]{:S(2)}) collective-permute-start(f32[500,256]{1,0:T(8,128)S(1)} %get-tuple-element.15), channel_id=1, source_target_pairs={{0,4},{4,0},{8,12},{12,8},{16,20},{20,16},{24,28},{28,24},{1,5},{5... | collective-permute-start | bytes 1536008 | tf_op jit(solution)/shard_map/ppermute | solution.py:298
  31.8 11.2 %collective-permute-start.3 = (bf16[2,500,512]{2,0,1:T(2,128)(2,1)S(1)}, bf16[2,500,512]{2,0,1:T(2,128)(2,1)}, u32[]{:S(2)}, u32[]{:S(2)}) collective-permute-start(bf16[2,500,512]{2,0,1:T(2,128)(2,1)S(1)} %copy-done.4), channel_id=1, source_target_pairs={{0,4},{4,0},{8,12},{12,8},{16,20},{20,16},{24,28},{28,24},{1,5},{5... | collective-permute-start | bytes 3072008 | tf_op jit(solution)/shard_map/ppermute | solution.py:298
  33.4 7.2 %collective-permute-start.1 = (bf16[500,256]{1,0:T(8,128)(2,1)S(1)}, bf16[500,256]{1,0:T(8,128)(2,1)S(1)}, u32[]{:S(2)}, u32[]{:S(2)}) collective-permute-start(bf16[500,256]{1,0:T(8,128)(2,1)S(1)} %get-tuple-element.28), channel_id=1, source_target_pairs={{0,8},{4,20},{8,0},{12,28},{16,24},{20,4},{24,16},{28,12},{1,9},{5... | collective-permute-start | bytes 768008 | tf_op jit(solution)/shard_map/ppermute | solution.py:304
  40.7 6.4 %collective-permute-start.2 = (bf16[500,256]{1,0:T(8,128)(2,1)S(1)}, bf16[500,256]{1,0:T(8,128)(2,1)S(1)}, u32[]{:S(2)}, u32[]{:S(2)}) collective-permute-start(bf16[500,256]{1,0:T(8,128)(2,1)S(1)} %get-tuple-element.26), channel_id=1, source_target_pairs={{0,16},{4,12},{8,24},{12,4},{16,0},{20,28},{24,8},{28,20},{1,17},{... | collective-permute-start | bytes 768008 | tf_op jit(solution)/shard_map/ppermute | solution.py:304
  48.6 7.2 %collective-permute-start.7 = (bf16[2,128,128]{2,1,0:T(8,128)(2,1)S(1)}, bf16[2,128,128]{2,1,0:T(8,128)(2,1)S(1)}, u32[]{:S(2)}, u32[]{:S(2)}) collective-permute-start(bf16[2,128,128]{2,1,0:T(8,128)(2,1)S(1)} %get-tuple-element.21), channel_id=1, source_target_pairs={{0,1},{1,2},{2,3},{3,0},{4,5},{5,6},{6,7},{7,4},{8,9},{9,10},{10,1... | collective-permute-start | bytes 196616 | tf_op jit(solution)/shard_map/ppermute | solution.py:307
  50.8 7.8 %collective-permute-start.8 = (bf16[2,128,128]{2,1,0:T(8,128)(2,1)S(1)}, bf16[2,128,128]{2,1,0:T(8,128)(2,1)S(1)}, u32[]{:S(2)}, u32[]{:S(2)}) collective-permute-start(bf16[2,128,128]{2,1,0:T(8,128)(2,1)S(1)} %get-tuple-element.22), channel_id=1, source_target_pairs={{0,2},{1,3},{2,0},{3,1},{4,6},{5,7},{6,4},{7,5},{8,10},{9,11},{10,... | collective-permute-start | bytes 196616 | tf_op jit(solution)/shard_map/ppermute | solution.py:307
  53.4 6.0 %collective-permute-start.9 = (bf16[2,128,128]{2,1,0:T(8,128)(2,1)S(1)}, bf16[2,128,128]{2,1,0:T(8,128)(2,1)S(1)}, u32[]{:S(2)}, u32[]{:S(2)}) collective-permute-start(bf16[2,128,128]{2,1,0:T(8,128)(2,1)S(1)} %get-tuple-element.23), channel_id=1, source_target_pairs={{0,3},{1,0},{2,1},{3,2},{4,7},{5,4},{6,5},{7,6},{8,11},{9,8},{10,9... | collective-permute-start | bytes 196616 | tf_op jit(solution)/shard_map/ppermute | solution.py:307
  54.8 8.9 %collective-permute-start.4 = (bf16[2,128,128]{2,1,0:T(8,128)(2,1)S(1)}, bf16[2,128,128]{2,1,0:T(8,128)(2,1)S(1)}, u32[]{:S(2)}, u32[]{:S(2)}) collective-permute-start(bf16[2,128,128]{2,1,0:T(8,128)(2,1)S(1)} %get-tuple-element.17), channel_id=1, source_target_pairs={{0,1},{1,2},{2,3},{3,0},{4,5},{5,6},{6,7},{7,4},{8,9},{9,10},{10,1... | collective-permute-start | bytes 196616 | tf_op jit(solution)/shard_map/ppermute | solution.py:307
  55.5 8.7 %collective-permute-start.5 = (bf16[2,128,128]{2,1,0:T(8,128)(2,1)S(1)}, bf16[2,128,128]{2,1,0:T(8,128)(2,1)S(1)}, u32[]{:S(2)}, u32[]{:S(2)}) collective-permute-start(bf16[2,128,128]{2,1,0:T(8,128)(2,1)S(1)} %get-tuple-element.18), channel_id=1, source_target_pairs={{0,2},{1,3},{2,0},{3,1},{4,6},{5,7},{6,4},{7,5},{8,10},{9,11},{10,... | collective-permute-start | bytes 196616 | tf_op jit(solution)/shard_map/ppermute | solution.py:307
  55.8 8.4 %collective-permute-start.6 = (bf16[2,128,128]{2,1,0:T(8,128)(2,1)S(1)}, bf16[2,128,128]{2,1,0:T(8,128)(2,1)S(1)}, u32[]{:S(2)}, u32[]{:S(2)}) collective-permute-start(bf16[2,128,128]{2,1,0:T(8,128)(2,1)S(1)} %get-tuple-element.19), channel_id=1, source_target_pairs={{0,3},{1,0},{2,1},{3,2},{4,7},{5,4},{6,5},{7,6},{8,11},{9,8},{10,9... | collective-permute-start | bytes 196616 | tf_op jit(solution)/shard_map/ppermute | solution.py:307
  59.4 9.9 %collective-permute-start.14 = (bf16[2,128,128]{2,1,0:T(8,128)(2,1)S(1)}, bf16[2,128,128]{2,1,0:T(8,128)(2,1)S(1)}, u32[]{:S(2)}, u32[]{:S(2)}) collective-permute-start(bf16[2,128,128]{2,1,0:T(8,128)(2,1)S(1)} %add_convert_fusion), channel_id=1, source_target_pairs={{0,1},{1,2},{2,3},{3,0},{4,5},{5,6},{6,7},{7,4},{8,9},{9,10},{10,1... | collective-permute-start | bytes 196616 | tf_op jit(solution)/shard_map/ppermute | solution.py:307
  60.5 11.0 %collective-permute-start.15 = (bf16[2,128,128]{2,1,0:T(8,128)(2,1)S(1)}, bf16[2,128,128]{2,1,0:T(8,128)(2,1)S(1)}, u32[]{:S(2)}, u32[]{:S(2)}) collective-permute-start(bf16[2,128,128]{2,1,0:T(8,128)(2,1)S(1)} %add_convert_fusion), channel_id=1, source_target_pairs={{0,2},{1,3},{2,0},{3,1},{4,6},{5,7},{6,4},{7,5},{8,10},{9,11},{10,... | collective-permute-start | bytes 196616 | tf_op jit(solution)/shard_map/ppermute | solution.py:307
  63.7 7.8 %collective-permute-start.16 = (bf16[2,128,128]{2,1,0:T(8,128)(2,1)S(1)}, bf16[2,128,128]{2,1,0:T(8,128)(2,1)S(1)}, u32[]{:S(2)}, u32[]{:S(2)}) collective-permute-start(bf16[2,128,128]{2,1,0:T(8,128)(2,1)S(1)} %add_convert_fusion), channel_id=1, source_target_pairs={{0,3},{1,0},{2,1},{3,2},{4,7},{5,4},{6,5},{7,6},{8,11},{9,8},{10,9... | collective-permute-start | bytes 196616 | tf_op jit(solution)/shard_map/ppermute | solution.py:307
  64.3 9.1 %collective-permute-start.10 = (bf16[2,128,128]{2,1,0:T(8,128)(2,1)S(1)}, bf16[2,128,128]{2,1,0:T(8,128)(2,1)S(1)}, u32[]{:S(2)}, u32[]{:S(2)}) collective-permute-start(bf16[2,128,128]{2,1,0:T(8,128)(2,1)S(1)} %add_convert_fusion.1), channel_id=1, source_target_pairs={{0,1},{1,2},{2,3},{3,0},{4,5},{5,6},{6,7},{7,4},{8,9},{9,10},{10,1... | collective-permute-start | bytes 196616 | tf_op jit(solution)/shard_map/ppermute | solution.py:307
  69.1 5.7 %collective-permute-start.11 = (bf16[2,128,128]{2,1,0:T(8,128)(2,1)S(1)}, bf16[2,128,128]{2,1,0:T(8,128)(2,1)S(1)}, u32[]{:S(2)}, u32[]{:S(2)}) collective-permute-start(bf16[2,128,128]{2,1,0:T(8,128)(2,1)S(1)} %add_convert_fusion.1), channel_id=1, source_target_pairs={{0,2},{1,3},{2,0},{3,1},{4,6},{5,7},{6,4},{7,5},{8,10},{9,11},{10,... | collective-permute-start | bytes 196616 | tf_op jit(solution)/shard_map/ppermute | solution.py:307
  69.3 5.5 %collective-permute-start.12 = (bf16[2,128,128]{2,1,0:T(8,128)(2,1)S(1)}, bf16[2,128,128]{2,1,0:T(8,128)(2,1)S(1)}, u32[]{:S(2)}, u32[]{:S(2)}) collective-permute-start(bf16[2,128,128]{2,1,0:T(8,128)(2,1)S(1)} %add_convert_fusion.1), channel_id=1, source_target_pairs={{0,3},{1,0},{2,1},{3,2},{4,7},{5,4},{6,5},{7,6},{8,11},{9,8},{10,9... | collective-permute-start | bytes 196616 | tf_op jit(solution)/shard_map/ppermute | solution.py:307
  71.6 4.6 %collective-permute-start.17 = (bf16[4,2,128,128]{3,2,1,0:T(8,128)(2,1)S(1)}, bf16[4,2,128,128]{3,2,1,0:T(8,128)(2,1)S(1)}, u32[]{:S(2)}, u32[]{:S(2)}) collective-permute-start(bf16[4,2,128,128]{3,2,1,0:T(8,128)(2,1)S(1)} %pad_maximum_fusion.1.refs_1_), channel_id=1, source_target_pairs={{0,4},{4,0},{8,12},{12,8},{16,20},{20,16},{24,28},{28,24},{1,5},{5... | collective-permute-start | bytes 786440 | tf_op jit(solution)/shard_map/ppermute | solution.py:298
  71.6 8.5 %collective-permute-start.25 = (bf16[4,2,128,128]{3,2,1,0:T(8,128)(2,1)S(1)}, bf16[4,2,128,128]{3,2,1,0:T(8,128)(2,1)S(1)}, u32[]{:S(2)}, u32[]{:S(2)}) collective-permute-start(bf16[4,2,128,128]{3,2,1,0:T(8,128)(2,1)S(1)} %pad_maximum_fusion.1.refs_1_), channel_id=1, source_target_pairs={{0,16},{4,12},{8,24},{12,4},{16,0},{20,28},{24,8},{28,20},{1,17},{... | collective-permute-start | bytes 786440 | tf_op jit(solution)/shard_map/ppermute | solution.py:304
  73.3 8.1 %collective-permute-start.20 = (bf16[4,2,128,128]{3,2,1,0:T(8,128)(2,1)S(1)}, bf16[4,2,128,128]{3,2,1,0:T(8,128)(2,1)S(1)}, u32[]{:S(2)}, u32[]{:S(2)}) collective-permute-start(bf16[4,2,128,128]{3,2,1,0:T(8,128)(2,1)S(1)} %pad_maximum_fusion.1.refs_1_), channel_id=1, source_target_pairs={{0,8},{4,20},{8,0},{12,28},{16,24},{20,4},{24,16},{28,12},{1,9},{5... | collective-permute-start | bytes 786440 | tf_op jit(solution)/shard_map/ppermute | solution.py:304
  74.9 12.2 %collective-permute-start.18 = (bf16[4,2,128,128]{3,2,1,0:T(8,128)(2,1)S(1)}, bf16[4,2,128,128]{3,2,1,0:T(8,128)(2,1)S(1)}, u32[]{:S(2)}, u32[]{:S(2)}) collective-permute-start(bf16[4,2,128,128]{3,2,1,0:T(8,128)(2,1)S(1)} %pad_maximum_fusion.refs_0_), channel_id=1, source_target_pairs={{0,8},{4,20},{8,0},{12,28},{16,24},{20,4},{24,16},{28,12},{1,9},{5... | collective-permute-start | bytes 786440 | tf_op jit(solution)/shard_map/ppermute | solution.py:304
  76.1 12.4 %collective-permute-start.13 = (bf16[4,2,128,128]{3,2,1,0:T(8,128)(2,1)S(1)}, bf16[4,2,128,128]{3,2,1,0:T(8,128)(2,1)S(1)}, u32[]{:S(2)}, u32[]{:S(2)}) collective-permute-start(bf16[4,2,128,128]{3,2,1,0:T(8,128)(2,1)S(1)} %pad_maximum_fusion.refs_0_), channel_id=1, source_target_pairs={{0,4},{4,0},{8,12},{12,8},{16,20},{20,16},{24,28},{28,24},{1,5},{5... | collective-permute-start | bytes 786440 | tf_op jit(solution)/shard_map/ppermute | solution.py:298
  76.2 12.4 %collective-permute-start.24 = (bf16[4,2,128,128]{3,2,1,0:T(8,128)(2,1)S(1)}, bf16[4,2,128,128]{3,2,1,0:T(8,128)(2,1)S(1)}, u32[]{:S(2)}, u32[]{:S(2)}) collective-permute-start(bf16[4,2,128,128]{3,2,1,0:T(8,128)(2,1)S(1)} %pad_maximum_fusion.refs_0_), channel_id=1, source_target_pairs={{0,16},{4,12},{8,24},{12,4},{16,0},{20,28},{24,8},{28,20},{1,17},{... | collective-permute-start | bytes 786440 | tf_op jit(solution)/shard_map/ppermute | solution.py:304
  80.2 8.9 %collective-permute-start.29 = (bf16[4,2,128,128]{3,2,1,0:T(8,128)(2,1)S(1)}, bf16[4,2,128,128]{3,2,1,0:T(8,128)(2,1)S(1)}, u32[]{:S(2)}, u32[]{:S(2)}) collective-permute-start(bf16[4,2,128,128]{3,2,1,0:T(8,128)(2,1)S(1)} %collective-permute-done.25.refs_1_), channel_id=1, source_target_pairs={{0,4},{4,0},{8,12},{12,8},{16,20},{20,16},{24,28},{28,24},{1,5},{5... | collective-permute-start | bytes 786440 | tf_op jit(solution)/shard_map/ppermute | solution.py:298
  81.4 7.9 %collective-permute-start.21 = (bf16[4,2,128,128]{3,2,1,0:T(8,128)(2,1)S(1)}, bf16[4,2,128,128]{3,2,1,0:T(8,128)(2,1)S(1)}, u32[]{:S(2)}, u32[]{:S(2)}) collective-permute-start(bf16[4,2,128,128]{3,2,1,0:T(8,128)(2,1)S(1)} %collective-permute-done.20.refs_1_), channel_id=1, source_target_pairs={{0,16},{4,12},{8,24},{12,4},{16,0},{20,28},{24,8},{28,20},{1,17},{... | collective-permute-start | bytes 786440 | tf_op jit(solution)/shard_map/ppermute | solution.py:304
  87.0 6.4 %collective-permute-start.19 = (bf16[4,2,128,128]{3,2,1,0:T(8,128)(2,1)S(1)}, bf16[4,2,128,128]{3,2,1,0:T(8,128)(2,1)S(1)}, u32[]{:S(2)}, u32[]{:S(2)}) collective-permute-start(bf16[4,2,128,128]{3,2,1,0:T(8,128)(2,1)S(1)} %collective-permute-done.18.refs_0_), channel_id=1, source_target_pairs={{0,16},{4,12},{8,24},{12,4},{16,0},{20,28},{24,8},{28,20},{1,17},{... | collective-permute-start | bytes 786440 | tf_op jit(solution)/shard_map/ppermute | solution.py:304
  88.5 10.5 %collective-permute-start.27 = (bf16[4,2,128,128]{3,2,1,0:T(8,128)(2,1)S(1)}, bf16[4,2,128,128]{3,2,1,0:T(8,128)(2,1)S(1)}, u32[]{:S(2)}, u32[]{:S(2)}) collective-permute-start(bf16[4,2,128,128]{3,2,1,0:T(8,128)(2,1)S(1)} %collective-permute-done.20.refs_1_), channel_id=1, source_target_pairs={{0,4},{4,0},{8,12},{12,8},{16,20},{20,16},{24,28},{28,24},{1,5},{5... | collective-permute-start | bytes 786440 | tf_op jit(solution)/shard_map/ppermute | solution.py:298
  88.6 10.5 %collective-permute-start.26 = (bf16[4,2,128,128]{3,2,1,0:T(8,128)(2,1)S(1)}, bf16[4,2,128,128]{3,2,1,0:T(8,128)(2,1)S(1)}, u32[]{:S(2)}, u32[]{:S(2)}) collective-permute-start(bf16[4,2,128,128]{3,2,1,0:T(8,128)(2,1)S(1)} %collective-permute-done.18.refs_0_), channel_id=1, source_target_pairs={{0,4},{4,0},{8,12},{12,8},{16,20},{20,16},{24,28},{28,24},{1,5},{5... | collective-permute-start | bytes 786440 | tf_op jit(solution)/shard_map/ppermute | solution.py:298
  89.1 7.6 %collective-permute-start.28 = (bf16[4,2,128,128]{3,2,1,0:T(8,128)(2,1)S(1)}, bf16[4,2,128,128]{3,2,1,0:T(8,128)(2,1)S(1)}, u32[]{:S(2)}, u32[]{:S(2)}) collective-permute-start(bf16[4,2,128,128]{3,2,1,0:T(8,128)(2,1)S(1)} %collective-permute-done.24.refs_0_), channel_id=1, source_target_pairs={{0,4},{4,0},{8,12},{12,8},{16,20},{20,16},{24,28},{28,24},{1,5},{5... | collective-permute-start | bytes 786440 | tf_op jit(solution)/shard_map/ppermute | solution.py:298
  89.3 12.1 %collective-permute-start.23 = (bf16[4,2,128,128]{3,2,1,0:T(8,128)(2,1)S(1)}, bf16[4,2,128,128]{3,2,1,0:T(8,128)(2,1)S(1)}, u32[]{:S(2)}, u32[]{:S(2)}) collective-permute-start(bf16[4,2,128,128]{3,2,1,0:T(8,128)(2,1)S(1)} %collective-permute-done.21.refs_1_), channel_id=1, source_target_pairs={{0,4},{4,0},{8,12},{12,8},{16,20},{20,16},{24,28},{28,24},{1,5},{5... | collective-permute-start | bytes 786440 | tf_op jit(solution)/shard_map/ppermute | solution.py:298
  93.4 8.1 %collective-permute-start.22 = (bf16[4,2,128,128]{3,2,1,0:T(8,128)(2,1)S(1)}, bf16[4,2,128,128]{3,2,1,0:T(8,128)(2,1)S(1)}, u32[]{:S(2)}, u32[]{:S(2)}) collective-permute-start(bf16[4,2,128,128]{3,2,1,0:T(8,128)(2,1)S(1)} %collective-permute-done.19.refs_0_), channel_id=1, source_target_pairs={{0,4},{4,0},{8,12},{12,8},{16,20},{20,16},{24,28},{28,24},{1,5},{5... | collective-permute-start | bytes 786440 | tf_op jit(solution)/shard_map/ppermute | solution.py:298
  (3 other events, 17.5 us)

commit v4 on v3

--- a/solution.py
+++ b/solution.py
@@ -103,7 +103,7 @@
 def unit_forces(coords, wavevec, mode_shapes):
     modes, nodes = mode_shapes.shape
     waves = wavevec.shape[1]
-    block, piece, sub = 4096, 1024, 256
+    block, piece, sub = 4096, 1024, 1024
     out = jax.ShapeDtypeStruct((modes, waves), jnp.float32)
     return pl.pallas_call(
         functools.partial(forces_kernel, piece, sub),
@@ -122,7 +122,7 @@
             pltpu.VMEM((piece, 2 * waves), jnp.bfloat16),
             pltpu.VMEM((piece, 2 * waves), jnp.bfloat16),
         ],
-        compiler_params=BIG,
+        compiler_params=pltpu.CompilerParams(vmem_limit_bytes=60 << 20),
         cost_estimate=pl.CostEstimate(
             flops=12 * modes * nodes * waves, bytes_accessed=2 * modes * nodes, transcendentals=0
         ),
@@ -240,14 +240,15 @@
 def spectra_kernel(blocks, place_ref, left_ref, *refs):
     data, out_ref = refs[: 2 * CHUNKS], refs[-1]
     depth, rows = data[0].shape[-2:]
-    scale = 1.0 / (CHUNKS * depth)
-    for z in range(blocks):
-        at = lax.rem(lax.axis_index("mode") - z + blocks, blocks)
-        total = 0.0
-        for n, ref in enumerate(data):
-            total = total + jnp.dot(left_ref[n], ref[at], preferred_element_type=jnp.float32)
-        out_ref[0, :, z * rows : (z + 1) * rows] = total[:rows] * scale
-        out_ref[1, :, z * rows : (z + 1) * rows] = total[rows:] * scale
+    mode = lax.axis_index("mode")
+    order = [lax.rem(mode - z + blocks, blocks) for z in range(blocks)]
+    right = jnp.concatenate(
+        [jnp.concatenate([ref[at] for at in order], axis=1) for ref in data], axis=0
+    )
+    left = jnp.concatenate([left_ref[n] for n in range(len(data))], axis=1)
+    total = jnp.dot(left, right, preferred_element_type=jnp.float32) * (1.0 / (CHUNKS * depth))
+    out_ref[0] = total[:rows]
+    out_ref[1] = total[rows:]
 
 
 def cross_spectra(place, blocks, groups, spectra, left, ours, theirs):
@@ -278,7 +279,7 @@
         input_output_aliases={2 + 2 * CHUNKS: 0} if started else {},
         compiler_params=BIG,
         cost_estimate=pl.CostEstimate(
-            flops=8 * CHUNKS * depth * rows * rows * blocks,
+            flops=160 * CHUNKS * depth * rows * rows * blocks,
             bytes_accessed=32 * rows * rows * blocks,
             transcendentals=0,
         ),
@@ -314,24 +315,20 @@
     last = across(kept.astype(jnp.bfloat16), bits - 1)
     totals, sends = partial_fields(blocks, kept, last, wave_amp, modal_frf, radiation, mate)
 
-    fields, gathered, mates = [], [], []
+    fields = []
     for total, sent in zip(totals, sends):
         for k, block in enumerate(sent):
             total = total + along(block, k + 1).astype(jnp.float32)
         fields.append(total.astype(jnp.bfloat16))
-    for field in fields:
-        parts = [jnp.stack([field] + [along(field, k) for k in range(1, blocks)])]
-        for step in range(bits):
-            parts = parts + [across(x, step) for x in parts]
-        gathered.append(parts)
-        mates.append([to_mate(x) for x in parts])
-    left, field_pressure = own_rows(
-        [field[0] for field in fields] + [parts[0][0, 1] for parts in mates]
-    )
-    spectra = None
-    for p in range(groups):
+    gathered = [
+        [jnp.stack([field] + [along(field, k) for k in range(1, blocks)])] for field in fields
+    ]
+    mates = [[to_mate(x) for x in parts] for parts in gathered]
+    left, field_pressure = own_rows([x[0] for x in fields] + [x[0][0, 1] for x in mates])
+
+    def add_part(spectra, p):
         at = jnp.bitwise_xor(group, jnp.where(core == 0, p, reverse(p)))
-        spectra = cross_spectra(
+        return cross_spectra(
             jnp.stack([at, core]).astype(jnp.int32),
             blocks,
             groups,
@@ -340,6 +337,20 @@
             [parts[p] for parts in gathered],
             [parts[reverse(p)] for parts in mates],
         )
+
+    spectra = add_part(None, 0)
+    for step in range(bits):
+        for parts in gathered:
+            parts += [across(x, step) for x in parts]
+    for parts, arrived in zip(mates, gathered):
+        parts += [to_mate(x) for x in arrived[1:-1]]
+    for p in range(1, groups - 1):
+        spectra = add_part(spectra, p)
+    spectra, lasts = lax.optimization_barrier((spectra, [parts[-1] for parts in gathered]))
+    for c in range(CHUNKS):
+        gathered[c][-1] = lasts[c]
+        mates[c].append(to_mate(lasts[c]))
+    spectra = add_part(spectra, groups - 1)
     return (spectra, field_pressure)
 
 

time: 104 us -> 97.3 us (0.936)
  waiting for transfers between devices: 21.5 us -> 17.9 us
  Pallas kernels: 40.9 us -> 38.4 us
  local copies, waits for them, and re-layouts: 3.25 us -> 1.57 us
  other arithmetic: 0.5 us -> 1.67 us
    ppermute x8, waiting for transfers between devices: 18.8 us -> 12.4 us  [across(): return lax.ppermute(x, 'node', [(i, flip(i)) for i in range(nodes)])]
    unnamed x11 -> x7, local copies, waits for them, and re-layouts: 1.85 us -> 0.17 us
    pallas_call x1, Pallas kernels: 29 us -> 27.4 us  [unit_forces(): pl.pallas_call(functools.partial(forces_kernel, piece, sub), grid=(nodes...]
    ppermute x10, waiting for transfers between devices: 1.46 us -> 2.99 us  [to_mate(): return lax.ppermute(x, 'node', [(i, i ^ 1) for i in range(nodes)])]
    ppermute x12, waiting for transfers between devices: 1.26 us -> 2.46 us  [along(): lax.ppermute(x, 'mode', [(i, (i + k) % blocks) for i in range(blocks)])]
    convert_element_type x1, other arithmetic: 0.07 us -> 1.14 us  [body(): kept = kept + across(kept.astype(jnp.bfloat16), step).astype(jnp.float32)]
  transfers between devices with their start and end apart: 30 -> 30, of which waited for: 10 -> 10; matrix products, arithmetic and copies ran while one was open for 2% -> 3% of each run, Pallas kernels for 8% -> 8%
where the time goes in v4:
time: 97.3 us; the launch traced here: 97.1 us
  Pallas kernels  38.4 us (39%)
  starting transfers between devices  36.8 us (38%)
  waiting for transfers between devices  17.9 us (18%)
  other arithmetic  1.67 us (2%)
  local copies, waits for them, and re-layouts  1.57 us (2%)
    pallas_call x1, Pallas kernels, unit_forces(): pl.pallas_call(functools.partial(forces_kernel, piece, sub), grid=(nodes...  27.4 us
    ppermute x12, starting transfers between devices, along(): lax.ppermute(x, 'mode', [(i, (i + k) % blocks) for i in range(blocks)])  21.5 us
    ppermute x8, starting transfers between devices, across(): return lax.ppermute(x, 'node', [(i, flip(i)) for i in range(nodes)])  13.3 us
    ppermute x8, waiting for transfers between devices, across(): return lax.ppermute(x, 'node', [(i, flip(i)) for i in range(nodes)])  12.4 us
    pallas_call x4, Pallas kernels, cross_spectra(): pl.pallas_call(functools.partial(spectra_kernel, blocks), grid_spec=pltpu...  8.63 us
    ppermute x10, waiting for transfers between devices, to_mate(): return lax.ppermute(x, 'node', [(i, i ^ 1) for i in range(nodes)])  2.99 us
    ppermute x12, waiting for transfers between devices, along(): lax.ppermute(x, 'mode', [(i, (i + k) % blocks) for i in range(blocks)])  2.46 us
    ppermute x10, starting transfers between devices, to_mate(): return lax.ppermute(x, 'node', [(i, i ^ 1) for i in range(nodes)])  2.04 us
  transfers between devices with their start and end apart: 30, of which 10 were waited for; matrix products, arithmetic and copies ran while one was open for 3% of the time, Pallas kernels for 8%

profile of v4, /device:TPU:0, one launch (start us, length us, event | category | flops | bytes accessed | tf_op | source)
XLA Modules:
  0.0 97.1 jit_solution(15640125971588582165)
XLA Ops:
  0.6 27.4 %shard_map.77 = (f32[500,256]{1,0:T(8,128)}, f32[500,256]{1,0:T(8,128)}) custom-call(f32[3,24576]{1,0:T(4,128)} %coords_ref.1, f32[3,256]{1,0:T(4,128)} %wave_ref.1, bf16[500,24576]{1,0:T(8,128)(2,1)} %shapes_ref.1), custom_call_target="tpu_custom_call" | custom-call | flops 37748736000 | bytes 24576000 | tf_op jit(solution)/shard_map/pallas_call | solution.py:108
  28.6 1.7 %collective-permute-done = f32[500,256]{1,0:T(8,128)S(1)} collective-permute-done((f32[500,256]{1,0:T(8,128)}, f32[500,256]{1,0:T(8,128)S(1)}, u32[]{:S(2)}, u32[]{:S(2)}) %collective-permute-start) | collective-permute-done | bytes 512032 | tf_op jit(solution)/shard_map/ppermute | solution.py:299
  30.3 1.1 %fusion.1 = (bf16[500,256]{1,0:T(8,128)(2,1)S(1)}, f32[500,256]{1,0:T(8,128)S(1)}) fusion(f32[500,256]{1,0:T(8,128)} %get-tuple-element.17, f32[500,256]{1,0:T(8,128)S(1)} %collective-permute-done), kind=kLoop, calls=%fused_computation.14 | loop fusion | flops 256000 | bytes 1792000 | tf_op jit(solution)/shard_map/convert_element_type | solution.py:314
  31.4 2.9 %collective-permute-start.1 = (bf16[500,256]{1,0:T(8,128)(2,1)S(1)}, bf16[500,256]{1,0:T(8,128)(2,1)S(1)}, u32[]{:S(2)}, u32[]{:S(2)}) collective-permute-start(bf16[500,256]{1,0:T(8,128)(2,1)S(1)} %get-tuple-element.34), channel_id=1, source_target_pairs={{0,8},{4,20},{8,0},{12,28},{16,24},{20,4},{24,16},{28,12},{1,9},{5... | collective-permute-start | bytes 768008 | tf_op jit(solution)/shard_map/ppermute | solution.py:305
  34.3 4.3 %collective-permute-done.1 = bf16[500,256]{1,0:T(8,128)(2,1)S(1)} collective-permute-done((bf16[500,256]{1,0:T(8,128)(2,1)S(1)}, bf16[500,256]{1,0:T(8,128)(2,1)S(1)}, u32[]{:S(2)}, u32[]{:S(2)}) %collective-permute-start.1) | collective-permute-done | bytes 256032 | tf_op jit(solution)/shard_map/ppermute | solution.py:305
  38.7 2.1 %collective-permute-start.2 = (bf16[500,256]{1,0:T(8,128)(2,1)S(1)}, bf16[500,256]{1,0:T(8,128)(2,1)S(1)}, u32[]{:S(2)}, u32[]{:S(2)}) collective-permute-start(bf16[500,256]{1,0:T(8,128)(2,1)S(1)} %get-tuple-element.32), channel_id=1, source_target_pairs={{0,16},{4,12},{8,24},{12,4},{16,0},{20,28},{24,8},{28,20},{1,17},{... | collective-permute-start | bytes 768008 | tf_op jit(solution)/shard_map/ppermute | solution.py:305
  41.2 1.4 %copy.14.mate_ref = bf16[2,500,512]{2,1,0:T(8,128)(2,1)S(1)} copy(bf16[2,500,512]{2,0,1:T(2,128)(2,1)} %collective-permute-done.3) | data formatting | bytes 2048000 | tf_op jit(solution)/shard_map/ppermute | solution.py:299
  42.6 2.6 %collective-permute-done.2.last_ref = bf16[500,256]{1,0:T(8,128)(2,1)S(1)} collective-permute-done((bf16[500,256]{1,0:T(8,128)(2,1)S(1)}, bf16[500,256]{1,0:T(8,128)(2,1)S(1)}, u32[]{:S(2)}, u32[]{:S(2)}) %collective-permute-start.2) | collective-permute-done | bytes 256032 | tf_op jit(solution)/shard_map/ppermute | solution.py:305
  45.1 1.5 %shard_map.78 = (f32[2,128,128]{2,1,0:T(8,128)S(1)}, f32[2,128,128]{2,1,0:T(8,128)S(1)}, bf16[2,128,128]{2,1,0:T(8,128)(2,1)S(1)}, bf16[2,128,128]{2,1,0:T(8,128...) custom-call(f32[500,256]{1,0:T(8,128)S(1)} %get-tuple-element.33.kep, ...), custom_call_target="tpu_custom_call" | custom-call | flops 524288000 | bytes 2048000 | tf_op jit(solution)/shard_map/pallas_call | solution.py:190
  46.6 2.1 %collective-permute-start.7 = (bf16[2,128,128]{2,1,0:T(8,128)(2,1)S(1)}, bf16[2,128,128]{2,1,0:T(8,128)(2,1)S(1)}, u32[]{:S(2)}, u32[]{:S(2)}) collective-permute-start(bf16[2,128,128]{2,1,0:T(8,128)(2,1)S(1)} %get-tuple-element.24), channel_id=1, source_target_pairs={{0,1},{1,2},{2,3},{3,0},{4,5},{5,6},{6,7},{7,4},{8,9},{9,10},{10,1... | collective-permute-start | bytes 196616 | tf_op jit(solution)/shard_map/ppermute | solution.py:308
  48.8 2.6 %collective-permute-start.8 = (bf16[2,128,128]{2,1,0:T(8,128)(2,1)S(1)}, bf16[2,128,128]{2,1,0:T(8,128)(2,1)S(1)}, u32[]{:S(2)}, u32[]{:S(2)}) collective-permute-start(bf16[2,128,128]{2,1,0:T(8,128)(2,1)S(1)} %get-tuple-element.25), channel_id=1, source_target_pairs={{0,2},{1,3},{2,0},{3,1},{4,6},{5,7},{6,4},{7,5},{8,10},{9,11},{10,... | collective-permute-start | bytes 196616 | tf_op jit(solution)/shard_map/ppermute | solution.py:308
  51.4 1.3 %collective-permute-start.9 = (bf16[2,128,128]{2,1,0:T(8,128)(2,1)S(1)}, bf16[2,128,128]{2,1,0:T(8,128)(2,1)S(1)}, u32[]{:S(2)}, u32[]{:S(2)}) collective-permute-start(bf16[2,128,128]{2,1,0:T(8,128)(2,1)S(1)} %get-tuple-element.26), channel_id=1, source_target_pairs={{0,3},{1,0},{2,1},{3,2},{4,7},{5,4},{6,5},{7,6},{8,11},{9,8},{10,9... | collective-permute-start | bytes 196616 | tf_op jit(solution)/shard_map/ppermute | solution.py:308
  52.8 0.7 collective-permute-start.4
  53.8 2.8 %collective-permute-start.6 = (bf16[2,128,128]{2,1,0:T(8,128)(2,1)S(1)}, bf16[2,128,128]{2,1,0:T(8,128)(2,1)S(1)}, u32[]{:S(2)}, u32[]{:S(2)}) collective-permute-start(bf16[2,128,128]{2,1,0:T(8,128)(2,1)S(1)} %get-tuple-element.22), channel_id=1, source_target_pairs={{0,3},{1,0},{2,1},{3,2},{4,7},{5,4},{6,5},{7,6},{8,11},{9,8},{10,9... | collective-permute-start | bytes 196616 | tf_op jit(solution)/shard_map/ppermute | solution.py:308
  56.6 0.7 collective-permute-done.9
  57.4 1.1 %collective-permute-start.14 = (bf16[2,128,128]{2,1,0:T(8,128)(2,1)S(1)}, bf16[2,128,128]{2,1,0:T(8,128)(2,1)S(1)}, u32[]{:S(2)}, u32[]{:S(2)}) collective-permute-start(bf16[2,128,128]{2,1,0:T(8,128)(2,1)S(1)} %add_convert_fusion), channel_id=1, source_target_pairs={{0,1},{1,2},{2,3},{3,0},{4,5},{5,6},{6,7},{7,4},{8,9},{9,10},{10,1... | collective-permute-start | bytes 196616 | tf_op jit(solution)/shard_map/ppermute | solution.py:308
  58.5 3.2 %collective-permute-start.15 = (bf16[2,128,128]{2,1,0:T(8,128)(2,1)S(1)}, bf16[2,128,128]{2,1,0:T(8,128)(2,1)S(1)}, u32[]{:S(2)}, u32[]{:S(2)}) collective-permute-start(bf16[2,128,128]{2,1,0:T(8,128)(2,1)S(1)} %add_convert_fusion), channel_id=1, source_target_pairs={{0,2},{1,3},{2,0},{3,1},{4,6},{5,7},{6,4},{7,5},{8,10},{9,11},{10,... | collective-permute-start | bytes 196616 | tf_op jit(solution)/shard_map/ppermute | solution.py:308
  62.2 4.8 %collective-permute-start.10 = (bf16[2,128,128]{2,1,0:T(8,128)(2,1)S(1)}, bf16[2,128,128]{2,1,0:T(8,128)(2,1)S(1)}, u32[]{:S(2)}, u32[]{:S(2)}) collective-permute-start(bf16[2,128,128]{2,1,0:T(8,128)(2,1)S(1)} %add_convert_fusion.1), channel_id=1, source_target_pairs={{0,1},{1,2},{2,3},{3,0},{4,5},{5,6},{6,7},{7,4},{8,9},{9,10},{10,1... | collective-permute-start | bytes 196616 | tf_op jit(solution)/shard_map/ppermute | solution.py:308
  67.3 2.2 %collective-permute-start.12 = (bf16[2,128,128]{2,1,0:T(8,128)(2,1)S(1)}, bf16[2,128,128]{2,1,0:T(8,128)(2,1)S(1)}, u32[]{:S(2)}, u32[]{:S(2)}) collective-permute-start(bf16[2,128,128]{2,1,0:T(8,128)(2,1)S(1)} %add_convert_fusion.1), channel_id=1, source_target_pairs={{0,3},{1,0},{2,1},{3,2},{4,7},{5,4},{6,5},{7,6},{8,11},{9,8},{10,9... | collective-permute-start | bytes 196616 | tf_op jit(solution)/shard_map/ppermute | solution.py:308
  69.6 1.6 %collective-permute-start.19 = (bf16[4,2,128,128]{3,2,1,0:T(8,128)(2,1)S(1)}, bf16[4,2,128,128]{3,2,1,0:T(8,128)(2,1)S(1)}, u32[]{:S(2)}, u32[]{:S(2)}) collective-permute-start(bf16[4,2,128,128]{3,2,1,0:T(8,128)(2,1)S(1)} %pad_maximum_fusion.1.refs_1_), channel_id=1, source_target_pairs={{0,16},{4,12},{8,24},{12,4},{16,0},{20,28},{24,8},{28,20},{1,17},{... | collective-permute-start | bytes 786440 | tf_op jit(solution)/shard_map/ppermute | solution.py:305
  71.2 1.2 %collective-permute-done.11 = bf16[2,128,128]{2,1,0:T(8,128)(2,1)S(1)} collective-permute-done((bf16[2,128,128]{2,1,0:T(8,128)(2,1)S(1)}, bf16[2,128,128]{2,1,0:T(8,128)(2,1)S(1)}, u32[]{:S(2)}, u32[]{:S(2)}) %collective-permute-start.11) | collective-permute-done | bytes 65568 | tf_op jit(solution)/shard_map/ppermute | solution.py:308
  72.6 1.6 %collective-permute-start.18 = (bf16[4,2,128,128]{3,2,1,0:T(8,128)(2,1)S(1)}, bf16[4,2,128,128]{3,2,1,0:T(8,128)(2,1)S(1)}, u32[]{:S(2)}, u32[]{:S(2)}) collective-permute-start(bf16[4,2,128,128]{3,2,1,0:T(8,128)(2,1)S(1)} %pad_maximum_fusion.refs_0_), channel_id=1, source_target_pairs={{0,16},{4,12},{8,24},{12,4},{16,0},{20,28},{24,8},{28,20},{1,17},{... | collective-permute-start | bytes 786440 | tf_op jit(solution)/shard_map/ppermute | solution.py:305
  74.2 1.5 %collective-permute-start.22 = (bf16[4,2,128,128]{3,2,1,0:T(8,128)(2,1)S(1)}, bf16[4,2,128,128]{3,2,1,0:T(8,128)(2,1)S(1)}, u32[]{:S(2)}, u32[]{:S(2)}) collective-permute-start(bf16[4,2,128,128]{3,2,1,0:T(8,128)(2,1)S(1)} %pad_maximum_fusion.1.refs_1_), channel_id=1, source_target_pairs={{0,8},{4,20},{8,0},{12,28},{16,24},{20,4},{24,16},{28,12},{1,9},{5... | collective-permute-start | bytes 786440 | tf_op jit(solution)/shard_map/ppermute | solution.py:305
  76.2 5.0 %collective-permute-done.18.refs_0_ = bf16[4,2,128,128]{3,2,1,0:T(8,128)(2,1)S(1)} collective-permute-done((bf16[4,2,128,128]{3,2,1,0:T(8,128)(2,1)S(1)}, bf16[4,2,128,128]{3,2,1,0:T(8,128)(2,1)S(1)}, u32[]{:S(2)}, u32[]{:S(2)}) %collective-permute-start.18) | collective-permute-done | bytes 262176 | tf_op jit(solution)/shard_map/ppermute | solution.py:305
  81.2 0.9 shard_map.79
  82.6 1.5 %collective-permute-start.27 = (bf16[4,2,128,128]{3,2,1,0:T(8,128)(2,1)S(1)}, bf16[4,2,128,128]{3,2,1,0:T(8,128)(2,1)S(1)}, u32[]{:S(2)}, u32[]{:S(2)}) collective-permute-start(bf16[4,2,128,128]{3,2,1,0:T(8,128)(2,1)S(1)} %collective-permute-done.22.refs_1_), channel_id=1, source_target_pairs={{0,16},{4,12},{8,24},{12,4},{16,0},{20,28},{24,8},{28,20},{1,17},{... | collective-permute-start | bytes 786440 | tf_op jit(solution)/shard_map/ppermute | solution.py:305
  84.5 2.2 %shard_map.80.refs_4_ = f32[2,128,4096]{2,1,0:T(8,128)} custom-call(s32[2]{0:T(128)S(1)} %pad_add_fusion.3.place_ref, bf16[4,256,128]{2,1,0:T(8,128)(2,1)S(1)} %get-tuple-element.27.left_ref, bf16[4,2,128,128]{3,2,1,0:T(8,128)(2,1)S(1)} %pad_maximum_fusion.refs_0_, bf16[4,2,128,128]{3,2,1,0:T(8,128)(2,1)S(1)} %pad_maximum_fusion.1.refs_1_, ...), custom_call_target="tpu_custom_call" | custom-call | flops 2684354560 | bytes 2097152 | tf_op jit(solution)/shard_map/pallas_call | solution.py:265
  86.6 1.5 %collective-permute-start.26 = (bf16[4,2,128,128]{3,2,1,0:T(8,128)(2,1)S(1)}, bf16[4,2,128,128]{3,2,1,0:T(8,128)(2,1)S(1)}, u32[]{:S(2)}, u32[]{:S(2)}) collective-permute-start(bf16[4,2,128,128]{3,2,1,0:T(8,128)(2,1)S(1)} %collective-permute-done.20.refs_0_), channel_id=1, source_target_pairs={{0,16},{4,12},{8,24},{12,4},{16,0},{20,28},{24,8},{28,20},{1,17},{... | collective-permute-start | bytes 786440 | tf_op jit(solution)/shard_map/ppermute | solution.py:305
  88.1 2.2 %shard_map.81.refs_4_ = f32[2,128,4096]{2,1,0:T(8,128)} custom-call(s32[2]{0:T(128)S(1)} %pad_add_fusion.2.place_ref, bf16[4,256,128]{2,1,0:T(8,128)(2,1)S(1)} %get-tuple-element.27.left_ref, bf16[4,2,128,128]{3,2,1,0:T(8,128)(2,1)S(1)} %collective-permute-done.20.refs_0_, ...), custom_call_target="tpu_custom_call", output_to_operand_aliasing={{}: (6, {})} | custom-call | flops 2684354560 | bytes 2097152 | tf_op jit(solution)/shard_map/pallas_call | solution.py:265
  90.3 2.2 %shard_map.82.refs_4_ = f32[2,128,4096]{2,1,0:T(8,128)} custom-call(s32[2]{0:T(128)S(1)} %pad_add_fusion.1.place_ref, bf16[4,256,128]{2,1,0:T(8,128)(2,1)S(1)} %get-tuple-element.27.left_ref, bf16[4,2,128,128]{3,2,1,0:T(8,128)(2,1)S(1)} %collective-permute-done.18.refs_0_, ...), custom_call_target="tpu_custom_call", output_to_operand_aliasing={{}: (6, {})} | custom-call | flops 2684354560 | bytes 2097152 | tf_op jit(solution)/shard_map/pallas_call | solution.py:265
  93.6 0.9 collective-permute-done.28.refs_2_
  94.9 2.2 %shard_map.83 = f32[2,128,4096]{2,1,0:T(8,128)} custom-call(s32[2]{0:T(128)S(1)} %pad_add_fusion.place_ref, bf16[4,256,128]{2,1,0:T(8,128)(2,1)S(1)} %get-tuple-element.27.left_ref, bf16[4,2,128,128]{3,2,1,0:T(8,128)(2,1)S(1)} %collective-permute-done.26.refs_0_, ...), custom_call_target="tpu_custom_call", output_to_operand_aliasing={{}: (6, {})} | custom-call | flops 2684354560 | bytes 2097152 | tf_op jit(solution)/shard_map/pallas_call | solution.py:265
  (57 shorter events, 5.3 us)
Async XLA Ops:
  0.6 27.9 %copy-start.2 = (bf16[2,500,512]{2,0,1:T(2,128)(2,1)S(1)}, bf16[2,500,512]{2,0,1:T(2,128)(2,1)}, u32[]{:S(2)}) copy-start(bf16[2,500,512]{2,0,1:T(2,128)(2,1)} %param.11) | copy-start | bytes 3072004
  28.1 17.1 %copy-start.1 = (f32[2,256]{1,0:T(2,128)S(1)}, f32[2,256]{1,0:T(2,128)}, u32[]{:S(2)}) copy-start(f32[2,256]{1,0:T(2,128)} %amp_ref.1) | copy-start | bytes 6148
  28.1 2.2 %collective-permute-start = (f32[500,256]{1,0:T(8,128)}, f32[500,256]{1,0:T(8,128)S(1)}, u32[]{:S(2)}, u32[]{:S(2)}) collective-permute-start(f32[500,256]{1,0:T(8,128)} %get-tuple-element.18), channel_id=1, source_target_pairs={{0,4},{4,0},{8,12},{12,8},{16,20},{20,16},{24,28},{28,24},{1,5},{5... | collective-permute-start | bytes 1536008 | tf_op jit(solution)/shard_map/ppermute | solution.py:299
  28.5 12.7 %collective-permute-start.3 = (bf16[2,500,512]{2,0,1:T(2,128)(2,1)S(1)}, bf16[2,500,512]{2,0,1:T(2,128)(2,1)}, u32[]{:S(2)}, u32[]{:S(2)}) collective-permute-start(bf16[2,500,512]{2,0,1:T(2,128)(2,1)S(1)} %copy-done.2), channel_id=1, source_target_pairs={{0,4},{4,0},{8,12},{12,8},{16,20},{20,16},{24,28},{28,24},{1,5},{5... | collective-permute-start | bytes 3072008 | tf_op jit(solution)/shard_map/ppermute | solution.py:299
  31.4 7.2 %collective-permute-start.1 = (bf16[500,256]{1,0:T(8,128)(2,1)S(1)}, bf16[500,256]{1,0:T(8,128)(2,1)S(1)}, u32[]{:S(2)}, u32[]{:S(2)}) collective-permute-start(bf16[500,256]{1,0:T(8,128)(2,1)S(1)} %get-tuple-element.34), channel_id=1, source_target_pairs={{0,8},{4,20},{8,0},{12,28},{16,24},{20,4},{24,16},{28,12},{1,9},{5... | collective-permute-start | bytes 768008 | tf_op jit(solution)/shard_map/ppermute | solution.py:305
  38.7 6.4 %collective-permute-start.2 = (bf16[500,256]{1,0:T(8,128)(2,1)S(1)}, bf16[500,256]{1,0:T(8,128)(2,1)S(1)}, u32[]{:S(2)}, u32[]{:S(2)}) collective-permute-start(bf16[500,256]{1,0:T(8,128)(2,1)S(1)} %get-tuple-element.32), channel_id=1, source_target_pairs={{0,16},{4,12},{8,24},{12,4},{16,0},{20,28},{24,8},{28,20},{1,17},{... | collective-permute-start | bytes 768008 | tf_op jit(solution)/shard_map/ppermute | solution.py:305
  46.6 7.2 %collective-permute-start.7 = (bf16[2,128,128]{2,1,0:T(8,128)(2,1)S(1)}, bf16[2,128,128]{2,1,0:T(8,128)(2,1)S(1)}, u32[]{:S(2)}, u32[]{:S(2)}) collective-permute-start(bf16[2,128,128]{2,1,0:T(8,128)(2,1)S(1)} %get-tuple-element.24), channel_id=1, source_target_pairs={{0,1},{1,2},{2,3},{3,0},{4,5},{5,6},{6,7},{7,4},{8,9},{9,10},{10,1... | collective-permute-start | bytes 196616 | tf_op jit(solution)/shard_map/ppermute | solution.py:308
  48.8 7.9 %collective-permute-start.8 = (bf16[2,128,128]{2,1,0:T(8,128)(2,1)S(1)}, bf16[2,128,128]{2,1,0:T(8,128)(2,1)S(1)}, u32[]{:S(2)}, u32[]{:S(2)}) collective-permute-start(bf16[2,128,128]{2,1,0:T(8,128)(2,1)S(1)} %get-tuple-element.25), channel_id=1, source_target_pairs={{0,2},{1,3},{2,0},{3,1},{4,6},{5,7},{6,4},{7,5},{8,10},{9,11},{10,... | collective-permute-start | bytes 196616 | tf_op jit(solution)/shard_map/ppermute | solution.py:308
  51.4 6.0 %collective-permute-start.9 = (bf16[2,128,128]{2,1,0:T(8,128)(2,1)S(1)}, bf16[2,128,128]{2,1,0:T(8,128)(2,1)S(1)}, u32[]{:S(2)}, u32[]{:S(2)}) collective-permute-start(bf16[2,128,128]{2,1,0:T(8,128)(2,1)S(1)} %get-tuple-element.26), channel_id=1, source_target_pairs={{0,3},{1,0},{2,1},{3,2},{4,7},{5,4},{6,5},{7,6},{8,11},{9,8},{10,9... | collective-permute-start | bytes 196616 | tf_op jit(solution)/shard_map/ppermute | solution.py:308
  52.8 9.0 %collective-permute-start.4 = (bf16[2,128,128]{2,1,0:T(8,128)(2,1)S(1)}, bf16[2,128,128]{2,1,0:T(8,128)(2,1)S(1)}, u32[]{:S(2)}, u32[]{:S(2)}) collective-permute-start(bf16[2,128,128]{2,1,0:T(8,128)(2,1)S(1)} %get-tuple-element.20), channel_id=1, source_target_pairs={{0,1},{1,2},{2,3},{3,0},{4,5},{5,6},{6,7},{7,4},{8,9},{9,10},{10,1... | collective-permute-start | bytes 196616 | tf_op jit(solution)/shard_map/ppermute | solution.py:308
  53.5 8.7 %collective-permute-start.5 = (bf16[2,128,128]{2,1,0:T(8,128)(2,1)S(1)}, bf16[2,128,128]{2,1,0:T(8,128)(2,1)S(1)}, u32[]{:S(2)}, u32[]{:S(2)}) collective-permute-start(bf16[2,128,128]{2,1,0:T(8,128)(2,1)S(1)} %get-tuple-element.21), channel_id=1, source_target_pairs={{0,2},{1,3},{2,0},{3,1},{4,6},{5,7},{6,4},{7,5},{8,10},{9,11},{10,... | collective-permute-start | bytes 196616 | tf_op jit(solution)/shard_map/ppermute | solution.py:308
  53.8 8.4 %collective-permute-start.6 = (bf16[2,128,128]{2,1,0:T(8,128)(2,1)S(1)}, bf16[2,128,128]{2,1,0:T(8,128)(2,1)S(1)}, u32[]{:S(2)}, u32[]{:S(2)}) collective-permute-start(bf16[2,128,128]{2,1,0:T(8,128)(2,1)S(1)} %get-tuple-element.22), channel_id=1, source_target_pairs={{0,3},{1,0},{2,1},{3,2},{4,7},{5,4},{6,5},{7,6},{8,11},{9,8},{10,9... | collective-permute-start | bytes 196616 | tf_op jit(solution)/shard_map/ppermute | solution.py:308
  57.4 9.9 %collective-permute-start.14 = (bf16[2,128,128]{2,1,0:T(8,128)(2,1)S(1)}, bf16[2,128,128]{2,1,0:T(8,128)(2,1)S(1)}, u32[]{:S(2)}, u32[]{:S(2)}) collective-permute-start(bf16[2,128,128]{2,1,0:T(8,128)(2,1)S(1)} %add_convert_fusion), channel_id=1, source_target_pairs={{0,1},{1,2},{2,3},{3,0},{4,5},{5,6},{6,7},{7,4},{8,9},{9,10},{10,1... | collective-permute-start | bytes 196616 | tf_op jit(solution)/shard_map/ppermute | solution.py:308
  58.5 11.0 %collective-permute-start.15 = (bf16[2,128,128]{2,1,0:T(8,128)(2,1)S(1)}, bf16[2,128,128]{2,1,0:T(8,128)(2,1)S(1)}, u32[]{:S(2)}, u32[]{:S(2)}) collective-permute-start(bf16[2,128,128]{2,1,0:T(8,128)(2,1)S(1)} %add_convert_fusion), channel_id=1, source_target_pairs={{0,2},{1,3},{2,0},{3,1},{4,6},{5,7},{6,4},{7,5},{8,10},{9,11},{10,... | collective-permute-start | bytes 196616 | tf_op jit(solution)/shard_map/ppermute | solution.py:308
  61.7 7.8 %collective-permute-start.16 = (bf16[2,128,128]{2,1,0:T(8,128)(2,1)S(1)}, bf16[2,128,128]{2,1,0:T(8,128)(2,1)S(1)}, u32[]{:S(2)}, u32[]{:S(2)}) collective-permute-start(bf16[2,128,128]{2,1,0:T(8,128)(2,1)S(1)} %add_convert_fusion), channel_id=1, source_target_pairs={{0,3},{1,0},{2,1},{3,2},{4,7},{5,4},{6,5},{7,6},{8,11},{9,8},{10,9... | collective-permute-start | bytes 196616 | tf_op jit(solution)/shard_map/ppermute | solution.py:308
  62.2 9.0 %collective-permute-start.10 = (bf16[2,128,128]{2,1,0:T(8,128)(2,1)S(1)}, bf16[2,128,128]{2,1,0:T(8,128)(2,1)S(1)}, u32[]{:S(2)}, u32[]{:S(2)}) collective-permute-start(bf16[2,128,128]{2,1,0:T(8,128)(2,1)S(1)} %add_convert_fusion.1), channel_id=1, source_target_pairs={{0,1},{1,2},{2,3},{3,0},{4,5},{5,6},{6,7},{7,4},{8,9},{9,10},{10,1... | collective-permute-start | bytes 196616 | tf_op jit(solution)/shard_map/ppermute | solution.py:308
  67.1 5.4 %collective-permute-start.11 = (bf16[2,128,128]{2,1,0:T(8,128)(2,1)S(1)}, bf16[2,128,128]{2,1,0:T(8,128)(2,1)S(1)}, u32[]{:S(2)}, u32[]{:S(2)}) collective-permute-start(bf16[2,128,128]{2,1,0:T(8,128)(2,1)S(1)} %add_convert_fusion.1), channel_id=1, source_target_pairs={{0,2},{1,3},{2,0},{3,1},{4,6},{5,7},{6,4},{7,5},{8,10},{9,11},{10,... | collective-permute-start | bytes 196616 | tf_op jit(solution)/shard_map/ppermute | solution.py:308
  67.3 5.2 %collective-permute-start.12 = (bf16[2,128,128]{2,1,0:T(8,128)(2,1)S(1)}, bf16[2,128,128]{2,1,0:T(8,128)(2,1)S(1)}, u32[]{:S(2)}, u32[]{:S(2)}) collective-permute-start(bf16[2,128,128]{2,1,0:T(8,128)(2,1)S(1)} %add_convert_fusion.1), channel_id=1, source_target_pairs={{0,3},{1,0},{2,1},{3,2},{4,7},{5,4},{6,5},{7,6},{8,11},{9,8},{10,9... | collective-permute-start | bytes 196616 | tf_op jit(solution)/shard_map/ppermute | solution.py:308
  69.6 6.1 %collective-permute-start.17 = (bf16[4,2,128,128]{3,2,1,0:T(8,128)(2,1)S(1)}, bf16[4,2,128,128]{3,2,1,0:T(8,128)(2,1)S(1)}, u32[]{:S(2)}, u32[]{:S(2)}) collective-permute-start(bf16[4,2,128,128]{3,2,1,0:T(8,128)(2,1)S(1)} %pad_maximum_fusion.1.refs_1_), channel_id=1, source_target_pairs={{0,4},{4,0},{8,12},{12,8},{16,20},{20,16},{24,28},{28,24},{1,5},{5... | collective-permute-start | bytes 786440 | tf_op jit(solution)/shard_map/ppermute | solution.py:299
  69.6 6.6 %collective-permute-start.19 = (bf16[4,2,128,128]{3,2,1,0:T(8,128)(2,1)S(1)}, bf16[4,2,128,128]{3,2,1,0:T(8,128)(2,1)S(1)}, u32[]{:S(2)}, u32[]{:S(2)}) collective-permute-start(bf16[4,2,128,128]{3,2,1,0:T(8,128)(2,1)S(1)} %pad_maximum_fusion.1.refs_1_), channel_id=1, source_target_pairs={{0,16},{4,12},{8,24},{12,4},{16,0},{20,28},{24,8},{28,20},{1,17},{... | collective-permute-start | bytes 786440 | tf_op jit(solution)/shard_map/ppermute | solution.py:305
  72.5 8.7 %collective-permute-start.13 = (bf16[4,2,128,128]{3,2,1,0:T(8,128)(2,1)S(1)}, bf16[4,2,128,128]{3,2,1,0:T(8,128)(2,1)S(1)}, u32[]{:S(2)}, u32[]{:S(2)}) collective-permute-start(bf16[4,2,128,128]{3,2,1,0:T(8,128)(2,1)S(1)} %pad_maximum_fusion.refs_0_), channel_id=1, source_target_pairs={{0,4},{4,0},{8,12},{12,8},{16,20},{20,16},{24,28},{28,24},{1,5},{5... | collective-permute-start | bytes 786440 | tf_op jit(solution)/shard_map/ppermute | solution.py:299
  72.6 8.6 %collective-permute-start.18 = (bf16[4,2,128,128]{3,2,1,0:T(8,128)(2,1)S(1)}, bf16[4,2,128,128]{3,2,1,0:T(8,128)(2,1)S(1)}, u32[]{:S(2)}, u32[]{:S(2)}) collective-permute-start(bf16[4,2,128,128]{3,2,1,0:T(8,128)(2,1)S(1)} %pad_maximum_fusion.refs_0_), channel_id=1, source_target_pairs={{0,16},{4,12},{8,24},{12,4},{16,0},{20,28},{24,8},{28,20},{1,17},{... | collective-permute-start | bytes 786440 | tf_op jit(solution)/shard_map/ppermute | solution.py:305
  74.2 7.9 %collective-permute-start.22 = (bf16[4,2,128,128]{3,2,1,0:T(8,128)(2,1)S(1)}, bf16[4,2,128,128]{3,2,1,0:T(8,128)(2,1)S(1)}, u32[]{:S(2)}, u32[]{:S(2)}) collective-permute-start(bf16[4,2,128,128]{3,2,1,0:T(8,128)(2,1)S(1)} %pad_maximum_fusion.1.refs_1_), channel_id=1, source_target_pairs={{0,8},{4,20},{8,0},{12,28},{16,24},{20,4},{24,16},{28,12},{1,9},{5... | collective-permute-start | bytes 786440 | tf_op jit(solution)/shard_map/ppermute | solution.py:305
  75.7 8.5 %collective-permute-start.20 = (bf16[4,2,128,128]{3,2,1,0:T(8,128)(2,1)S(1)}, bf16[4,2,128,128]{3,2,1,0:T(8,128)(2,1)S(1)}, u32[]{:S(2)}, u32[]{:S(2)}) collective-permute-start(bf16[4,2,128,128]{3,2,1,0:T(8,128)(2,1)S(1)} %pad_maximum_fusion.refs_0_), channel_id=1, source_target_pairs={{0,8},{4,20},{8,0},{12,28},{16,24},{20,4},{24,16},{28,12},{1,9},{5... | collective-permute-start | bytes 786440 | tf_op jit(solution)/shard_map/ppermute | solution.py:305
  76.2 10.4 %collective-permute-start.25 = (bf16[4,2,128,128]{3,2,1,0:T(8,128)(2,1)S(1)}, bf16[4,2,128,128]{3,2,1,0:T(8,128)(2,1)S(1)}, u32[]{:S(2)}, u32[]{:S(2)}) collective-permute-start(bf16[4,2,128,128]{3,2,1,0:T(8,128)(2,1)S(1)} %collective-permute-done.19.refs_1_), channel_id=1, source_target_pairs={{0,4},{4,0},{8,12},{12,8},{16,20},{20,16},{24,28},{28,24},{1,5},{5... | collective-permute-start | bytes 786440 | tf_op jit(solution)/shard_map/ppermute | solution.py:299
  81.2 6.9 %collective-permute-start.24 = (bf16[4,2,128,128]{3,2,1,0:T(8,128)(2,1)S(1)}, bf16[4,2,128,128]{3,2,1,0:T(8,128)(2,1)S(1)}, u32[]{:S(2)}, u32[]{:S(2)}) collective-permute-start(bf16[4,2,128,128]{3,2,1,0:T(8,128)(2,1)S(1)} %collective-permute-done.18.refs_0_), channel_id=1, source_target_pairs={{0,4},{4,0},{8,12},{12,8},{16,20},{20,16},{24,28},{28,24},{1,5},{5... | collective-permute-start | bytes 786440 | tf_op jit(solution)/shard_map/ppermute | solution.py:299
  82.1 8.2 %collective-permute-start.23 = (bf16[4,2,128,128]{3,2,1,0:T(8,128)(2,1)S(1)}, bf16[4,2,128,128]{3,2,1,0:T(8,128)(2,1)S(1)}, u32[]{:S(2)}, u32[]{:S(2)}) collective-permute-start(bf16[4,2,128,128]{3,2,1,0:T(8,128)(2,1)S(1)} %collective-permute-done.22.refs_1_), channel_id=1, source_target_pairs={{0,4},{4,0},{8,12},{12,8},{16,20},{20,16},{24,28},{28,24},{1,5},{5... | collective-permute-start | bytes 786440 | tf_op jit(solution)/shard_map/ppermute | solution.py:299
  82.6 9.9 %collective-permute-start.27 = (bf16[4,2,128,128]{3,2,1,0:T(8,128)(2,1)S(1)}, bf16[4,2,128,128]{3,2,1,0:T(8,128)(2,1)S(1)}, u32[]{:S(2)}, u32[]{:S(2)}) collective-permute-start(bf16[4,2,128,128]{3,2,1,0:T(8,128)(2,1)S(1)} %collective-permute-done.22.refs_1_), channel_id=1, source_target_pairs={{0,16},{4,12},{8,24},{12,4},{16,0},{20,28},{24,8},{28,20},{1,17},{... | collective-permute-start | bytes 786440 | tf_op jit(solution)/shard_map/ppermute | solution.py:305
  84.1 6.2 %collective-permute-start.21 = (bf16[4,2,128,128]{3,2,1,0:T(8,128)(2,1)S(1)}, bf16[4,2,128,128]{3,2,1,0:T(8,128)(2,1)S(1)}, u32[]{:S(2)}, u32[]{:S(2)}) collective-permute-start(bf16[4,2,128,128]{3,2,1,0:T(8,128)(2,1)S(1)} %collective-permute-done.20.refs_0_), channel_id=1, source_target_pairs={{0,4},{4,0},{8,12},{12,8},{16,20},{20,16},{24,28},{28,24},{1,5},{5... | collective-permute-start | bytes 786440 | tf_op jit(solution)/shard_map/ppermute | solution.py:299
  86.6 6.4 %collective-permute-start.26 = (bf16[4,2,128,128]{3,2,1,0:T(8,128)(2,1)S(1)}, bf16[4,2,128,128]{3,2,1,0:T(8,128)(2,1)S(1)}, u32[]{:S(2)}, u32[]{:S(2)}) collective-permute-start(bf16[4,2,128,128]{3,2,1,0:T(8,128)(2,1)S(1)} %collective-permute-done.20.refs_0_), channel_id=1, source_target_pairs={{0,16},{4,12},{8,24},{12,4},{16,0},{20,28},{24,8},{28,20},{1,17},{... | collective-permute-start | bytes 786440 | tf_op jit(solution)/shard_map/ppermute | solution.py:305
  93.0 1.5 %collective-permute-start.28 = (bf16[4,2,128,128]{3,2,1,0:T(8,128)(2,1)S(1)}, bf16[4,2,128,128]{3,2,1,0:T(8,128)(2,1)S(1)}, u32[]{:S(2)}, u32[]{:S(2)}) collective-permute-start(bf16[4,2,128,128]{3,2,1,0:T(8,128)(2,1)S(1)} %collective-permute-done.26.refs_0_), channel_id=1, source_target_pairs={{0,4},{4,0},{8,12},{12,8},{16,20},{20,16},{24,28},{28,24},{1,5},{5... | collective-permute-start | bytes 786440 | tf_op jit(solution)/shard_map/ppermute | solution.py:299
  93.0 1.9 %collective-permute-start.29 = (bf16[4,2,128,128]{3,2,1,0:T(8,128)(2,1)S(1)}, bf16[4,2,128,128]{3,2,1,0:T(8,128)(2,1)S(1)}, u32[]{:S(2)}, u32[]{:S(2)}) collective-permute-start(bf16[4,2,128,128]{3,2,1,0:T(8,128)(2,1)S(1)} %collective-permute-done.27.refs_1_), channel_id=1, source_target_pairs={{0,4},{4,0},{8,12},{12,8},{16,20},{20,16},{24,28},{28,24},{1,5},{5... | collective-permute-start | bytes 786440 | tf_op jit(solution)/shard_map/ppermute | solution.py:299
  (1 other events, 17.1 us)

commit v5 on v4

--- a/solution.py
+++ b/solution.py
@@ -13,6 +13,7 @@
 WAVE_PIECES = (0, 1, 0, 1, 2, 0)
 TURNS = 0.15915494309189535
 CHUNKS = 2
+ROWS, LANES, DIRECT = 32, 256, 1
 BIG = pltpu.CompilerParams(vmem_limit_bytes=48 << 20)
 
 
@@ -35,65 +36,80 @@
 
 def forces_kernel(
     piece,
-    sub,
     coords_ref,
     wave_ref,
     shapes_ref,
     mine_ref,
     other_ref,
+    spread,
     wave_pieces,
     even_turns,
     odd_turns,
     even,
     odd,
 ):
-    step, steps = pl.program_id(0), pl.num_programs(0)
+    step = pl.program_id(0)
     waves = wave_ref.shape[1]
     own = waves // 2
     count = shapes_ref.shape[1] // piece
     nodes = coords_ref.shape[1]
     turns, load = (even_turns, odd_turns), (even, odd)
+    direct = DIRECT * LANES
 
     def phase(start, into):
-        for j in range(0, piece, sub):
-            at = pl.multiple_of(start + j, sub)
-            into[j : j + sub, :] = lax.dot_general(
-                pieces(coords_ref[:, pl.ds(at, sub)], COORD_PIECES),
-                wave_pieces[...],
-                (((0,), (0,)), ((), ())),
-                preferred_element_type=jnp.float32,
-            )
-
-    def points(angles, into):
-        for j in range(0, piece, 64):
-            rows = slice(j, j + 64)
-            cosine, sine = (x.astype(jnp.bfloat16) for x in circle(angles[rows, :]))
-            into[rows, :own] = cosine[:, :own]
-            into[rows, own : 2 * own] = sine[:, :own]
-            into[rows, 2 * own : 3 * own] = cosine[:, own:]
-            into[rows, 3 * own :] = sine[:, own:]
+        at = pl.multiple_of(start + direct, LANES)
+        into[...] = jnp.dot(
+            wave_pieces[...],
+            pieces(coords_ref[:, pl.ds(at, piece - direct)], COORD_PIECES),
+            preferred_element_type=jnp.float32,
+        )
+
+    def points(start, angles, into):
+        for j in range(0, piece, LANES):
+            columns = slice(j, j + LANES)
+            if j < direct:
+                at = pl.multiple_of(start + j, LANES)
+                x, y, z = (coords_ref[i : i + 1, pl.ds(at, LANES)] for i in range(3))
+            for w in range(0, waves, ROWS):
+                rows = slice(w, w + ROWS)
+                if j < direct:
+                    a, b, c = (spread[i, rows, :] for i in range(3))
+                    angle = a * x + b * y + c * z
+                else:
+                    angle = angles[rows, j - direct : j - direct + LANES]
+                cosine, sine = circle(angle)
+                to = w if w < own else w + own
+                into[to : to + ROWS, columns] = cosine.astype(jnp.bfloat16)
+                into[to + own : to + own + ROWS, columns] = sine.astype(jnp.bfloat16)
 
     @pl.when(step == 0)
     def _():
         first, second = wave_ref[:, :own], wave_ref[:, own:]
         swap = lax.rem(lax.axis_index("node"), 2) == 1
-        ordered = jnp.concatenate(
+        ordered = TURNS * jnp.concatenate(
             [jnp.where(swap, second, first), jnp.where(swap, first, second)], axis=1
         )
-        wave_pieces[...] = pieces(ordered * TURNS, WAVE_PIECES)
+        wave_pieces[...] = pieces(ordered, WAVE_PIECES).astype(jnp.float32).T.astype(jnp.bfloat16)
+        columns = jnp.concatenate([ordered, jnp.zeros((5, waves), jnp.float32)], axis=0).T
+        for i in range(3):
+            spread[i] = jnp.broadcast_to(columns[:, i : i + 1], (waves, LANES))
         mine_ref[...] = jnp.zeros_like(mine_ref)
         other_ref[...] = jnp.zeros_like(other_ref)
         phase(0, turns[0])
         phase(piece, turns[1])
-        points(turns[0], load[0])
+        points(0, turns[0], load[0])
+
+    def wrapped(start):
+        return jnp.where(start >= nodes, 0, start)
 
     for p in range(count):
-        ahead = (step * count + p + 2) * piece
-        phase(jnp.where(ahead >= nodes, 0, ahead), turns[p % 2])
-        points(turns[(p + 1) % 2], load[(p + 1) % 2])
-        product = jnp.dot(
+        here = (step * count + p) * piece
+        phase(wrapped(here + 2 * piece), turns[p % 2])
+        points(wrapped(here + piece), turns[(p + 1) % 2], load[(p + 1) % 2])
+        product = lax.dot_general(
             shapes_ref[:, p * piece : (p + 1) * piece],
             load[p % 2][...],
+            (((1,), (1,)), ((), ())),
             preferred_element_type=jnp.float32,
         )
         mine_ref[...] += product[:, :waves]
@@ -103,10 +119,10 @@
 def unit_forces(coords, wavevec, mode_shapes):
     modes, nodes = mode_shapes.shape
     waves = wavevec.shape[1]
-    block, piece, sub = 4096, 1024, 1024
+    block, piece = 4096, 1024
     out = jax.ShapeDtypeStruct((modes, waves), jnp.float32)
     return pl.pallas_call(
-        functools.partial(forces_kernel, piece, sub),
+        functools.partial(forces_kernel, piece),
         grid=(nodes // block,),
         in_specs=[
             pl.BlockSpec((3, nodes), lambda i: (0, 0)),
@@ -116,11 +132,12 @@
         out_specs=[pl.BlockSpec((modes, waves), lambda i: (0, 0))] * 2,
         out_shape=[out, out],
         scratch_shapes=[
-            pltpu.VMEM((8 * len(WAVE_PIECES), waves), jnp.bfloat16),
-            pltpu.VMEM((piece, waves), jnp.float32),
-            pltpu.VMEM((piece, waves), jnp.float32),
-            pltpu.VMEM((piece, 2 * waves), jnp.bfloat16),
-            pltpu.VMEM((piece, 2 * waves), jnp.bfloat16),
+            pltpu.VMEM((3, waves, LANES), jnp.float32),
+            pltpu.VMEM((waves, 8 * len(WAVE_PIECES)), jnp.bfloat16),
+            pltpu.VMEM((waves, piece - DIRECT * LANES), jnp.float32),
+            pltpu.VMEM((waves, piece - DIRECT * LANES), jnp.float32),
+            pltpu.VMEM((2 * waves, piece), jnp.bfloat16),
+            pltpu.VMEM((2 * waves, piece), jnp.bfloat16),
         ],
         compiler_params=pltpu.CompilerParams(vmem_limit_bytes=60 << 20),
         cost_estimate=pl.CostEstimate(
@@ -242,37 +259,35 @@
     depth, rows = data[0].shape[-2:]
     mode = lax.axis_index("mode")
     order = [lax.rem(mode - z + blocks, blocks) for z in range(blocks)]
-    right = jnp.concatenate(
-        [jnp.concatenate([ref[at] for at in order], axis=1) for ref in data], axis=0
-    )
     left = jnp.concatenate([left_ref[n] for n in range(len(data))], axis=1)
-    total = jnp.dot(left, right, preferred_element_type=jnp.float32) * (1.0 / (CHUNKS * depth))
-    out_ref[0] = total[:rows]
-    out_ref[1] = total[rows:]
+    for side in range(2):
+        sides = [jnp.bitwise_xor(side, place_ref[1]), jnp.bitwise_xor(side, 1 - place_ref[1])]
+        right = jnp.concatenate(
+            [
+                jnp.concatenate([ref[at, sides[n // CHUNKS]] for at in order], axis=1)
+                for n, ref in enumerate(data)
+            ],
+            axis=0,
+        )
+        total = jnp.dot(left, right, preferred_element_type=jnp.float32) * (1.0 / (CHUNKS * depth))
+        columns = slice(side * blocks * rows, (side + 1) * blocks * rows)
+        out_ref[0, :, columns] = total[:rows]
+        out_ref[1, :, columns] = total[rows:]
 
 
 def cross_spectra(place, blocks, groups, spectra, left, ours, theirs):
     depth, rows = ours[0].shape[-2:]
-
-    def of_ours(s, place_ref):
-        return (0, jnp.bitwise_xor(s, place_ref[1]), 0, 0)
-
-    def of_theirs(s, place_ref):
-        return (0, jnp.bitwise_xor(s, 1 - place_ref[1]), 0, 0)
-
-    block = (blocks, None, depth, rows)
     started = spectra is not None
     return pl.pallas_call(
         functools.partial(spectra_kernel, blocks),
         grid_spec=pltpu.PrefetchScalarGridSpec(
             num_scalar_prefetch=1,
-            grid=(2,),
+            grid=(1,),
             in_specs=[pl.BlockSpec(left.shape, lambda s, place_ref: (0, 0, 0))]
-            + [pl.BlockSpec(block, of_ours)] * CHUNKS
-            + [pl.BlockSpec(block, of_theirs)] * CHUNKS
+            + [pl.BlockSpec(ours[0].shape, lambda s, place_ref: (0, 0, 0, 0))] * (2 * CHUNKS)
             + [pl.BlockSpec(memory_space=pl.ANY)] * started,
             out_specs=pl.BlockSpec(
-                (2, rows, blocks * rows), lambda s, place_ref: (0, 0, 2 * place_ref[0] + s)
+                (2, rows, 2 * blocks * rows), lambda s, place_ref: (0, 0, place_ref[0])
             ),
         ),
         out_shape=jax.ShapeDtypeStruct((2, rows, 2 * groups * blocks * rows), jnp.float32),

time: 97.3 us -> 95.9 us (0.986)
  Pallas kernels: 38.4 us -> 36.7 us
    pallas_call x1, Pallas kernels: 27.4 us -> 26.4 us  [unit_forces(): pl.pallas_call(functools.partial(forces_kernel, piece), grid=(nodes // bl...]
  transfers between devices with their start and end apart: 30 -> 30, of which waited for: 10 -> 10; matrix products, arithmetic and copies ran while one was open for 3% -> 3% of each run, Pallas kernels for 8% -> 7%
where the time goes in v5:
time: 95.9 us; the launch traced here: 95.7 us
  starting transfers between devices  36.9 us (38%)
  Pallas kernels  36.7 us (38%)
  waiting for transfers between devices  18.2 us (19%)
  other arithmetic  1.67 us (2%)
  local copies, waits for them, and re-layouts  1.57 us (2%)
    pallas_call x1, Pallas kernels, unit_forces(): pl.pallas_call(functools.partial(forces_kernel, piece), grid=(nodes // bl...  26.4 us
    ppermute x12, starting transfers between devices, along(): lax.ppermute(x, 'mode', [(i, (i + k) % blocks) for i in range(blocks)])  21.5 us
    ppermute x8, starting transfers between devices, across(): return lax.ppermute(x, 'node', [(i, flip(i)) for i in range(nodes)])  13.2 us
    ppermute x8, waiting for transfers between devices, across(): return lax.ppermute(x, 'node', [(i, flip(i)) for i in range(nodes)])  12.8 us
    pallas_call x4, Pallas kernels, cross_spectra(): pl.pallas_call(functools.partial(spectra_kernel, blocks), grid_spec=pltpu...  7.89 us
    ppermute x10, waiting for transfers between devices, to_mate(): return lax.ppermute(x, 'node', [(i, i ^ 1) for i in range(nodes)])  2.99 us
    ppermute x12, waiting for transfers between devices, along(): lax.ppermute(x, 'mode', [(i, (i + k) % blocks) for i in range(blocks)])  2.46 us
    ppermute x10, starting transfers between devices, to_mate(): return lax.ppermute(x, 'node', [(i, i ^ 1) for i in range(nodes)])  2.12 us
  transfers between devices with their start and end apart: 30, of which 10 were waited for; matrix products, arithmetic and copies ran while one was open for 3% of the time, Pallas kernels for 7%

profile of v5, /device:TPU:0, one launch (start us, length us, event | category | flops | bytes accessed | tf_op | source)
XLA Modules:
  0.0 95.7 jit_solution(9289232825841456497)
XLA Ops:
  0.6 26.4 %shard_map.77 = (f32[500,256]{1,0:T(8,128)}, f32[500,256]{1,0:T(8,128)}) custom-call(f32[3,24576]{1,0:T(4,128)} %coords_ref.1, f32[3,256]{1,0:T(4,128)} %wave_ref.1, bf16[500,24576]{1,0:T(8,128)(2,1)} %shapes_ref.1), custom_call_target="tpu_custom_call" | custom-call | flops 37748736000 | bytes 24576000 | tf_op jit(solution)/shard_map/pallas_call | solution.py:124
  27.7 1.6 %collective-permute-done = f32[500,256]{1,0:T(8,128)S(1)} collective-permute-done((f32[500,256]{1,0:T(8,128)}, f32[500,256]{1,0:T(8,128)S(1)}, u32[]{:S(2)}, u32[]{:S(2)}) %collective-permute-start) | collective-permute-done | bytes 512032 | tf_op jit(solution)/shard_map/ppermute | solution.py:314
  29.3 1.1 %fusion.1 = (bf16[500,256]{1,0:T(8,128)(2,1)S(1)}, f32[500,256]{1,0:T(8,128)S(1)}) fusion(f32[500,256]{1,0:T(8,128)} %get-tuple-element.17, f32[500,256]{1,0:T(8,128)S(1)} %collective-permute-done), kind=kLoop, calls=%fused_computation.14 | loop fusion | flops 256000 | bytes 1792000 | tf_op jit(solution)/shard_map/convert_element_type | solution.py:329
  30.5 2.9 %collective-permute-start.1 = (bf16[500,256]{1,0:T(8,128)(2,1)S(1)}, bf16[500,256]{1,0:T(8,128)(2,1)S(1)}, u32[]{:S(2)}, u32[]{:S(2)}) collective-permute-start(bf16[500,256]{1,0:T(8,128)(2,1)S(1)} %get-tuple-element.34), channel_id=1, source_target_pairs={{0,8},{4,20},{8,0},{12,28},{16,24},{20,4},{24,16},{28,12},{1,9},{5... | collective-permute-start | bytes 768008 | tf_op jit(solution)/shard_map/ppermute | solution.py:320
  33.4 4.3 %collective-permute-done.1 = bf16[500,256]{1,0:T(8,128)(2,1)S(1)} collective-permute-done((bf16[500,256]{1,0:T(8,128)(2,1)S(1)}, bf16[500,256]{1,0:T(8,128)(2,1)S(1)}, u32[]{:S(2)}, u32[]{:S(2)}) %collective-permute-start.1) | collective-permute-done | bytes 256032 | tf_op jit(solution)/shard_map/ppermute | solution.py:320
  37.8 2.1 %collective-permute-start.2 = (bf16[500,256]{1,0:T(8,128)(2,1)S(1)}, bf16[500,256]{1,0:T(8,128)(2,1)S(1)}, u32[]{:S(2)}, u32[]{:S(2)}) collective-permute-start(bf16[500,256]{1,0:T(8,128)(2,1)S(1)} %get-tuple-element.32), channel_id=1, source_target_pairs={{0,16},{4,12},{8,24},{12,4},{16,0},{20,28},{24,8},{28,20},{1,17},{... | collective-permute-start | bytes 768008 | tf_op jit(solution)/shard_map/ppermute | solution.py:320
  40.2 1.4 %copy.14.mate_ref = bf16[2,500,512]{2,1,0:T(8,128)(2,1)S(1)} copy(bf16[2,500,512]{2,0,1:T(2,128)(2,1)} %collective-permute-done.3) | data formatting | bytes 2048000 | tf_op jit(solution)/shard_map/ppermute | solution.py:314
  41.6 2.6 %collective-permute-done.2.last_ref = bf16[500,256]{1,0:T(8,128)(2,1)S(1)} collective-permute-done((bf16[500,256]{1,0:T(8,128)(2,1)S(1)}, bf16[500,256]{1,0:T(8,128)(2,1)S(1)}, u32[]{:S(2)}, u32[]{:S(2)}) %collective-permute-start.2) | collective-permute-done | bytes 256032 | tf_op jit(solution)/shard_map/ppermute | solution.py:320
  44.2 1.5 %shard_map.78 = (f32[2,128,128]{2,1,0:T(8,128)S(1)}, f32[2,128,128]{2,1,0:T(8,128)S(1)}, bf16[2,128,128]{2,1,0:T(8,128)(2,1)S(1)}, bf16[2,128,128]{2,1,0:T(8,128...) custom-call(f32[500,256]{1,0:T(8,128)S(1)} %get-tuple-element.33.kep, ...), custom_call_target="tpu_custom_call" | custom-call | flops 524288000 | bytes 2048000 | tf_op jit(solution)/shard_map/pallas_call | solution.py:207
  45.7 2.1 %collective-permute-start.7 = (bf16[2,128,128]{2,1,0:T(8,128)(2,1)S(1)}, bf16[2,128,128]{2,1,0:T(8,128)(2,1)S(1)}, u32[]{:S(2)}, u32[]{:S(2)}) collective-permute-start(bf16[2,128,128]{2,1,0:T(8,128)(2,1)S(1)} %get-tuple-element.24), channel_id=1, source_target_pairs={{0,1},{1,2},{2,3},{3,0},{4,5},{5,6},{6,7},{7,4},{8,9},{9,10},{10,1... | collective-permute-start | bytes 196616 | tf_op jit(solution)/shard_map/ppermute | solution.py:323
  47.8 2.6 %collective-permute-start.8 = (bf16[2,128,128]{2,1,0:T(8,128)(2,1)S(1)}, bf16[2,128,128]{2,1,0:T(8,128)(2,1)S(1)}, u32[]{:S(2)}, u32[]{:S(2)}) collective-permute-start(bf16[2,128,128]{2,1,0:T(8,128)(2,1)S(1)} %get-tuple-element.25), channel_id=1, source_target_pairs={{0,2},{1,3},{2,0},{3,1},{4,6},{5,7},{6,4},{7,5},{8,10},{9,11},{10,... | collective-permute-start | bytes 196616 | tf_op jit(solution)/shard_map/ppermute | solution.py:323
  50.4 1.3 %collective-permute-start.9 = (bf16[2,128,128]{2,1,0:T(8,128)(2,1)S(1)}, bf16[2,128,128]{2,1,0:T(8,128)(2,1)S(1)}, u32[]{:S(2)}, u32[]{:S(2)}) collective-permute-start(bf16[2,128,128]{2,1,0:T(8,128)(2,1)S(1)} %get-tuple-element.26), channel_id=1, source_target_pairs={{0,3},{1,0},{2,1},{3,2},{4,7},{5,4},{6,5},{7,6},{8,11},{9,8},{10,9... | collective-permute-start | bytes 196616 | tf_op jit(solution)/shard_map/ppermute | solution.py:323
  52.9 2.8 %collective-permute-start.6 = (bf16[2,128,128]{2,1,0:T(8,128)(2,1)S(1)}, bf16[2,128,128]{2,1,0:T(8,128)(2,1)S(1)}, u32[]{:S(2)}, u32[]{:S(2)}) collective-permute-start(bf16[2,128,128]{2,1,0:T(8,128)(2,1)S(1)} %get-tuple-element.22), channel_id=1, source_target_pairs={{0,3},{1,0},{2,1},{3,2},{4,7},{5,4},{6,5},{7,6},{8,11},{9,8},{10,9... | collective-permute-start | bytes 196616 | tf_op jit(solution)/shard_map/ppermute | solution.py:323
  55.7 0.7 collective-permute-done.9
  56.5 1.1 %collective-permute-start.14 = (bf16[2,128,128]{2,1,0:T(8,128)(2,1)S(1)}, bf16[2,128,128]{2,1,0:T(8,128)(2,1)S(1)}, u32[]{:S(2)}, u32[]{:S(2)}) collective-permute-start(bf16[2,128,128]{2,1,0:T(8,128)(2,1)S(1)} %add_convert_fusion), channel_id=1, source_target_pairs={{0,1},{1,2},{2,3},{3,0},{4,5},{5,6},{6,7},{7,4},{8,9},{9,10},{10,1... | collective-permute-start | bytes 196616 | tf_op jit(solution)/shard_map/ppermute | solution.py:323
  57.6 3.2 %collective-permute-start.15 = (bf16[2,128,128]{2,1,0:T(8,128)(2,1)S(1)}, bf16[2,128,128]{2,1,0:T(8,128)(2,1)S(1)}, u32[]{:S(2)}, u32[]{:S(2)}) collective-permute-start(bf16[2,128,128]{2,1,0:T(8,128)(2,1)S(1)} %add_convert_fusion), channel_id=1, source_target_pairs={{0,2},{1,3},{2,0},{3,1},{4,6},{5,7},{6,4},{7,5},{8,10},{9,11},{10,... | collective-permute-start | bytes 196616 | tf_op jit(solution)/shard_map/ppermute | solution.py:323
  61.3 4.8 %collective-permute-start.10 = (bf16[2,128,128]{2,1,0:T(8,128)(2,1)S(1)}, bf16[2,128,128]{2,1,0:T(8,128)(2,1)S(1)}, u32[]{:S(2)}, u32[]{:S(2)}) collective-permute-start(bf16[2,128,128]{2,1,0:T(8,128)(2,1)S(1)} %add_convert_fusion.1), channel_id=1, source_target_pairs={{0,1},{1,2},{2,3},{3,0},{4,5},{5,6},{6,7},{7,4},{8,9},{9,10},{10,1... | collective-permute-start | bytes 196616 | tf_op jit(solution)/shard_map/ppermute | solution.py:323
  66.4 2.2 %collective-permute-start.12 = (bf16[2,128,128]{2,1,0:T(8,128)(2,1)S(1)}, bf16[2,128,128]{2,1,0:T(8,128)(2,1)S(1)}, u32[]{:S(2)}, u32[]{:S(2)}) collective-permute-start(bf16[2,128,128]{2,1,0:T(8,128)(2,1)S(1)} %add_convert_fusion.1), channel_id=1, source_target_pairs={{0,3},{1,0},{2,1},{3,2},{4,7},{5,4},{6,5},{7,6},{8,11},{9,8},{10,9... | collective-permute-start | bytes 196616 | tf_op jit(solution)/shard_map/ppermute | solution.py:323
  68.7 1.6 %collective-permute-start.19 = (bf16[4,2,128,128]{3,2,1,0:T(8,128)(2,1)S(1)}, bf16[4,2,128,128]{3,2,1,0:T(8,128)(2,1)S(1)}, u32[]{:S(2)}, u32[]{:S(2)}) collective-permute-start(bf16[4,2,128,128]{3,2,1,0:T(8,128)(2,1)S(1)} %pad_maximum_fusion.1.refs_1_), channel_id=1, source_target_pairs={{0,16},{4,12},{8,24},{12,4},{16,0},{20,28},{24,8},{28,20},{1,17},{... | collective-permute-start | bytes 786440 | tf_op jit(solution)/shard_map/ppermute | solution.py:320
  70.3 1.2 %collective-permute-done.11 = bf16[2,128,128]{2,1,0:T(8,128)(2,1)S(1)} collective-permute-done((bf16[2,128,128]{2,1,0:T(8,128)(2,1)S(1)}, bf16[2,128,128]{2,1,0:T(8,128)(2,1)S(1)}, u32[]{:S(2)}, u32[]{:S(2)}) %collective-permute-start.11) | collective-permute-done | bytes 65568 | tf_op jit(solution)/shard_map/ppermute | solution.py:323
  71.6 1.6 %collective-permute-start.18 = (bf16[4,2,128,128]{3,2,1,0:T(8,128)(2,1)S(1)}, bf16[4,2,128,128]{3,2,1,0:T(8,128)(2,1)S(1)}, u32[]{:S(2)}, u32[]{:S(2)}) collective-permute-start(bf16[4,2,128,128]{3,2,1,0:T(8,128)(2,1)S(1)} %pad_maximum_fusion.refs_0_), channel_id=1, source_target_pairs={{0,16},{4,12},{8,24},{12,4},{16,0},{20,28},{24,8},{28,20},{1,17},{... | collective-permute-start | bytes 786440 | tf_op jit(solution)/shard_map/ppermute | solution.py:320
  73.2 1.5 %collective-permute-start.22 = (bf16[4,2,128,128]{3,2,1,0:T(8,128)(2,1)S(1)}, bf16[4,2,128,128]{3,2,1,0:T(8,128)(2,1)S(1)}, u32[]{:S(2)}, u32[]{:S(2)}) collective-permute-start(bf16[4,2,128,128]{3,2,1,0:T(8,128)(2,1)S(1)} %pad_maximum_fusion.1.refs_1_), channel_id=1, source_target_pairs={{0,8},{4,20},{8,0},{12,28},{16,24},{20,4},{24,16},{28,12},{1,9},{5... | collective-permute-start | bytes 786440 | tf_op jit(solution)/shard_map/ppermute | solution.py:320
  75.3 5.0 %collective-permute-done.18.refs_0_ = bf16[4,2,128,128]{3,2,1,0:T(8,128)(2,1)S(1)} collective-permute-done((bf16[4,2,128,128]{3,2,1,0:T(8,128)(2,1)S(1)}, bf16[4,2,128,128]{3,2,1,0:T(8,128)(2,1)S(1)}, u32[]{:S(2)}, u32[]{:S(2)}) %collective-permute-start.18) | collective-permute-done | bytes 262176 | tf_op jit(solution)/shard_map/ppermute | solution.py:320
  80.3 0.9 shard_map.79
  81.6 1.5 %collective-permute-start.27 = (bf16[4,2,128,128]{3,2,1,0:T(8,128)(2,1)S(1)}, bf16[4,2,128,128]{3,2,1,0:T(8,128)(2,1)S(1)}, u32[]{:S(2)}, u32[]{:S(2)}) collective-permute-start(bf16[4,2,128,128]{3,2,1,0:T(8,128)(2,1)S(1)} %collective-permute-done.22.refs_1_), channel_id=1, source_target_pairs={{0,16},{4,12},{8,24},{12,4},{16,0},{20,28},{24,8},{28,20},{1,17},{... | collective-permute-start | bytes 786440 | tf_op jit(solution)/shard_map/ppermute | solution.py:320
  83.5 2.0 %shard_map.80.refs_4_ = f32[2,128,4096]{2,1,0:T(8,128)} custom-call(s32[2]{0:T(128)S(1)} %pad_add_fusion.3.place_ref, bf16[4,256,128]{2,1,0:T(8,128)(2,1)S(1)} %get-tuple-element.27.left_ref, bf16[4,2,128,128]{3,2,1,0:T(8,128)(2,1)S(1)} %pad_maximum_fusion.refs_0_, bf16[4,2,128,128]{3,2,1,0:T(8,128)(2,1)S(1)} %pad_maximum_fusion.1.refs_1_, ...), custom_call_target="tpu_custom_call" | custom-call | flops 2684354560 | bytes 2097152 | tf_op jit(solution)/shard_map/pallas_call | solution.py:281
  85.5 1.5 %collective-permute-start.26 = (bf16[4,2,128,128]{3,2,1,0:T(8,128)(2,1)S(1)}, bf16[4,2,128,128]{3,2,1,0:T(8,128)(2,1)S(1)}, u32[]{:S(2)}, u32[]{:S(2)}) collective-permute-start(bf16[4,2,128,128]{3,2,1,0:T(8,128)(2,1)S(1)} %collective-permute-done.20.refs_0_), channel_id=1, source_target_pairs={{0,16},{4,12},{8,24},{12,4},{16,0},{20,28},{24,8},{28,20},{1,17},{... | collective-permute-start | bytes 786440 | tf_op jit(solution)/shard_map/ppermute | solution.py:320
  87.0 2.0 %shard_map.81.refs_4_ = f32[2,128,4096]{2,1,0:T(8,128)} custom-call(s32[2]{0:T(128)S(1)} %pad_add_fusion.2.place_ref, bf16[4,256,128]{2,1,0:T(8,128)(2,1)S(1)} %get-tuple-element.27.left_ref, bf16[4,2,128,128]{3,2,1,0:T(8,128)(2,1)S(1)} %collective-permute-done.20.refs_0_, ...), custom_call_target="tpu_custom_call", output_to_operand_aliasing={{}: (6, {})} | custom-call | flops 2684354560 | bytes 2097152 | tf_op jit(solution)/shard_map/pallas_call | solution.py:281
  89.0 2.0 %shard_map.82.refs_4_ = f32[2,128,4096]{2,1,0:T(8,128)} custom-call(s32[2]{0:T(128)S(1)} %pad_add_fusion.1.place_ref, bf16[4,256,128]{2,1,0:T(8,128)(2,1)S(1)} %get-tuple-element.27.left_ref, bf16[4,2,128,128]{3,2,1,0:T(8,128)(2,1)S(1)} %collective-permute-done.18.refs_0_, ...), custom_call_target="tpu_custom_call", output_to_operand_aliasing={{}: (6, {})} | custom-call | flops 2684354560 | bytes 2097152 | tf_op jit(solution)/shard_map/pallas_call | solution.py:281
  91.0 0.9 collective-permute-done.26.refs_0_
  92.4 0.9 collective-permute-done.28.refs_2_
  93.8 2.0 %shard_map.83 = f32[2,128,4096]{2,1,0:T(8,128)} custom-call(s32[2]{0:T(128)S(1)} %pad_add_fusion.place_ref, bf16[4,256,128]{2,1,0:T(8,128)(2,1)S(1)} %get-tuple-element.27.left_ref, bf16[4,2,128,128]{3,2,1,0:T(8,128)(2,1)S(1)} %collective-permute-done.26.refs_0_, ...), custom_call_target="tpu_custom_call", output_to_operand_aliasing={{}: (6, {})} | custom-call | flops 2684354560 | bytes 2097152 | tf_op jit(solution)/shard_map/pallas_call | solution.py:281
  (57 shorter events, 5.5 us)
Async XLA Ops:
  0.6 27.0 %copy-start.2 = (bf16[2,500,512]{2,0,1:T(2,128)(2,1)S(1)}, bf16[2,500,512]{2,0,1:T(2,128)(2,1)}, u32[]{:S(2)}) copy-start(bf16[2,500,512]{2,0,1:T(2,128)(2,1)} %param.11) | copy-start | bytes 3072004
  27.1 17.1 %copy-start.1 = (f32[2,256]{1,0:T(2,128)S(1)}, f32[2,256]{1,0:T(2,128)}, u32[]{:S(2)}) copy-start(f32[2,256]{1,0:T(2,128)} %amp_ref.1) | copy-start | bytes 6148
  27.1 2.3 %collective-permute-start = (f32[500,256]{1,0:T(8,128)}, f32[500,256]{1,0:T(8,128)S(1)}, u32[]{:S(2)}, u32[]{:S(2)}) collective-permute-start(f32[500,256]{1,0:T(8,128)} %get-tuple-element.18), channel_id=1, source_target_pairs={{0,4},{4,0},{8,12},{12,8},{16,20},{20,16},{24,28},{28,24},{1,5},{5... | collective-permute-start | bytes 1536008 | tf_op jit(solution)/shard_map/ppermute | solution.py:314
  27.6 12.6 %collective-permute-start.3 = (bf16[2,500,512]{2,0,1:T(2,128)(2,1)S(1)}, bf16[2,500,512]{2,0,1:T(2,128)(2,1)}, u32[]{:S(2)}, u32[]{:S(2)}) collective-permute-start(bf16[2,500,512]{2,0,1:T(2,128)(2,1)S(1)} %copy-done.2), channel_id=1, source_target_pairs={{0,4},{4,0},{8,12},{12,8},{16,20},{20,16},{24,28},{28,24},{1,5},{5... | collective-permute-start | bytes 3072008 | tf_op jit(solution)/shard_map/ppermute | solution.py:314
  30.5 7.2 %collective-permute-start.1 = (bf16[500,256]{1,0:T(8,128)(2,1)S(1)}, bf16[500,256]{1,0:T(8,128)(2,1)S(1)}, u32[]{:S(2)}, u32[]{:S(2)}) collective-permute-start(bf16[500,256]{1,0:T(8,128)(2,1)S(1)} %get-tuple-element.34), channel_id=1, source_target_pairs={{0,8},{4,20},{8,0},{12,28},{16,24},{20,4},{24,16},{28,12},{1,9},{5... | collective-permute-start | bytes 768008 | tf_op jit(solution)/shard_map/ppermute | solution.py:320
  37.8 6.4 %collective-permute-start.2 = (bf16[500,256]{1,0:T(8,128)(2,1)S(1)}, bf16[500,256]{1,0:T(8,128)(2,1)S(1)}, u32[]{:S(2)}, u32[]{:S(2)}) collective-permute-start(bf16[500,256]{1,0:T(8,128)(2,1)S(1)} %get-tuple-element.32), channel_id=1, source_target_pairs={{0,16},{4,12},{8,24},{12,4},{16,0},{20,28},{24,8},{28,20},{1,17},{... | collective-permute-start | bytes 768008 | tf_op jit(solution)/shard_map/ppermute | solution.py:320
  45.7 7.2 %collective-permute-start.7 = (bf16[2,128,128]{2,1,0:T(8,128)(2,1)S(1)}, bf16[2,128,128]{2,1,0:T(8,128)(2,1)S(1)}, u32[]{:S(2)}, u32[]{:S(2)}) collective-permute-start(bf16[2,128,128]{2,1,0:T(8,128)(2,1)S(1)} %get-tuple-element.24), channel_id=1, source_target_pairs={{0,1},{1,2},{2,3},{3,0},{4,5},{5,6},{6,7},{7,4},{8,9},{9,10},{10,1... | collective-permute-start | bytes 196616 | tf_op jit(solution)/shard_map/ppermute | solution.py:323
  47.8 7.8 %collective-permute-start.8 = (bf16[2,128,128]{2,1,0:T(8,128)(2,1)S(1)}, bf16[2,128,128]{2,1,0:T(8,128)(2,1)S(1)}, u32[]{:S(2)}, u32[]{:S(2)}) collective-permute-start(bf16[2,128,128]{2,1,0:T(8,128)(2,1)S(1)} %get-tuple-element.25), channel_id=1, source_target_pairs={{0,2},{1,3},{2,0},{3,1},{4,6},{5,7},{6,4},{7,5},{8,10},{9,11},{10,... | collective-permute-start | bytes 196616 | tf_op jit(solution)/shard_map/ppermute | solution.py:323
  50.4 6.0 %collective-permute-start.9 = (bf16[2,128,128]{2,1,0:T(8,128)(2,1)S(1)}, bf16[2,128,128]{2,1,0:T(8,128)(2,1)S(1)}, u32[]{:S(2)}, u32[]{:S(2)}) collective-permute-start(bf16[2,128,128]{2,1,0:T(8,128)(2,1)S(1)} %get-tuple-element.26), channel_id=1, source_target_pairs={{0,3},{1,0},{2,1},{3,2},{4,7},{5,4},{6,5},{7,6},{8,11},{9,8},{10,9... | collective-permute-start | bytes 196616 | tf_op jit(solution)/shard_map/ppermute | solution.py:323
  51.8 9.0 %collective-permute-start.4 = (bf16[2,128,128]{2,1,0:T(8,128)(2,1)S(1)}, bf16[2,128,128]{2,1,0:T(8,128)(2,1)S(1)}, u32[]{:S(2)}, u32[]{:S(2)}) collective-permute-start(bf16[2,128,128]{2,1,0:T(8,128)(2,1)S(1)} %get-tuple-element.20), channel_id=1, source_target_pairs={{0,1},{1,2},{2,3},{3,0},{4,5},{5,6},{6,7},{7,4},{8,9},{9,10},{10,1... | collective-permute-start | bytes 196616 | tf_op jit(solution)/shard_map/ppermute | solution.py:323
  52.5 8.7 %collective-permute-start.5 = (bf16[2,128,128]{2,1,0:T(8,128)(2,1)S(1)}, bf16[2,128,128]{2,1,0:T(8,128)(2,1)S(1)}, u32[]{:S(2)}, u32[]{:S(2)}) collective-permute-start(bf16[2,128,128]{2,1,0:T(8,128)(2,1)S(1)} %get-tuple-element.21), channel_id=1, source_target_pairs={{0,2},{1,3},{2,0},{3,1},{4,6},{5,7},{6,4},{7,5},{8,10},{9,11},{10,... | collective-permute-start | bytes 196616 | tf_op jit(solution)/shard_map/ppermute | solution.py:323
  52.9 8.4 %collective-permute-start.6 = (bf16[2,128,128]{2,1,0:T(8,128)(2,1)S(1)}, bf16[2,128,128]{2,1,0:T(8,128)(2,1)S(1)}, u32[]{:S(2)}, u32[]{:S(2)}) collective-permute-start(bf16[2,128,128]{2,1,0:T(8,128)(2,1)S(1)} %get-tuple-element.22), channel_id=1, source_target_pairs={{0,3},{1,0},{2,1},{3,2},{4,7},{5,4},{6,5},{7,6},{8,11},{9,8},{10,9... | collective-permute-start | bytes 196616 | tf_op jit(solution)/shard_map/ppermute | solution.py:323
  56.5 9.9 %collective-permute-start.14 = (bf16[2,128,128]{2,1,0:T(8,128)(2,1)S(1)}, bf16[2,128,128]{2,1,0:T(8,128)(2,1)S(1)}, u32[]{:S(2)}, u32[]{:S(2)}) collective-permute-start(bf16[2,128,128]{2,1,0:T(8,128)(2,1)S(1)} %add_convert_fusion), channel_id=1, source_target_pairs={{0,1},{1,2},{2,3},{3,0},{4,5},{5,6},{6,7},{7,4},{8,9},{9,10},{10,1... | collective-permute-start | bytes 196616 | tf_op jit(solution)/shard_map/ppermute | solution.py:323
  57.6 11.0 %collective-permute-start.15 = (bf16[2,128,128]{2,1,0:T(8,128)(2,1)S(1)}, bf16[2,128,128]{2,1,0:T(8,128)(2,1)S(1)}, u32[]{:S(2)}, u32[]{:S(2)}) collective-permute-start(bf16[2,128,128]{2,1,0:T(8,128)(2,1)S(1)} %add_convert_fusion), channel_id=1, source_target_pairs={{0,2},{1,3},{2,0},{3,1},{4,6},{5,7},{6,4},{7,5},{8,10},{9,11},{10,... | collective-permute-start | bytes 196616 | tf_op jit(solution)/shard_map/ppermute | solution.py:323
  60.8 7.8 %collective-permute-start.16 = (bf16[2,128,128]{2,1,0:T(8,128)(2,1)S(1)}, bf16[2,128,128]{2,1,0:T(8,128)(2,1)S(1)}, u32[]{:S(2)}, u32[]{:S(2)}) collective-permute-start(bf16[2,128,128]{2,1,0:T(8,128)(2,1)S(1)} %add_convert_fusion), channel_id=1, source_target_pairs={{0,3},{1,0},{2,1},{3,2},{4,7},{5,4},{6,5},{7,6},{8,11},{9,8},{10,9... | collective-permute-start | bytes 196616 | tf_op jit(solution)/shard_map/ppermute | solution.py:323
  61.3 9.0 %collective-permute-start.10 = (bf16[2,128,128]{2,1,0:T(8,128)(2,1)S(1)}, bf16[2,128,128]{2,1,0:T(8,128)(2,1)S(1)}, u32[]{:S(2)}, u32[]{:S(2)}) collective-permute-start(bf16[2,128,128]{2,1,0:T(8,128)(2,1)S(1)} %add_convert_fusion.1), channel_id=1, source_target_pairs={{0,1},{1,2},{2,3},{3,0},{4,5},{5,6},{6,7},{7,4},{8,9},{9,10},{10,1... | collective-permute-start | bytes 196616 | tf_op jit(solution)/shard_map/ppermute | solution.py:323
  66.1 5.4 %collective-permute-start.11 = (bf16[2,128,128]{2,1,0:T(8,128)(2,1)S(1)}, bf16[2,128,128]{2,1,0:T(8,128)(2,1)S(1)}, u32[]{:S(2)}, u32[]{:S(2)}) collective-permute-start(bf16[2,128,128]{2,1,0:T(8,128)(2,1)S(1)} %add_convert_fusion.1), channel_id=1, source_target_pairs={{0,2},{1,3},{2,0},{3,1},{4,6},{5,7},{6,4},{7,5},{8,10},{9,11},{10,... | collective-permute-start | bytes 196616 | tf_op jit(solution)/shard_map/ppermute | solution.py:323
  66.4 5.2 %collective-permute-start.12 = (bf16[2,128,128]{2,1,0:T(8,128)(2,1)S(1)}, bf16[2,128,128]{2,1,0:T(8,128)(2,1)S(1)}, u32[]{:S(2)}, u32[]{:S(2)}) collective-permute-start(bf16[2,128,128]{2,1,0:T(8,128)(2,1)S(1)} %add_convert_fusion.1), channel_id=1, source_target_pairs={{0,3},{1,0},{2,1},{3,2},{4,7},{5,4},{6,5},{7,6},{8,11},{9,8},{10,9... | collective-permute-start | bytes 196616 | tf_op jit(solution)/shard_map/ppermute | solution.py:323
  68.6 6.1 %collective-permute-start.17 = (bf16[4,2,128,128]{3,2,1,0:T(8,128)(2,1)S(1)}, bf16[4,2,128,128]{3,2,1,0:T(8,128)(2,1)S(1)}, u32[]{:S(2)}, u32[]{:S(2)}) collective-permute-start(bf16[4,2,128,128]{3,2,1,0:T(8,128)(2,1)S(1)} %pad_maximum_fusion.1.refs_1_), channel_id=1, source_target_pairs={{0,4},{4,0},{8,12},{12,8},{16,20},{20,16},{24,28},{28,24},{1,5},{5... | collective-permute-start | bytes 786440 | tf_op jit(solution)/shard_map/ppermute | solution.py:314
  68.7 6.6 %collective-permute-start.19 = (bf16[4,2,128,128]{3,2,1,0:T(8,128)(2,1)S(1)}, bf16[4,2,128,128]{3,2,1,0:T(8,128)(2,1)S(1)}, u32[]{:S(2)}, u32[]{:S(2)}) collective-permute-start(bf16[4,2,128,128]{3,2,1,0:T(8,128)(2,1)S(1)} %pad_maximum_fusion.1.refs_1_), channel_id=1, source_target_pairs={{0,16},{4,12},{8,24},{12,4},{16,0},{20,28},{24,8},{28,20},{1,17},{... | collective-permute-start | bytes 786440 | tf_op jit(solution)/shard_map/ppermute | solution.py:320
  71.6 8.7 %collective-permute-start.13 = (bf16[4,2,128,128]{3,2,1,0:T(8,128)(2,1)S(1)}, bf16[4,2,128,128]{3,2,1,0:T(8,128)(2,1)S(1)}, u32[]{:S(2)}, u32[]{:S(2)}) collective-permute-start(bf16[4,2,128,128]{3,2,1,0:T(8,128)(2,1)S(1)} %pad_maximum_fusion.refs_0_), channel_id=1, source_target_pairs={{0,4},{4,0},{8,12},{12,8},{16,20},{20,16},{24,28},{28,24},{1,5},{5... | collective-permute-start | bytes 786440 | tf_op jit(solution)/shard_map/ppermute | solution.py:314
  71.6 8.6 %collective-permute-start.18 = (bf16[4,2,128,128]{3,2,1,0:T(8,128)(2,1)S(1)}, bf16[4,2,128,128]{3,2,1,0:T(8,128)(2,1)S(1)}, u32[]{:S(2)}, u32[]{:S(2)}) collective-permute-start(bf16[4,2,128,128]{3,2,1,0:T(8,128)(2,1)S(1)} %pad_maximum_fusion.refs_0_), channel_id=1, source_target_pairs={{0,16},{4,12},{8,24},{12,4},{16,0},{20,28},{24,8},{28,20},{1,17},{... | collective-permute-start | bytes 786440 | tf_op jit(solution)/shard_map/ppermute | solution.py:320
  73.2 7.9 %collective-permute-start.22 = (bf16[4,2,128,128]{3,2,1,0:T(8,128)(2,1)S(1)}, bf16[4,2,128,128]{3,2,1,0:T(8,128)(2,1)S(1)}, u32[]{:S(2)}, u32[]{:S(2)}) collective-permute-start(bf16[4,2,128,128]{3,2,1,0:T(8,128)(2,1)S(1)} %pad_maximum_fusion.1.refs_1_), channel_id=1, source_target_pairs={{0,8},{4,20},{8,0},{12,28},{16,24},{20,4},{24,16},{28,12},{1,9},{5... | collective-permute-start | bytes 786440 | tf_op jit(solution)/shard_map/ppermute | solution.py:320
  74.7 8.4 %collective-permute-start.20 = (bf16[4,2,128,128]{3,2,1,0:T(8,128)(2,1)S(1)}, bf16[4,2,128,128]{3,2,1,0:T(8,128)(2,1)S(1)}, u32[]{:S(2)}, u32[]{:S(2)}) collective-permute-start(bf16[4,2,128,128]{3,2,1,0:T(8,128)(2,1)S(1)} %pad_maximum_fusion.refs_0_), channel_id=1, source_target_pairs={{0,8},{4,20},{8,0},{12,28},{16,24},{20,4},{24,16},{28,12},{1,9},{5... | collective-permute-start | bytes 786440 | tf_op jit(solution)/shard_map/ppermute | solution.py:320
  75.3 10.2 %collective-permute-start.25 = (bf16[4,2,128,128]{3,2,1,0:T(8,128)(2,1)S(1)}, bf16[4,2,128,128]{3,2,1,0:T(8,128)(2,1)S(1)}, u32[]{:S(2)}, u32[]{:S(2)}) collective-permute-start(bf16[4,2,128,128]{3,2,1,0:T(8,128)(2,1)S(1)} %collective-permute-done.19.refs_1_), channel_id=1, source_target_pairs={{0,4},{4,0},{8,12},{12,8},{16,20},{20,16},{24,28},{28,24},{1,5},{5... | collective-permute-start | bytes 786440 | tf_op jit(solution)/shard_map/ppermute | solution.py:314
  80.3 6.8 %collective-permute-start.24 = (bf16[4,2,128,128]{3,2,1,0:T(8,128)(2,1)S(1)}, bf16[4,2,128,128]{3,2,1,0:T(8,128)(2,1)S(1)}, u32[]{:S(2)}, u32[]{:S(2)}) collective-permute-start(bf16[4,2,128,128]{3,2,1,0:T(8,128)(2,1)S(1)} %collective-permute-done.18.refs_0_), channel_id=1, source_target_pairs={{0,4},{4,0},{8,12},{12,8},{16,20},{20,16},{24,28},{28,24},{1,5},{5... | collective-permute-start | bytes 786440 | tf_op jit(solution)/shard_map/ppermute | solution.py:314
  81.1 7.8 %collective-permute-start.23 = (bf16[4,2,128,128]{3,2,1,0:T(8,128)(2,1)S(1)}, bf16[4,2,128,128]{3,2,1,0:T(8,128)(2,1)S(1)}, u32[]{:S(2)}, u32[]{:S(2)}) collective-permute-start(bf16[4,2,128,128]{3,2,1,0:T(8,128)(2,1)S(1)} %collective-permute-done.22.refs_1_), channel_id=1, source_target_pairs={{0,4},{4,0},{8,12},{12,8},{16,20},{20,16},{24,28},{28,24},{1,5},{5... | collective-permute-start | bytes 786440 | tf_op jit(solution)/shard_map/ppermute | solution.py:314
  81.6 9.3 %collective-permute-start.27 = (bf16[4,2,128,128]{3,2,1,0:T(8,128)(2,1)S(1)}, bf16[4,2,128,128]{3,2,1,0:T(8,128)(2,1)S(1)}, u32[]{:S(2)}, u32[]{:S(2)}) collective-permute-start(bf16[4,2,128,128]{3,2,1,0:T(8,128)(2,1)S(1)} %collective-permute-done.22.refs_1_), channel_id=1, source_target_pairs={{0,16},{4,12},{8,24},{12,4},{16,0},{20,28},{24,8},{28,20},{1,17},{... | collective-permute-start | bytes 786440 | tf_op jit(solution)/shard_map/ppermute | solution.py:320
  83.2 5.8 %collective-permute-start.21 = (bf16[4,2,128,128]{3,2,1,0:T(8,128)(2,1)S(1)}, bf16[4,2,128,128]{3,2,1,0:T(8,128)(2,1)S(1)}, u32[]{:S(2)}, u32[]{:S(2)}) collective-permute-start(bf16[4,2,128,128]{3,2,1,0:T(8,128)(2,1)S(1)} %collective-permute-done.20.refs_0_), channel_id=1, source_target_pairs={{0,4},{4,0},{8,12},{12,8},{16,20},{20,16},{24,28},{28,24},{1,5},{5... | collective-permute-start | bytes 786440 | tf_op jit(solution)/shard_map/ppermute | solution.py:314
  85.5 6.4 %collective-permute-start.26 = (bf16[4,2,128,128]{3,2,1,0:T(8,128)(2,1)S(1)}, bf16[4,2,128,128]{3,2,1,0:T(8,128)(2,1)S(1)}, u32[]{:S(2)}, u32[]{:S(2)}) collective-permute-start(bf16[4,2,128,128]{3,2,1,0:T(8,128)(2,1)S(1)} %collective-permute-done.20.refs_0_), channel_id=1, source_target_pairs={{0,16},{4,12},{8,24},{12,4},{16,0},{20,28},{24,8},{28,20},{1,17},{... | collective-permute-start | bytes 786440 | tf_op jit(solution)/shard_map/ppermute | solution.py:320
  91.9 1.5 %collective-permute-start.28 = (bf16[4,2,128,128]{3,2,1,0:T(8,128)(2,1)S(1)}, bf16[4,2,128,128]{3,2,1,0:T(8,128)(2,1)S(1)}, u32[]{:S(2)}, u32[]{:S(2)}) collective-permute-start(bf16[4,2,128,128]{3,2,1,0:T(8,128)(2,1)S(1)} %collective-permute-done.26.refs_0_), channel_id=1, source_target_pairs={{0,4},{4,0},{8,12},{12,8},{16,20},{20,16},{24,28},{28,24},{1,5},{5... | collective-permute-start | bytes 786440 | tf_op jit(solution)/shard_map/ppermute | solution.py:314
  91.9 1.9 %collective-permute-start.29 = (bf16[4,2,128,128]{3,2,1,0:T(8,128)(2,1)S(1)}, bf16[4,2,128,128]{3,2,1,0:T(8,128)(2,1)S(1)}, u32[]{:S(2)}, u32[]{:S(2)}) collective-permute-start(bf16[4,2,128,128]{3,2,1,0:T(8,128)(2,1)S(1)} %collective-permute-done.27.refs_1_), channel_id=1, source_target_pairs={{0,4},{4,0},{8,12},{12,8},{16,20},{20,16},{24,28},{28,24},{1,5},{5... | collective-permute-start | bytes 786440 | tf_op jit(solution)/shard_map/ppermute | solution.py:314
  (1 other events, 17.1 us)

commit v6 on v5

--- a/solution.py
+++ b/solution.py
@@ -322,6 +322,7 @@
     def along(x, k):
         return lax.ppermute(x, "mode", [(i, (i + k) % blocks) for i in range(blocks)])
 
+    far_first = sorted(range(1, blocks), key=lambda k: (-min(k, blocks - k), -k))
     mate = to_mate(radiation)
     mine, other = unit_forces(coords, wavevec, mode_shapes)
     kept = mine + to_mate(other)
@@ -332,12 +333,13 @@
 
     fields = []
     for total, sent in zip(totals, sends):
-        for k, block in enumerate(sent):
-            total = total + along(block, k + 1).astype(jnp.float32)
+        for k in far_first:
+            total = total + along(sent[k - 1], k).astype(jnp.float32)
         fields.append(total.astype(jnp.bfloat16))
-    gathered = [
-        [jnp.stack([field] + [along(field, k) for k in range(1, blocks)])] for field in fields
-    ]
+    gathered = []
+    for field in fields:
+        came = {k: along(field, k) for k in far_first}
+        gathered.append([jnp.stack([field] + [came[k] for k in range(1, blocks)])])
     mates = [[to_mate(x) for x in parts] for parts in gathered]
     left, field_pressure = own_rows([x[0] for x in fields] + [x[0][0, 1] for x in mates])
 

time: 95.9 us -> 95.7 us (level)
  waiting for transfers between devices: 18.2 us -> 17 us
    ppermute x12, waiting for transfers between devices: 2.46 us -> 1.23 us  [along(): lax.ppermute(x, 'mode', [(i, (i + k) % blocks) for i in range(blocks)])]
  transfers between devices with their start and end apart: 30 -> 30, of which waited for: 10 -> 9; matrix products, arithmetic and copies ran while one was open for 3% -> 3% of each run, Pallas kernels for 7% -> 7%
where the time goes in v6:
time: 95.7 us; the launch traced here: 95.4 us
  starting transfers between devices  37.7 us (39%)
  Pallas kernels  36.7 us (38%)
  waiting for transfers between devices  17 us (18%)
  other arithmetic  1.67 us (2%)
  local copies, waits for them, and re-layouts  1.57 us (2%)
    pallas_call x1, Pallas kernels, unit_forces(): pl.pallas_call(functools.partial(forces_kernel, piece), grid=(nodes // bl...  26.4 us
    ppermute x12, starting transfers between devices, along(): lax.ppermute(x, 'mode', [(i, (i + k) % blocks) for i in range(blocks)])  22.3 us
    ppermute x8, starting transfers between devices, across(): return lax.ppermute(x, 'node', [(i, flip(i)) for i in range(nodes)])  13.2 us
    ppermute x8, waiting for transfers between devices, across(): return lax.ppermute(x, 'node', [(i, flip(i)) for i in range(nodes)])  12.8 us
    pallas_call x4, Pallas kernels, cross_spectra(): pl.pallas_call(functools.partial(spectra_kernel, blocks), grid_spec=pltpu...  7.91 us
    ppermute x10, waiting for transfers between devices, to_mate(): return lax.ppermute(x, 'node', [(i, i ^ 1) for i in range(nodes)])  2.99 us
    ppermute x10, starting transfers between devices, to_mate(): return lax.ppermute(x, 'node', [(i, i ^ 1) for i in range(nodes)])  2.19 us
  transfers between devices with their start and end apart: 30, of which 9 were waited for; matrix products, arithmetic and copies ran while one was open for 3% of the time, Pallas kernels for 7%

profile of v6, /device:TPU:0, one launch (start us, length us, event | category | flops | bytes accessed | tf_op | source)
XLA Modules:
  0.0 95.4 jit_solution(4838628750284106899)
XLA Ops:
  0.6 26.4 %shard_map.77 = (f32[500,256]{1,0:T(8,128)}, f32[500,256]{1,0:T(8,128)}) custom-call(f32[3,24576]{1,0:T(4,128)} %coords_ref.1, f32[3,256]{1,0:T(4,128)} %wave_ref.1, bf16[500,24576]{1,0:T(8,128)(2,1)} %shapes_ref.1), custom_call_target="tpu_custom_call" | custom-call | flops 37748736000 | bytes 24576000 | tf_op jit(solution)/shard_map/pallas_call | solution.py:124
  27.7 1.6 %collective-permute-done = f32[500,256]{1,0:T(8,128)S(1)} collective-permute-done((f32[500,256]{1,0:T(8,128)}, f32[500,256]{1,0:T(8,128)S(1)}, u32[]{:S(2)}, u32[]{:S(2)}) %collective-permute-start) | collective-permute-done | bytes 512032 | tf_op jit(solution)/shard_map/ppermute | solution.py:314
  29.3 1.1 %fusion.1 = (bf16[500,256]{1,0:T(8,128)(2,1)S(1)}, f32[500,256]{1,0:T(8,128)S(1)}) fusion(f32[500,256]{1,0:T(8,128)} %get-tuple-element.17, f32[500,256]{1,0:T(8,128)S(1)} %collective-permute-done), kind=kLoop, calls=%fused_computation.14 | loop fusion | flops 256000 | bytes 1792000 | tf_op jit(solution)/shard_map/convert_element_type | solution.py:330
  30.5 2.9 %collective-permute-start.1 = (bf16[500,256]{1,0:T(8,128)(2,1)S(1)}, bf16[500,256]{1,0:T(8,128)(2,1)S(1)}, u32[]{:S(2)}, u32[]{:S(2)}) collective-permute-start(bf16[500,256]{1,0:T(8,128)(2,1)S(1)} %get-tuple-element.34), channel_id=1, source_target_pairs={{0,8},{4,20},{8,0},{12,28},{16,24},{20,4},{24,16},{28,12},{1,9},{5... | collective-permute-start | bytes 768008 | tf_op jit(solution)/shard_map/ppermute | solution.py:320
  33.4 4.3 %collective-permute-done.1 = bf16[500,256]{1,0:T(8,128)(2,1)S(1)} collective-permute-done((bf16[500,256]{1,0:T(8,128)(2,1)S(1)}, bf16[500,256]{1,0:T(8,128)(2,1)S(1)}, u32[]{:S(2)}, u32[]{:S(2)}) %collective-permute-start.1) | collective-permute-done | bytes 256032 | tf_op jit(solution)/shard_map/ppermute | solution.py:320
  37.8 2.1 %collective-permute-start.2 = (bf16[500,256]{1,0:T(8,128)(2,1)S(1)}, bf16[500,256]{1,0:T(8,128)(2,1)S(1)}, u32[]{:S(2)}, u32[]{:S(2)}) collective-permute-start(bf16[500,256]{1,0:T(8,128)(2,1)S(1)} %get-tuple-element.32), channel_id=1, source_target_pairs={{0,16},{4,12},{8,24},{12,4},{16,0},{20,28},{24,8},{28,20},{1,17},{... | collective-permute-start | bytes 768008 | tf_op jit(solution)/shard_map/ppermute | solution.py:320
  40.2 1.4 %copy.14.mate_ref = bf16[2,500,512]{2,1,0:T(8,128)(2,1)S(1)} copy(bf16[2,500,512]{2,0,1:T(2,128)(2,1)} %collective-permute-done.3) | data formatting | bytes 2048000 | tf_op jit(solution)/shard_map/ppermute | solution.py:314
  41.6 2.6 %collective-permute-done.2.last_ref = bf16[500,256]{1,0:T(8,128)(2,1)S(1)} collective-permute-done((bf16[500,256]{1,0:T(8,128)(2,1)S(1)}, bf16[500,256]{1,0:T(8,128)(2,1)S(1)}, u32[]{:S(2)}, u32[]{:S(2)}) %collective-permute-start.2) | collective-permute-done | bytes 256032 | tf_op jit(solution)/shard_map/ppermute | solution.py:320
  44.2 1.5 %shard_map.78 = (f32[2,128,128]{2,1,0:T(8,128)S(1)}, f32[2,128,128]{2,1,0:T(8,128)S(1)}, bf16[2,128,128]{2,1,0:T(8,128)(2,1)S(1)}, bf16[2,128,128]{2,1,0:T(8,128...) custom-call(f32[500,256]{1,0:T(8,128)S(1)} %get-tuple-element.33.kep, ...), custom_call_target="tpu_custom_call" | custom-call | flops 524288000 | bytes 2048000 | tf_op jit(solution)/shard_map/pallas_call | solution.py:207
  45.7 3.2 %collective-permute-start.7 = (bf16[2,128,128]{2,1,0:T(8,128)(2,1)S(1)}, bf16[2,128,128]{2,1,0:T(8,128)(2,1)S(1)}, u32[]{:S(2)}, u32[]{:S(2)}) collective-permute-start(bf16[2,128,128]{2,1,0:T(8,128)(2,1)S(1)} %get-tuple-element.24), channel_id=1, source_target_pairs={{0,2},{1,3},{2,0},{3,1},{4,6},{5,7},{6,4},{7,5},{8,10},{9,11},{10,... | collective-permute-start | bytes 196616 | tf_op jit(solution)/shard_map/ppermute | solution.py:323
  48.9 1.3 %collective-permute-start.8 = (bf16[2,128,128]{2,1,0:T(8,128)(2,1)S(1)}, bf16[2,128,128]{2,1,0:T(8,128)(2,1)S(1)}, u32[]{:S(2)}, u32[]{:S(2)}) collective-permute-start(bf16[2,128,128]{2,1,0:T(8,128)(2,1)S(1)} %get-tuple-element.25), channel_id=1, source_target_pairs={{0,3},{1,0},{2,1},{3,2},{4,7},{5,4},{6,5},{7,6},{8,11},{9,8},{10,9... | collective-permute-start | bytes 196616 | tf_op jit(solution)/shard_map/ppermute | solution.py:323
  51.0 1.0 %collective-permute-start.4 = (bf16[2,128,128]{2,1,0:T(8,128)(2,1)S(1)}, bf16[2,128,128]{2,1,0:T(8,128)(2,1)S(1)}, u32[]{:S(2)}, u32[]{:S(2)}) collective-permute-start(bf16[2,128,128]{2,1,0:T(8,128)(2,1)S(1)} %get-tuple-element.20), channel_id=1, source_target_pairs={{0,2},{1,3},{2,0},{3,1},{4,6},{5,7},{6,4},{7,5},{8,10},{9,11},{10,... | collective-permute-start | bytes 196616 | tf_op jit(solution)/shard_map/ppermute | solution.py:323
  52.0 2.9 %collective-permute-start.5 = (bf16[2,128,128]{2,1,0:T(8,128)(2,1)S(1)}, bf16[2,128,128]{2,1,0:T(8,128)(2,1)S(1)}, u32[]{:S(2)}, u32[]{:S(2)}) collective-permute-start(bf16[2,128,128]{2,1,0:T(8,128)(2,1)S(1)} %get-tuple-element.21), channel_id=1, source_target_pairs={{0,3},{1,0},{2,1},{3,2},{4,7},{5,4},{6,5},{7,6},{8,11},{9,8},{10,9... | collective-permute-start | bytes 196616 | tf_op jit(solution)/shard_map/ppermute | solution.py:323
  54.9 1.4 %collective-permute-start.6 = (bf16[2,128,128]{2,1,0:T(8,128)(2,1)S(1)}, bf16[2,128,128]{2,1,0:T(8,128)(2,1)S(1)}, u32[]{:S(2)}, u32[]{:S(2)}) collective-permute-start(bf16[2,128,128]{2,1,0:T(8,128)(2,1)S(1)} %get-tuple-element.22), channel_id=1, source_target_pairs={{0,1},{1,2},{2,3},{3,0},{4,5},{5,6},{6,7},{7,4},{8,9},{9,10},{10,1... | collective-permute-start | bytes 196616 | tf_op jit(solution)/shard_map/ppermute | solution.py:323
  56.4 2.2 %collective-permute-start.14 = (bf16[2,128,128]{2,1,0:T(8,128)(2,1)S(1)}, bf16[2,128,128]{2,1,0:T(8,128)(2,1)S(1)}, u32[]{:S(2)}, u32[]{:S(2)}) collective-permute-start(bf16[2,128,128]{2,1,0:T(8,128)(2,1)S(1)} %add_convert_fusion), channel_id=1, source_target_pairs={{0,1},{1,2},{2,3},{3,0},{4,5},{5,6},{6,7},{7,4},{8,9},{9,10},{10,1... | collective-permute-start | bytes 196616 | tf_op jit(solution)/shard_map/ppermute | solution.py:323
  58.6 2.8 %collective-permute-start.15 = (bf16[2,128,128]{2,1,0:T(8,128)(2,1)S(1)}, bf16[2,128,128]{2,1,0:T(8,128)(2,1)S(1)}, u32[]{:S(2)}, u32[]{:S(2)}) collective-permute-start(bf16[2,128,128]{2,1,0:T(8,128)(2,1)S(1)} %add_convert_fusion), channel_id=1, source_target_pairs={{0,2},{1,3},{2,0},{3,1},{4,6},{5,7},{6,4},{7,5},{8,10},{9,11},{10,... | collective-permute-start | bytes 196616 | tf_op jit(solution)/shard_map/ppermute | solution.py:323
  61.4 2.8 %collective-permute-start.16 = (bf16[2,128,128]{2,1,0:T(8,128)(2,1)S(1)}, bf16[2,128,128]{2,1,0:T(8,128)(2,1)S(1)}, u32[]{:S(2)}, u32[]{:S(2)}) collective-permute-start(bf16[2,128,128]{2,1,0:T(8,128)(2,1)S(1)} %add_convert_fusion), channel_id=1, source_target_pairs={{0,3},{1,0},{2,1},{3,2},{4,7},{5,4},{6,5},{7,6},{8,11},{9,8},{10,9... | collective-permute-start | bytes 196616 | tf_op jit(solution)/shard_map/ppermute | solution.py:323
  64.3 1.4 %collective-permute-start.11 = (bf16[2,128,128]{2,1,0:T(8,128)(2,1)S(1)}, bf16[2,128,128]{2,1,0:T(8,128)(2,1)S(1)}, u32[]{:S(2)}, u32[]{:S(2)}) collective-permute-start(bf16[2,128,128]{2,1,0:T(8,128)(2,1)S(1)} %add_convert_fusion.1), channel_id=1, source_target_pairs={{0,2},{1,3},{2,0},{3,1},{4,6},{5,7},{6,4},{7,5},{8,10},{9,11},{10,... | collective-permute-start | bytes 196616 | tf_op jit(solution)/shard_map/ppermute | solution.py:323
  65.8 2.4 %collective-permute-start.12 = (bf16[2,128,128]{2,1,0:T(8,128)(2,1)S(1)}, bf16[2,128,128]{2,1,0:T(8,128)(2,1)S(1)}, u32[]{:S(2)}, u32[]{:S(2)}) collective-permute-start(bf16[2,128,128]{2,1,0:T(8,128)(2,1)S(1)} %add_convert_fusion.1), channel_id=1, source_target_pairs={{0,3},{1,0},{2,1},{3,2},{4,7},{5,4},{6,5},{7,6},{8,11},{9,8},{10,9... | collective-permute-start | bytes 196616 | tf_op jit(solution)/shard_map/ppermute | solution.py:323
  68.3 1.6 %collective-permute-start.19 = (bf16[4,2,128,128]{3,2,1,0:T(8,128)(2,1)S(1)}, bf16[4,2,128,128]{3,2,1,0:T(8,128)(2,1)S(1)}, u32[]{:S(2)}, u32[]{:S(2)}) collective-permute-start(bf16[4,2,128,128]{3,2,1,0:T(8,128)(2,1)S(1)} %pad_maximum_fusion.1.refs_1_), channel_id=1, source_target_pairs={{0,16},{4,12},{8,24},{12,4},{16,0},{20,28},{24,8},{28,20},{1,17},{... | collective-permute-start | bytes 786440 | tf_op jit(solution)/shard_map/ppermute | solution.py:320
  71.2 1.6 %collective-permute-start.18 = (bf16[4,2,128,128]{3,2,1,0:T(8,128)(2,1)S(1)}, bf16[4,2,128,128]{3,2,1,0:T(8,128)(2,1)S(1)}, u32[]{:S(2)}, u32[]{:S(2)}) collective-permute-start(bf16[4,2,128,128]{3,2,1,0:T(8,128)(2,1)S(1)} %pad_maximum_fusion.refs_0_), channel_id=1, source_target_pairs={{0,16},{4,12},{8,24},{12,4},{16,0},{20,28},{24,8},{28,20},{1,17},{... | collective-permute-start | bytes 786440 | tf_op jit(solution)/shard_map/ppermute | solution.py:320
  72.8 1.5 %collective-permute-start.22 = (bf16[4,2,128,128]{3,2,1,0:T(8,128)(2,1)S(1)}, bf16[4,2,128,128]{3,2,1,0:T(8,128)(2,1)S(1)}, u32[]{:S(2)}, u32[]{:S(2)}) collective-permute-start(bf16[4,2,128,128]{3,2,1,0:T(8,128)(2,1)S(1)} %pad_maximum_fusion.1.refs_1_), channel_id=1, source_target_pairs={{0,8},{4,20},{8,0},{12,28},{16,24},{20,4},{24,16},{28,12},{1,9},{5... | collective-permute-start | bytes 786440 | tf_op jit(solution)/shard_map/ppermute | solution.py:320
  74.8 5.0 %collective-permute-done.18.refs_0_ = bf16[4,2,128,128]{3,2,1,0:T(8,128)(2,1)S(1)} collective-permute-done((bf16[4,2,128,128]{3,2,1,0:T(8,128)(2,1)S(1)}, bf16[4,2,128,128]{3,2,1,0:T(8,128)(2,1)S(1)}, u32[]{:S(2)}, u32[]{:S(2)}) %collective-permute-start.18) | collective-permute-done | bytes 262176 | tf_op jit(solution)/shard_map/ppermute | solution.py:320
  79.8 0.9 shard_map.79
  81.2 1.5 %collective-permute-start.27 = (bf16[4,2,128,128]{3,2,1,0:T(8,128)(2,1)S(1)}, bf16[4,2,128,128]{3,2,1,0:T(8,128)(2,1)S(1)}, u32[]{:S(2)}, u32[]{:S(2)}) collective-permute-start(bf16[4,2,128,128]{3,2,1,0:T(8,128)(2,1)S(1)} %collective-permute-done.22.refs_1_), channel_id=1, source_target_pairs={{0,16},{4,12},{8,24},{12,4},{16,0},{20,28},{24,8},{28,20},{1,17},{... | collective-permute-start | bytes 786440 | tf_op jit(solution)/shard_map/ppermute | solution.py:320
  83.2 2.0 %shard_map.80.refs_4_ = f32[2,128,4096]{2,1,0:T(8,128)} custom-call(s32[2]{0:T(128)S(1)} %pad_add_fusion.3.place_ref, bf16[4,256,128]{2,1,0:T(8,128)(2,1)S(1)} %get-tuple-element.27.left_ref, bf16[4,2,128,128]{3,2,1,0:T(8,128)(2,1)S(1)} %pad_maximum_fusion.refs_0_, bf16[4,2,128,128]{3,2,1,0:T(8,128)(2,1)S(1)} %pad_maximum_fusion.1.refs_1_, ...), custom_call_target="tpu_custom_call" | custom-call | flops 2684354560 | bytes 2097152 | tf_op jit(solution)/shard_map/pallas_call | solution.py:281
  85.1 1.5 %collective-permute-start.26 = (bf16[4,2,128,128]{3,2,1,0:T(8,128)(2,1)S(1)}, bf16[4,2,128,128]{3,2,1,0:T(8,128)(2,1)S(1)}, u32[]{:S(2)}, u32[]{:S(2)}) collective-permute-start(bf16[4,2,128,128]{3,2,1,0:T(8,128)(2,1)S(1)} %collective-permute-done.20.refs_0_), channel_id=1, source_target_pairs={{0,16},{4,12},{8,24},{12,4},{16,0},{20,28},{24,8},{28,20},{1,17},{... | collective-permute-start | bytes 786440 | tf_op jit(solution)/shard_map/ppermute | solution.py:320
  86.6 2.0 %shard_map.81.refs_4_ = f32[2,128,4096]{2,1,0:T(8,128)} custom-call(s32[2]{0:T(128)S(1)} %pad_add_fusion.2.place_ref, bf16[4,256,128]{2,1,0:T(8,128)(2,1)S(1)} %get-tuple-element.27.left_ref, bf16[4,2,128,128]{3,2,1,0:T(8,128)(2,1)S(1)} %collective-permute-done.20.refs_0_, ...), custom_call_target="tpu_custom_call", output_to_operand_aliasing={{}: (6, {})} | custom-call | flops 2684354560 | bytes 2097152 | tf_op jit(solution)/shard_map/pallas_call | solution.py:281
  88.6 2.0 %shard_map.82.refs_4_ = f32[2,128,4096]{2,1,0:T(8,128)} custom-call(s32[2]{0:T(128)S(1)} %pad_add_fusion.1.place_ref, bf16[4,256,128]{2,1,0:T(8,128)(2,1)S(1)} %get-tuple-element.27.left_ref, bf16[4,2,128,128]{3,2,1,0:T(8,128)(2,1)S(1)} %collective-permute-done.18.refs_0_, ...), custom_call_target="tpu_custom_call", output_to_operand_aliasing={{}: (6, {})} | custom-call | flops 2684354560 | bytes 2097152 | tf_op jit(solution)/shard_map/pallas_call | solution.py:281
  90.6 0.9 collective-permute-done.26.refs_0_
  92.1 0.9 collective-permute-done.28.refs_2_
  93.4 2.0 %shard_map.83 = f32[2,128,4096]{2,1,0:T(8,128)} custom-call(s32[2]{0:T(128)S(1)} %pad_add_fusion.place_ref, bf16[4,256,128]{2,1,0:T(8,128)(2,1)S(1)} %get-tuple-element.27.left_ref, bf16[4,2,128,128]{3,2,1,0:T(8,128)(2,1)S(1)} %collective-permute-done.26.refs_0_, ...), custom_call_target="tpu_custom_call", output_to_operand_aliasing={{}: (6, {})} | custom-call | flops 2684354560 | bytes 2097152 | tf_op jit(solution)/shard_map/pallas_call | solution.py:281
  (57 shorter events, 5.8 us)
Async XLA Ops:
  0.6 27.0 %copy-start.2 = (bf16[2,500,512]{2,0,1:T(2,128)(2,1)S(1)}, bf16[2,500,512]{2,0,1:T(2,128)(2,1)}, u32[]{:S(2)}) copy-start(bf16[2,500,512]{2,0,1:T(2,128)(2,1)} %param.11) | copy-start | bytes 3072004
  27.1 17.1 %copy-start.1 = (f32[2,256]{1,0:T(2,128)S(1)}, f32[2,256]{1,0:T(2,128)}, u32[]{:S(2)}) copy-start(f32[2,256]{1,0:T(2,128)} %amp_ref.1) | copy-start | bytes 6148
  27.1 2.3 %collective-permute-start = (f32[500,256]{1,0:T(8,128)}, f32[500,256]{1,0:T(8,128)S(1)}, u32[]{:S(2)}, u32[]{:S(2)}) collective-permute-start(f32[500,256]{1,0:T(8,128)} %get-tuple-element.18), channel_id=1, source_target_pairs={{0,4},{4,0},{8,12},{12,8},{16,20},{20,16},{24,28},{28,24},{1,5},{5... | collective-permute-start | bytes 1536008 | tf_op jit(solution)/shard_map/ppermute | solution.py:314
  27.6 12.6 %collective-permute-start.3 = (bf16[2,500,512]{2,0,1:T(2,128)(2,1)S(1)}, bf16[2,500,512]{2,0,1:T(2,128)(2,1)}, u32[]{:S(2)}, u32[]{:S(2)}) collective-permute-start(bf16[2,500,512]{2,0,1:T(2,128)(2,1)S(1)} %copy-done.2), channel_id=1, source_target_pairs={{0,4},{4,0},{8,12},{12,8},{16,20},{20,16},{24,28},{28,24},{1,5},{5... | collective-permute-start | bytes 3072008 | tf_op jit(solution)/shard_map/ppermute | solution.py:314
  30.5 7.2 %collective-permute-start.1 = (bf16[500,256]{1,0:T(8,128)(2,1)S(1)}, bf16[500,256]{1,0:T(8,128)(2,1)S(1)}, u32[]{:S(2)}, u32[]{:S(2)}) collective-permute-start(bf16[500,256]{1,0:T(8,128)(2,1)S(1)} %get-tuple-element.34), channel_id=1, source_target_pairs={{0,8},{4,20},{8,0},{12,28},{16,24},{20,4},{24,16},{28,12},{1,9},{5... | collective-permute-start | bytes 768008 | tf_op jit(solution)/shard_map/ppermute | solution.py:320
  37.8 6.4 %collective-permute-start.2 = (bf16[500,256]{1,0:T(8,128)(2,1)S(1)}, bf16[500,256]{1,0:T(8,128)(2,1)S(1)}, u32[]{:S(2)}, u32[]{:S(2)}) collective-permute-start(bf16[500,256]{1,0:T(8,128)(2,1)S(1)} %get-tuple-element.32), channel_id=1, source_target_pairs={{0,16},{4,12},{8,24},{12,4},{16,0},{20,28},{24,8},{28,20},{1,17},{... | collective-permute-start | bytes 768008 | tf_op jit(solution)/shard_map/ppermute | solution.py:320
  45.7 9.2 %collective-permute-start.7 = (bf16[2,128,128]{2,1,0:T(8,128)(2,1)S(1)}, bf16[2,128,128]{2,1,0:T(8,128)(2,1)S(1)}, u32[]{:S(2)}, u32[]{:S(2)}) collective-permute-start(bf16[2,128,128]{2,1,0:T(8,128)(2,1)S(1)} %get-tuple-element.24), channel_id=1, source_target_pairs={{0,2},{1,3},{2,0},{3,1},{4,6},{5,7},{6,4},{7,5},{8,10},{9,11},{10,... | collective-permute-start | bytes 196616 | tf_op jit(solution)/shard_map/ppermute | solution.py:323
  48.9 7.5 %collective-permute-start.8 = (bf16[2,128,128]{2,1,0:T(8,128)(2,1)S(1)}, bf16[2,128,128]{2,1,0:T(8,128)(2,1)S(1)}, u32[]{:S(2)}, u32[]{:S(2)}) collective-permute-start(bf16[2,128,128]{2,1,0:T(8,128)(2,1)S(1)} %get-tuple-element.25), channel_id=1, source_target_pairs={{0,3},{1,0},{2,1},{3,2},{4,7},{5,4},{6,5},{7,6},{8,11},{9,8},{10,9... | collective-permute-start | bytes 196616 | tf_op jit(solution)/shard_map/ppermute | solution.py:323
  50.2 6.2 %collective-permute-start.9 = (bf16[2,128,128]{2,1,0:T(8,128)(2,1)S(1)}, bf16[2,128,128]{2,1,0:T(8,128)(2,1)S(1)}, u32[]{:S(2)}, u32[]{:S(2)}) collective-permute-start(bf16[2,128,128]{2,1,0:T(8,128)(2,1)S(1)} %get-tuple-element.26), channel_id=1, source_target_pairs={{0,1},{1,2},{2,3},{3,0},{4,5},{5,6},{6,7},{7,4},{8,9},{9,10},{10,1... | collective-permute-start | bytes 196616 | tf_op jit(solution)/shard_map/ppermute | solution.py:323
  51.0 10.4 %collective-permute-start.4 = (bf16[2,128,128]{2,1,0:T(8,128)(2,1)S(1)}, bf16[2,128,128]{2,1,0:T(8,128)(2,1)S(1)}, u32[]{:S(2)}, u32[]{:S(2)}) collective-permute-start(bf16[2,128,128]{2,1,0:T(8,128)(2,1)S(1)} %get-tuple-element.20), channel_id=1, source_target_pairs={{0,2},{1,3},{2,0},{3,1},{4,6},{5,7},{6,4},{7,5},{8,10},{9,11},{10,... | collective-permute-start | bytes 196616 | tf_op jit(solution)/shard_map/ppermute | solution.py:323
  52.0 12.2 %collective-permute-start.5 = (bf16[2,128,128]{2,1,0:T(8,128)(2,1)S(1)}, bf16[2,128,128]{2,1,0:T(8,128)(2,1)S(1)}, u32[]{:S(2)}, u32[]{:S(2)}) collective-permute-start(bf16[2,128,128]{2,1,0:T(8,128)(2,1)S(1)} %get-tuple-element.21), channel_id=1, source_target_pairs={{0,3},{1,0},{2,1},{3,2},{4,7},{5,4},{6,5},{7,6},{8,11},{9,8},{10,9... | collective-permute-start | bytes 196616 | tf_op jit(solution)/shard_map/ppermute | solution.py:323
  54.9 9.3 %collective-permute-start.6 = (bf16[2,128,128]{2,1,0:T(8,128)(2,1)S(1)}, bf16[2,128,128]{2,1,0:T(8,128)(2,1)S(1)}, u32[]{:S(2)}, u32[]{:S(2)}) collective-permute-start(bf16[2,128,128]{2,1,0:T(8,128)(2,1)S(1)} %get-tuple-element.22), channel_id=1, source_target_pairs={{0,1},{1,2},{2,3},{3,0},{4,5},{5,6},{6,7},{7,4},{8,9},{9,10},{10,1... | collective-permute-start | bytes 196616 | tf_op jit(solution)/shard_map/ppermute | solution.py:323
  56.4 9.4 %collective-permute-start.14 = (bf16[2,128,128]{2,1,0:T(8,128)(2,1)S(1)}, bf16[2,128,128]{2,1,0:T(8,128)(2,1)S(1)}, u32[]{:S(2)}, u32[]{:S(2)}) collective-permute-start(bf16[2,128,128]{2,1,0:T(8,128)(2,1)S(1)} %add_convert_fusion), channel_id=1, source_target_pairs={{0,1},{1,2},{2,3},{3,0},{4,5},{5,6},{6,7},{7,4},{8,9},{9,10},{10,1... | collective-permute-start | bytes 196616 | tf_op jit(solution)/shard_map/ppermute | solution.py:323
  58.6 9.6 %collective-permute-start.15 = (bf16[2,128,128]{2,1,0:T(8,128)(2,1)S(1)}, bf16[2,128,128]{2,1,0:T(8,128)(2,1)S(1)}, u32[]{:S(2)}, u32[]{:S(2)}) collective-permute-start(bf16[2,128,128]{2,1,0:T(8,128)(2,1)S(1)} %add_convert_fusion), channel_id=1, source_target_pairs={{0,2},{1,3},{2,0},{3,1},{4,6},{5,7},{6,4},{7,5},{8,10},{9,11},{10,... | collective-permute-start | bytes 196616 | tf_op jit(solution)/shard_map/ppermute | solution.py:323
  61.4 6.8 %collective-permute-start.16 = (bf16[2,128,128]{2,1,0:T(8,128)(2,1)S(1)}, bf16[2,128,128]{2,1,0:T(8,128)(2,1)S(1)}, u32[]{:S(2)}, u32[]{:S(2)}) collective-permute-start(bf16[2,128,128]{2,1,0:T(8,128)(2,1)S(1)} %add_convert_fusion), channel_id=1, source_target_pairs={{0,3},{1,0},{2,1},{3,2},{4,7},{5,4},{6,5},{7,6},{8,11},{9,8},{10,9... | collective-permute-start | bytes 196616 | tf_op jit(solution)/shard_map/ppermute | solution.py:323
  64.3 6.1 %collective-permute-start.10 = (bf16[2,128,128]{2,1,0:T(8,128)(2,1)S(1)}, bf16[2,128,128]{2,1,0:T(8,128)(2,1)S(1)}, u32[]{:S(2)}, u32[]{:S(2)}) collective-permute-start(bf16[2,128,128]{2,1,0:T(8,128)(2,1)S(1)} %add_convert_fusion.1), channel_id=1, source_target_pairs={{0,1},{1,2},{2,3},{3,0},{4,5},{5,6},{6,7},{7,4},{8,9},{9,10},{10,1... | collective-permute-start | bytes 196616 | tf_op jit(solution)/shard_map/ppermute | solution.py:323
  64.3 6.1 %collective-permute-start.11 = (bf16[2,128,128]{2,1,0:T(8,128)(2,1)S(1)}, bf16[2,128,128]{2,1,0:T(8,128)(2,1)S(1)}, u32[]{:S(2)}, u32[]{:S(2)}) collective-permute-start(bf16[2,128,128]{2,1,0:T(8,128)(2,1)S(1)} %add_convert_fusion.1), channel_id=1, source_target_pairs={{0,2},{1,3},{2,0},{3,1},{4,6},{5,7},{6,4},{7,5},{8,10},{9,11},{10,... | collective-permute-start | bytes 196616 | tf_op jit(solution)/shard_map/ppermute | solution.py:323
  65.8 5.3 %collective-permute-start.12 = (bf16[2,128,128]{2,1,0:T(8,128)(2,1)S(1)}, bf16[2,128,128]{2,1,0:T(8,128)(2,1)S(1)}, u32[]{:S(2)}, u32[]{:S(2)}) collective-permute-start(bf16[2,128,128]{2,1,0:T(8,128)(2,1)S(1)} %add_convert_fusion.1), channel_id=1, source_target_pairs={{0,3},{1,0},{2,1},{3,2},{4,7},{5,4},{6,5},{7,6},{8,11},{9,8},{10,9... | collective-permute-start | bytes 196616 | tf_op jit(solution)/shard_map/ppermute | solution.py:323
  68.3 6.0 %collective-permute-start.17 = (bf16[4,2,128,128]{3,2,1,0:T(8,128)(2,1)S(1)}, bf16[4,2,128,128]{3,2,1,0:T(8,128)(2,1)S(1)}, u32[]{:S(2)}, u32[]{:S(2)}) collective-permute-start(bf16[4,2,128,128]{3,2,1,0:T(8,128)(2,1)S(1)} %pad_maximum_fusion.1.refs_1_), channel_id=1, source_target_pairs={{0,4},{4,0},{8,12},{12,8},{16,20},{20,16},{24,28},{28,24},{1,5},{5... | collective-permute-start | bytes 786440 | tf_op jit(solution)/shard_map/ppermute | solution.py:314
  68.3 6.5 %collective-permute-start.19 = (bf16[4,2,128,128]{3,2,1,0:T(8,128)(2,1)S(1)}, bf16[4,2,128,128]{3,2,1,0:T(8,128)(2,1)S(1)}, u32[]{:S(2)}, u32[]{:S(2)}) collective-permute-start(bf16[4,2,128,128]{3,2,1,0:T(8,128)(2,1)S(1)} %pad_maximum_fusion.1.refs_1_), channel_id=1, source_target_pairs={{0,16},{4,12},{8,24},{12,4},{16,0},{20,28},{24,8},{28,20},{1,17},{... | collective-permute-start | bytes 786440 | tf_op jit(solution)/shard_map/ppermute | solution.py:320
  71.1 8.7 %collective-permute-start.13 = (bf16[4,2,128,128]{3,2,1,0:T(8,128)(2,1)S(1)}, bf16[4,2,128,128]{3,2,1,0:T(8,128)(2,1)S(1)}, u32[]{:S(2)}, u32[]{:S(2)}) collective-permute-start(bf16[4,2,128,128]{3,2,1,0:T(8,128)(2,1)S(1)} %pad_maximum_fusion.refs_0_), channel_id=1, source_target_pairs={{0,4},{4,0},{8,12},{12,8},{16,20},{20,16},{24,28},{28,24},{1,5},{5... | collective-permute-start | bytes 786440 | tf_op jit(solution)/shard_map/ppermute | solution.py:314
  71.2 8.6 %collective-permute-start.18 = (bf16[4,2,128,128]{3,2,1,0:T(8,128)(2,1)S(1)}, bf16[4,2,128,128]{3,2,1,0:T(8,128)(2,1)S(1)}, u32[]{:S(2)}, u32[]{:S(2)}) collective-permute-start(bf16[4,2,128,128]{3,2,1,0:T(8,128)(2,1)S(1)} %pad_maximum_fusion.refs_0_), channel_id=1, source_target_pairs={{0,16},{4,12},{8,24},{12,4},{16,0},{20,28},{24,8},{28,20},{1,17},{... | collective-permute-start | bytes 786440 | tf_op jit(solution)/shard_map/ppermute | solution.py:320
  72.8 7.9 %collective-permute-start.22 = (bf16[4,2,128,128]{3,2,1,0:T(8,128)(2,1)S(1)}, bf16[4,2,128,128]{3,2,1,0:T(8,128)(2,1)S(1)}, u32[]{:S(2)}, u32[]{:S(2)}) collective-permute-start(bf16[4,2,128,128]{3,2,1,0:T(8,128)(2,1)S(1)} %pad_maximum_fusion.1.refs_1_), channel_id=1, source_target_pairs={{0,8},{4,20},{8,0},{12,28},{16,24},{20,4},{24,16},{28,12},{1,9},{5... | collective-permute-start | bytes 786440 | tf_op jit(solution)/shard_map/ppermute | solution.py:320
  74.3 8.5 %collective-permute-start.20 = (bf16[4,2,128,128]{3,2,1,0:T(8,128)(2,1)S(1)}, bf16[4,2,128,128]{3,2,1,0:T(8,128)(2,1)S(1)}, u32[]{:S(2)}, u32[]{:S(2)}) collective-permute-start(bf16[4,2,128,128]{3,2,1,0:T(8,128)(2,1)S(1)} %pad_maximum_fusion.refs_0_), channel_id=1, source_target_pairs={{0,8},{4,20},{8,0},{12,28},{16,24},{20,4},{24,16},{28,12},{1,9},{5... | collective-permute-start | bytes 786440 | tf_op jit(solution)/shard_map/ppermute | solution.py:320
  74.8 10.3 %collective-permute-start.25 = (bf16[4,2,128,128]{3,2,1,0:T(8,128)(2,1)S(1)}, bf16[4,2,128,128]{3,2,1,0:T(8,128)(2,1)S(1)}, u32[]{:S(2)}, u32[]{:S(2)}) collective-permute-start(bf16[4,2,128,128]{3,2,1,0:T(8,128)(2,1)S(1)} %collective-permute-done.19.refs_1_), channel_id=1, source_target_pairs={{0,4},{4,0},{8,12},{12,8},{16,20},{20,16},{24,28},{28,24},{1,5},{5... | collective-permute-start | bytes 786440 | tf_op jit(solution)/shard_map/ppermute | solution.py:314
  79.8 6.8 %collective-permute-start.24 = (bf16[4,2,128,128]{3,2,1,0:T(8,128)(2,1)S(1)}, bf16[4,2,128,128]{3,2,1,0:T(8,128)(2,1)S(1)}, u32[]{:S(2)}, u32[]{:S(2)}) collective-permute-start(bf16[4,2,128,128]{3,2,1,0:T(8,128)(2,1)S(1)} %collective-permute-done.18.refs_0_), channel_id=1, source_target_pairs={{0,4},{4,0},{8,12},{12,8},{16,20},{20,16},{24,28},{28,24},{1,5},{5... | collective-permute-start | bytes 786440 | tf_op jit(solution)/shard_map/ppermute | solution.py:314
  80.7 7.9 %collective-permute-start.23 = (bf16[4,2,128,128]{3,2,1,0:T(8,128)(2,1)S(1)}, bf16[4,2,128,128]{3,2,1,0:T(8,128)(2,1)S(1)}, u32[]{:S(2)}, u32[]{:S(2)}) collective-permute-start(bf16[4,2,128,128]{3,2,1,0:T(8,128)(2,1)S(1)} %collective-permute-done.22.refs_1_), channel_id=1, source_target_pairs={{0,4},{4,0},{8,12},{12,8},{16,20},{20,16},{24,28},{28,24},{1,5},{5... | collective-permute-start | bytes 786440 | tf_op jit(solution)/shard_map/ppermute | solution.py:314
  81.2 9.4 %collective-permute-start.27 = (bf16[4,2,128,128]{3,2,1,0:T(8,128)(2,1)S(1)}, bf16[4,2,128,128]{3,2,1,0:T(8,128)(2,1)S(1)}, u32[]{:S(2)}, u32[]{:S(2)}) collective-permute-start(bf16[4,2,128,128]{3,2,1,0:T(8,128)(2,1)S(1)} %collective-permute-done.22.refs_1_), channel_id=1, source_target_pairs={{0,16},{4,12},{8,24},{12,4},{16,0},{20,28},{24,8},{28,20},{1,17},{... | collective-permute-start | bytes 786440 | tf_op jit(solution)/shard_map/ppermute | solution.py:320
  82.7 5.9 %collective-permute-start.21 = (bf16[4,2,128,128]{3,2,1,0:T(8,128)(2,1)S(1)}, bf16[4,2,128,128]{3,2,1,0:T(8,128)(2,1)S(1)}, u32[]{:S(2)}, u32[]{:S(2)}) collective-permute-start(bf16[4,2,128,128]{3,2,1,0:T(8,128)(2,1)S(1)} %collective-permute-done.20.refs_0_), channel_id=1, source_target_pairs={{0,4},{4,0},{8,12},{12,8},{16,20},{20,16},{24,28},{28,24},{1,5},{5... | collective-permute-start | bytes 786440 | tf_op jit(solution)/shard_map/ppermute | solution.py:314
  85.1 6.4 %collective-permute-start.26 = (bf16[4,2,128,128]{3,2,1,0:T(8,128)(2,1)S(1)}, bf16[4,2,128,128]{3,2,1,0:T(8,128)(2,1)S(1)}, u32[]{:S(2)}, u32[]{:S(2)}) collective-permute-start(bf16[4,2,128,128]{3,2,1,0:T(8,128)(2,1)S(1)} %collective-permute-done.20.refs_0_), channel_id=1, source_target_pairs={{0,16},{4,12},{8,24},{12,4},{16,0},{20,28},{24,8},{28,20},{1,17},{... | collective-permute-start | bytes 786440 | tf_op jit(solution)/shard_map/ppermute | solution.py:320
  91.5 1.5 %collective-permute-start.28 = (bf16[4,2,128,128]{3,2,1,0:T(8,128)(2,1)S(1)}, bf16[4,2,128,128]{3,2,1,0:T(8,128)(2,1)S(1)}, u32[]{:S(2)}, u32[]{:S(2)}) collective-permute-start(bf16[4,2,128,128]{3,2,1,0:T(8,128)(2,1)S(1)} %collective-permute-done.26.refs_0_), channel_id=1, source_target_pairs={{0,4},{4,0},{8,12},{12,8},{16,20},{20,16},{24,28},{28,24},{1,5},{5... | collective-permute-start | bytes 786440 | tf_op jit(solution)/shard_map/ppermute | solution.py:314
  91.5 1.9 %collective-permute-start.29 = (bf16[4,2,128,128]{3,2,1,0:T(8,128)(2,1)S(1)}, bf16[4,2,128,128]{3,2,1,0:T(8,128)(2,1)S(1)}, u32[]{:S(2)}, u32[]{:S(2)}) collective-permute-start(bf16[4,2,128,128]{3,2,1,0:T(8,128)(2,1)S(1)} %collective-permute-done.27.refs_1_), channel_id=1, source_target_pairs={{0,4},{4,0},{8,12},{12,8},{16,20},{20,16},{24,28},{28,24},{1,5},{5... | collective-permute-start | bytes 786440 | tf_op jit(solution)/shard_map/ppermute | solution.py:314
  (1 other events, 17.1 us)
